TPU v7x, 128 devices: a whole 4x4x4 slice. The times are simulated.
128 devices in a mesh: dp: 8 (over y, z_hi), fsdp: 16 (over x, z_lo, core).
Axes of the slice: x: 4, y: 4, z: 4 (z_hi: 2, z_lo: 2; z = z_hi * 2 + z_lo), core: 2. Of those that a mesh axis runs over, the one named last changes fastest.
Arguments:
- tokens: bfloat16 [16384, 5120], P(('dp', 'fsdp')), may hold values from -6 to 6
- cotangent: bfloat16 [16384, 5120], P(('dp', 'fsdp')), may hold values from -6 to 6
- advantage: float32 [16384], P(('dp', 'fsdp')), may hold values from -3 to 3
- chosen: int32 [8, 16, 4], P('dp', 'fsdp'), may hold values from 0 to 127, as said below
- chosen_count: int32 [8, 16], P('dp'), may hold values from 0 to 4, as said below
- gate_weight: bfloat16 [5120, 25600], P('fsdp', 'dp'), may hold values from -0.078125 to 0.078125
- up_weight: bfloat16 [5120, 25600], P('fsdp', 'dp'), may hold values from -0.078125 to 0.078125
- down_weight: bfloat16 [25600, 5120], P('dp', 'fsdp'), may hold values from -0.0390625 to 0.0390625
Outputs:
- input_grad: bfloat16 [16384, 5120], P(('dp', 'fsdp'))
- gate_grad: bfloat16 [5120, 25600], P('fsdp', 'dp')
- up_grad: bfloat16 [5120, 25600], P('fsdp', 'dp')
- down_grad: bfloat16 [25600, 5120], P('dp', 'fsdp')
Inputs may be any that keep to these rules, and one draw needn't show every extreme that they name: `chosen`: the 4 slots of one device name distinct local rows. `chosen_count`: the counts of the 16 devices that share one dp index sum to at most 32; some dp index reaches 32 and some device reaches 4 in every draw.
All inputs are finite; a program needn't handle non-finite values.
Results may differ from a plain program's by a relative error of at most 0.0058.
Values may be sent and summed in bfloat16 or wider, within the bound.
No kernel may reach another device: no remote copies, remote signals or barrier semaphores. Data moves between devices by JAX's collectives and lax.ppermute only.
A program may use at most 128 MiB of HBM per device.

v0:
```python
import jax
import jax.numpy as jnp
from jax import lax
from jax.sharding import PartitionSpec as P


def swiglu_backward(gate_pre, up_pre, hidden_delta):
    sigma = jax.nn.sigmoid(gate_pre)
    active = gate_pre * sigma
    hidden = (active * up_pre).astype(jnp.bfloat16)
    gate_delta = (hidden_delta * up_pre * sigma * (1.0 + gate_pre * (1.0 - sigma))).astype(
        jnp.bfloat16
    )
    up_delta = (hidden_delta * active).astype(jnp.bfloat16)
    return (hidden, gate_delta, up_delta)


def shards(tokens, cotangent, advantage, chosen, chosen_count, gate_weight, up_weight, down_weight):
    capacity = chosen.shape[2]
    rows_local = tokens.shape[0]
    width_full = tokens.shape[1]
    position = lax.axis_index("fsdp")
    counts = chosen_count[0]
    row_index = chosen[0, 0]
    slot_ids = jnp.arange(capacity, dtype=jnp.int32)
    alive_local = slot_ids < counts[position]
    picked = jnp.where(alive_local[:, None], tokens[row_index], jnp.zeros((), tokens.dtype))
    weighted = jnp.where(
        alive_local[:, None],
        cotangent[row_index].astype(jnp.float32) * advantage[row_index][:, None],
        jnp.float32(0.0),
    ).astype(jnp.bfloat16)
    local_x, local_y = (
        lax.all_to_all(picked, "fsdp", split_axis=1, concat_axis=0, tiled=True),
        lax.all_to_all(weighted, "fsdp", split_axis=1, concat_axis=0, tiled=True),
    )
    all_x, all_y = (
        lax.all_gather(local_x, "dp", axis=0, tiled=True),
        lax.all_gather(local_y, "dp", axis=0, tiled=True),
    )
    gate_part = jnp.dot(all_x, gate_weight, preferred_element_type=jnp.float32)
    up_part = jnp.dot(all_x, up_weight, preferred_element_type=jnp.float32)
    down_part = jnp.einsum("rd,fd->rf", all_y, down_weight, preferred_element_type=jnp.float32)
    gate_share, up_share, delta_share = (
        lax.psum_scatter(gate_part, "fsdp", scatter_dimension=1, tiled=True),
        lax.psum_scatter(up_part, "fsdp", scatter_dimension=1, tiled=True),
        lax.psum_scatter(down_part, "fsdp", scatter_dimension=1, tiled=True),
    )
    gate_pre, up_pre, hidden_delta = (
        lax.all_gather(gate_share, "fsdp", axis=1, tiled=True),
        lax.all_gather(up_share, "fsdp", axis=1, tiled=True),
        lax.all_gather(delta_share, "fsdp", axis=1, tiled=True),
    )
    hidden, gate_delta, up_delta = swiglu_backward(gate_pre, up_pre, hidden_delta)
    gate_grad = jnp.einsum("rd,rf->df", all_x, gate_delta, preferred_element_type=jnp.float32)
    up_grad = jnp.einsum("rd,rf->df", all_x, up_delta, preferred_element_type=jnp.float32)
    down_grad = jnp.einsum("rf,rd->fd", hidden, all_y, preferred_element_type=jnp.float32)
    backward_part = jnp.einsum(
        "rf,df->rd", gate_delta, gate_weight, preferred_element_type=jnp.float32
    )
    backward_part = backward_part + jnp.einsum(
        "rf,df->rd", up_delta, up_weight, preferred_element_type=jnp.float32
    )
    summed = lax.psum_scatter(backward_part, "dp", scatter_dimension=0, tiled=True)
    returned = lax.all_to_all(summed, "fsdp", split_axis=0, concat_axis=1, tiled=True)
    returned = jnp.where(alive_local[:, None], returned, jnp.float32(0.0))
    input_grad = jnp.zeros((rows_local, width_full), jnp.float32).at[row_index].set(returned)
    return (
        input_grad.astype(jnp.bfloat16),
        gate_grad.astype(jnp.bfloat16),
        up_grad.astype(jnp.bfloat16),
        down_grad.astype(jnp.bfloat16),
    )


def solution(mesh):
    in_specs = (
        P(("dp", "fsdp"), None),
        P(("dp", "fsdp"), None),
        P(("dp", "fsdp")),
        P("dp", "fsdp", None),
        P("dp", None),
        P("fsdp", "dp"),
        P("fsdp", "dp"),
        P("dp", "fsdp"),
    )
    out_specs = (P(("dp", "fsdp"), None), P("fsdp", "dp"), P("fsdp", "dp"), P("dp", "fsdp"))
    return jax.shard_map(shards, mesh=mesh, in_specs=in_specs, out_specs=out_specs, check_vma=False)
```

profile of v0, /device:TPU:1, one launch (start us, length us, event | category | flops | bytes accessed | tf_op | source)
XLA Modules:
  0.0 570.1 jit_solution(8721170465568946389)
XLA Ops:
  7.2 0.0 copy-start
  7.2 0.0 reduce-scatter.5.cloned.1.call-start
  7.2 1.4 constant_dynamic-slice_fusion
  8.6 0.6 iota_compare_fusion
  9.3 0.7 fusion.9
  9.9 1.3 gather_fusion.1
  11.2 2.1 gather_fusion
  13.3 0.1 reshape.71
  13.4 0.1 fusion.5
  13.5 12.8 %all_to_all.51 = bf16[4,16,320]{2,0,1:T(4,128)(2,1)S(1)} all-to-all(bf16[4,16,320]{2,0,1:T(4,128)(2,1)S(1)} %fusion.5), channel_id=1, replica_groups=mesh['dp'=8,'fsdp'=16] {'fsdp'}, dimensions={1} | all-to-all | bytes 81920 | tf_op jit(solution)/shard_map/all_to_all | solution.py:35
  26.4 29.5 %all_gather.15 = bf16[512,320]{1,0:T(8,128)(2,1)S(1)} all-gather(bf16[64,320]{1,0:T(8,128)(2,1)S(1)} %all_to_all.40), channel_id=1, replica_groups=mesh['dp'=8,'fsdp'=16] {'dp'}, dimensions={0}, use_global_device_ids=true | all-gather | bytes 368640 | tf_op jit(solution)/shard_map/all_gather | solution.py:39
  55.9 6.2 %fusion.11 = f32[512,3200]{0,1:T(8,128)} fusion(bf16[512,320]{1,0:T(8,128)(2,1)S(1)} %all_gather.15, bf16[3200,320]{0,1:T(8,128)(2,1)} %param.15), kind=kOutput, calls=%fused_computation.28 | convolution fusion | flops 1048576000 | bytes 8929280 | tf_op jit(solution)/shard_map/rd,fd->rf/dot_general | solution.py:43
  62.1 0.0 reduce-scatter.5.cloned.1.call-update
  62.1 0.0 reduce-scatter.9.cloned.1.call-start
  62.2 2.1 gather_fusion.2
  64.3 0.1 gather.14
  64.4 0.1 copy_select_fusion
  64.5 14.2 %all_to_all.52 = bf16[4,16,320]{2,0,1:T(4,128)(2,1)S(1)} all-to-all(bf16[4,16,320]{2,0,1:T(4,128)(2,1)S(1)} %copy_select_fusion), channel_id=1, replica_groups=mesh['dp'=8,'fsdp'=16] {'fsdp'}, dimensions={1} | all-to-all | bytes 81920 | tf_op jit(solution)/shard_map/all_to_all | solution.py:34
  78.8 33.2 %all_gather.17 = bf16[512,320]{1,0:T(8,128)(2,1)S(1)} all-gather(bf16[64,320]{1,0:T(8,128)(2,1)S(1)} %all_to_all.43), channel_id=1, replica_groups=mesh['dp'=8,'fsdp'=16] {'dp'}, dimensions={0}, use_global_device_ids=true | all-gather | bytes 368640 | tf_op jit(solution)/shard_map/all_gather | solution.py:38
  112.0 0.0 copy-done
  112.0 4.7 fusion.13
  116.6 0.0 reduce-scatter.9.cloned.1.call-update
  116.7 0.0 reduce-scatter.7.cloned.1.call-start
  116.7 6.3 %fusion.12 = f32[512,3200]{0,1:T(8,128)} fusion(bf16[512,320]{1,0:T(8,128)(2,1)S(1)} %all_gather.17, bf16[320,3200]{1,0:T(8,128)(2,1)} %param.14), kind=kOutput, calls=%fused_computation.29 | convolution fusion | flops 1048576000 | bytes 8929280 | tf_op jit(solution)/shard_map/dot_general | solution.py:42
  123.0 0.0 reduce-scatter.7.cloned.1.call-update
  123.0 0.0 all-gather.4.cloned.1.call-start
  123.1 30.2 %reduce-scatter.5.cloned.1.call-done = f32[512,200]{0,1:T(8,128)} async-done(((f32[512,3200]{0,1:T(8,128)}), f32[512,200]{0,1:T(8,128)}) %reduce-scatter.5.cloned.1.call-update) | async-done | bytes 409616 | tf_op jit(solution)/shard_map/reduce_scatter | solution.py:47
  153.3 0.0 all-gather.4.cloned.1.call-update
  153.3 0.0 all-gather.8.cloned.1.call-start
  153.3 85.1 %reduce-scatter.9.cloned.1.call-done = f32[512,200]{0,1:T(8,128)} async-done(((f32[512,3200]{0,1:T(8,128)}), f32[512,200]{0,1:T(8,128)}) %reduce-scatter.9.cloned.1.call-update) | async-done | bytes 409616 | tf_op jit(solution)/shard_map/reduce_scatter | solution.py:45
  238.5 0.0 all-gather.8.cloned.1.call-update
  238.5 0.0 all-gather.6.cloned.1.call-start
  238.5 81.8 %reduce-scatter.7.cloned.1.call-done = f32[512,200]{0,1:T(8,128)} async-done(((f32[512,3200]{0,1:T(8,128)}), f32[512,200]{0,1:T(8,128)}) %reduce-scatter.7.cloned.1.call-update) | async-done | bytes 409616 | tf_op jit(solution)/shard_map/reduce_scatter | solution.py:46
  320.3 0.0 all-gather.6.cloned.1.call-update
  320.4 0.2 reduce-scatter.11.cloned.1.call-start
  320.6 45.4 %all-gather.4.cloned.1.call-done = f32[512,3200]{0,1:T(8,128)} async-done(((f32[512,200]{0,1:T(8,128)}), f32[512,3200]{0,1:T(8,128)}) %all-gather.4.cloned.1.call-update) | async-done | bytes 6553616 | tf_op jit(solution)/shard_map/all_gather | solution.py:52
  366.0 46.0 %all-gather.8.cloned.1.call-done = f32[512,3200]{0,1:T(8,128)} async-done(((f32[512,200]{0,1:T(8,128)}), f32[512,3200]{0,1:T(8,128)}) %all-gather.8.cloned.1.call-update) | async-done | bytes 6553616 | tf_op jit(solution)/shard_map/all_gather | solution.py:50
  412.1 46.1 %all-gather.6.cloned.1.call-done = f32[512,3200]{0,1:T(8,128)} async-done(((f32[512,200]{0,1:T(8,128)}), f32[512,3200]{0,1:T(8,128)}) %all-gather.6.cloned.1.call-update) | async-done | bytes 6553616 | tf_op jit(solution)/shard_map/all_gather | solution.py:51
  458.1 8.5 %multiply_convert_fusion.1 = (bf16[512,3200]{0,1:T(8,128)(2,1)S(1)}, bf16[512,3200]{0,1:T(8,128)(2,1)S(1)}) fusion(f32[512,3200]{0,1:T(8,128)} %all-gather.4.cloned.1.call-done, f32[512,3200]{0,1:T(8,128)} %all-gather.8.cloned.1.call-done, f32[512,3200]{0,1:T(8,128)} %all-gather.6.cloned.1.call-done), kind=kLoop, calls=%fused_computation.5 | loop fusion | flops 21299200 | bytes 26214400 | tf_op jit(solution)/shard_map/convert_element_type | solution.py:14
  466.6 0.0 copy-start.3
  466.7 0.0 copy-start.2
  466.7 0.0 copy-start.4
  466.7 1.9 fusion.14
  468.6 0.0 copy-done.3
  468.6 0.9 copy-done.2
  469.6 0.2 copy-done.4
  469.8 2.8 convolution_add_fusion
  472.6 0.0 reduce-scatter.11.cloned.1.call-update
  472.6 4.8 convolution_convert_fusion.2
  477.4 8.4 %convolution_convert_fusion = bf16[3200,320]{0,1:T(8,128)(2,1)} fusion(bf16[512,320]{1,0:T(8,128)(2,1)S(1)} %all_gather.15, f32[512,3200]{0,1:T(8,128)} %all-gather.6.cloned.1.call-done, f32[512,3200]{0,1:T(8,128)} %all-gather.8.cloned.1.call-done), kind=kOutput, calls=%fused_computation.9 | convolution fusion | flops 1059430400 | bytes 15482880 | tf_op jit(solution)/shard_map/rf,rd->fd/dot_general | solution.py:57
  485.7 57.6 %reduce-scatter.11.cloned.1.call-done = f32[64,320]{1,0:T(8,128)} async-done(((f32[512,320]{1,0:T(8,128)}), f32[64,320]{1,0:T(8,128)}) %reduce-scatter.11.cloned.1.call-update) | async-done | bytes 81936 | tf_op jit(solution)/shard_map/reduce_scatter | solution.py:64
  543.3 1.6 all_to_all.44
  544.9 7.0 %all-to-all-start.2 = ((f32[16,4,320]{2,1,0:T(4,128)}), f32[16,4,320]{2,1,0:T(4,128)S(1)}, u32[]{:S(2)}, u32[]{:S(2)}) async-start(f32[16,4,320]{2,1,0:T(4,128)} %all_to_all.44), calls=%async_computation.6 | async-start | bytes 196608 | tf_op jit(solution)/shard_map/all_to_all | solution.py:65
  551.9 4.8 convolution_convert_fusion.1
  556.6 1.2 all-to-all-done.2
  557.8 0.0 copy-start.1
  557.8 0.1 all_to_all.47
  557.9 2.3 scatter_custom_fusion
  560.3 3.0 convert_element_type.37
  563.2 0.0 copy-done.1
  (4 shorter events, 0.1 us)
Async XLA Ops:
  7.2 104.8 %copy-start = (bf16[320,3200]{1,0:T(8,128)(2,1)S(1)}, bf16[320,3200]{1,0:T(8,128)(2,1)}, u32[]{:S(2)}) copy-start(bf16[320,3200]{1,0:T(8,128)(2,1)} %param.13) | copy-start | bytes 6144004
  7.2 146.1 %reduce-scatter.5.cloned.1.call-start = ((), (), s32[]{:S(2)}) async-start(), calls=%async_computation.7 | async-start | bytes 6963200 | tf_op jit(solution)/shard_map/reduce_scatter | solution.py:47
  62.1 176.4 %reduce-scatter.9.cloned.1.call-start = ((), (), s32[]{:S(2)}) async-start(), calls=%async_computation.11 | async-start | bytes 6963200 | tf_op jit(solution)/shard_map/reduce_scatter | solution.py:45
  116.7 203.7 %reduce-scatter.7.cloned.1.call-start = ((), (), s32[]{:S(2)}) async-start(), calls=%async_computation.9 | async-start | bytes 6963200 | tf_op jit(solution)/shard_map/reduce_scatter | solution.py:46
  123.0 243.0 %all-gather.4.cloned.1.call-start = ((), (), s32[]{:S(2)}) async-start(), calls=%async_computation.8 | async-start | bytes 6963200 | tf_op jit(solution)/shard_map/all_gather | solution.py:52
  153.3 258.8 %all-gather.8.cloned.1.call-start = ((), (), s32[]{:S(2)}) async-start(), calls=%async_computation.12 | async-start | bytes 6963200 | tf_op jit(solution)/shard_map/all_gather | solution.py:50
  238.5 219.6 %all-gather.6.cloned.1.call-start = ((), (), s32[]{:S(2)}) async-start(), calls=%async_computation.10 | async-start | bytes 6963200 | tf_op jit(solution)/shard_map/all_gather | solution.py:51
  320.4 222.9 %reduce-scatter.11.cloned.1.call-start = ((), (), s32[]{:S(2)}) async-start(), calls=%async_computation.13 | async-start | bytes 884736 | tf_op jit(solution)/shard_map/reduce_scatter | solution.py:64
  466.6 2.0 copy-start.3
  466.7 2.9 copy-start.2
  466.7 3.1 copy-start.4
  544.9 12.9 %all-to-all-start.2 = ((f32[16,4,320]{2,1,0:T(4,128)}), f32[16,4,320]{2,1,0:T(4,128)S(1)}, u32[]{:S(2)}, u32[]{:S(2)}) async-start(f32[16,4,320]{2,1,0:T(4,128)} %all_to_all.44), calls=%async_computation.6 | async-start | bytes 196608 | tf_op jit(solution)/shard_map/all_to_all | solution.py:65
  557.8 5.4 copy-start.1
Sparse Core Ops, SparseCore 0:
  62.2 90.9 reduce-scatter.4
  155.8 82.5 reduce-scatter.8
  240.9 79.4 reduce-scatter.6
  322.0 43.9 all-gather.3
  367.7 44.3 all-gather.7
  413.7 44.3 all-gather.5
  472.7 70.5 reduce-scatter.10
where the time goes:
time: 571 us; the launch traced here: 570 us
  waiting for transfers between devices  393 us (69%)
  blocking collectives  89.8 us (16%)
  matrix products  39.8 us (7%)
  other arithmetic  15.3 us (3%)
  between operations  14.2 us (2%)
  local copies, waits for them, and re-layouts  10 us (2%)
  starting transfers between devices  7.47 us (1%)
    reduce_scatter x1, waiting for transfers between devices, shards(): lax.psum_scatter(gate_part, 'fsdp', scatter_dimension=1, tiled=True)  85.1 us
    reduce_scatter x1, waiting for transfers between devices, shards(): lax.psum_scatter(up_part, 'fsdp', scatter_dimension=1, tiled=True)  81.8 us
    reduce_scatter x1, waiting for transfers between devices, shards(): lax.psum_scatter(backward_part, 'dp', scatter_dimension=0, tiled=True)  57.6 us
    all_gather x1, waiting for transfers between devices, shards(): lax.all_gather(up_share, 'fsdp', axis=1, tiled=True)  46.1 us
    all_gather x1, waiting for transfers between devices, shards(): lax.all_gather(gate_share, 'fsdp', axis=1, tiled=True)  46 us
    all_gather x1, waiting for transfers between devices, shards(): lax.all_gather(delta_share, 'fsdp', axis=1, tiled=True)  45.4 us
    all_gather x1, blocking collectives, shards(): lax.all_gather(local_x, 'dp', axis=0, tiled=True)  33.2 us
    reduce_scatter x1, waiting for transfers between devices, shards(): lax.psum_scatter(down_part, 'fsdp', scatter_dimension=1, tiled=True)  30.2 us
  transfers between devices with their start and end apart: 8, of which 8 were waited for; matrix products, arithmetic and copies ran while one was open for 5% of the time, Pallas kernels for 0%

commit v1 on v0

v1 whole, which is shorter than its diff:
```python
import jax
import jax.numpy as jnp
from jax import lax
from jax.sharding import Mesh, PartitionSpec as P

AXES = ("y", "zh", "x", "zl", "c")
SIZES = (4, 2, 4, 2, 2)
N_DP, N_FSDP, N_DEV = 8, 16, 128
CAP = 4
GROUP = 32
LIVE = N_DP * GROUP
DL = 320
FL = 3200
WIN = 1664
HI = FL - WIN
FAR = 512.0
SWAP = [(0, 1), (1, 0)]
BF, F32 = jnp.bfloat16, jnp.float32


def swiglu_backward(gate_pre, up_pre, hidden_delta):
    sigma = jax.nn.sigmoid(gate_pre)
    active = gate_pre * sigma
    hidden = (active * up_pre).astype(BF)
    gate_delta = (hidden_delta * up_pre * sigma * (1.0 + gate_pre * (1.0 - sigma))).astype(BF)
    up_delta = (hidden_delta * active).astype(BF)
    return (hidden, gate_delta, up_delta)


def dot(a, b, ca, cb):
    return lax.dot_general(a, b, (((ca,), (cb,)), ((), ())), preferred_element_type=F32)


def shards(tokens, cotangent, advantage, chosen, chosen_count, gate_weight, up_weight, down_weight):
    c = lax.axis_index("c")
    first = c == 0
    f_index = lax.axis_index(("x", "zl", "c"))
    d_index = lax.axis_index(("y", "zh"))

    def window(w, axis):
        lo = lax.slice_in_dim(w, 0, WIN, axis=axis)
        hi = lax.slice_in_dim(w, HI, FL, axis=axis)
        return jnp.where(first, lo, hi), lax.ppermute(jnp.where(first, hi, lo), "c", SWAP)

    gate_own, gate_sib = window(gate_weight, 1)
    up_own, up_sib = window(up_weight, 1)
    down_own, down_sib = window(down_weight, 0)

    counts = chosen_count[0]
    rows = chosen[0, 0]
    slots = jnp.arange(CAP, dtype=jnp.int32)
    live = slots < counts[f_index]
    before = jnp.sum(jnp.where(jnp.arange(N_FSDP) < f_index, counts, 0))
    place = jnp.where(live, d_index * GROUP + before + slots, int(FAR)).astype(BF)
    picked = jnp.where(live[:, None], tokens[rows], jnp.zeros((), BF))
    weighted = jnp.where(
        live[:, None], cotangent[rows].astype(F32) * advantage[rows][:, None], F32(0.0)
    ).astype(BF)
    message = jnp.concatenate(
        [
            picked.reshape(CAP, N_FSDP, DL),
            weighted.reshape(CAP, N_FSDP, DL),
            jnp.broadcast_to(place[:, None, None], (CAP, N_FSDP, 128)),
        ],
        axis=2,
    ).transpose(1, 0, 2)
    message = jnp.broadcast_to(message[None], (N_DP, N_FSDP, CAP, 768)).reshape(N_DEV, CAP, 768)
    got = lax.all_to_all(message, AXES, 0, 0, tiled=True).reshape(N_DEV * CAP, 768)
    pack = (jnp.arange(LIVE, dtype=jnp.int32)[:, None] == got[:, 640].astype(jnp.int32)[None, :]).astype(BF)
    own = dot(pack, got[:, :640], 1, 0).astype(BF)
    sib = lax.ppermute(own, "c", SWAP)
    x_own, y_own = own[:, :DL], own[:, DL:]
    x_sib, y_sib = sib[:, :DL], sib[:, DL:]

    gate_part = dot(x_own, gate_own, 1, 0) + dot(x_sib, gate_sib, 1, 0)
    up_part = dot(x_own, up_own, 1, 0) + dot(x_sib, up_sib, 1, 0)
    down_part = dot(y_own, down_own, 1, 1) + dot(y_sib, down_sib, 1, 1)
    parts = jnp.concatenate(
        [gate_part.astype(BF), up_part.astype(BF), down_part.astype(BF)], axis=1
    ).reshape(N_DP, GROUP, 3 * WIN)
    share = lax.all_to_all(parts, ("x", "zl"), 0, 0, tiled=True)
    share = jnp.sum(share.astype(F32), axis=0)
    hidden, gate_delta, up_delta = swiglu_backward(
        share[:, :WIN], share[:, WIN : 2 * WIN], share[:, 2 * WIN :]
    )
    values = jnp.concatenate([hidden, gate_delta, up_delta], axis=1)
    values = lax.all_to_all(
        jnp.broadcast_to(values[None], (N_DP, GROUP, 3 * WIN)), ("x", "zl"), 0, 0, tiled=True
    ).reshape(LIVE, 3 * WIN)
    other = lax.ppermute(values, "c", SWAP)
    lo = jnp.where(first, values, other)
    hi = jnp.where(first, other, values)

    def whole(k):
        return jnp.concatenate(
            [lo[:, k * WIN : (k + 1) * WIN], hi[:, k * WIN + WIN - HI : (k + 1) * WIN]], axis=1
        )

    hidden, gate_delta, up_delta = whole(0), whole(1), whole(2)

    back = dot(gate_delta, gate_weight, 1, 1) + dot(up_delta, up_weight, 1, 1)
    back = dot(pack, back.astype(BF), 0, 0).astype(BF).reshape(N_DEV, CAP, DL)
    back = lax.all_to_all(back, AXES, 0, 0, tiled=True)
    back = jnp.sum(back.reshape(N_DP, N_FSDP, CAP, DL).astype(F32), axis=0)
    back = back.transpose(1, 0, 2).reshape(CAP, N_FSDP * DL)

    gate_grad = dot(x_own, gate_delta, 0, 0).astype(BF)
    up_grad = dot(x_own, up_delta, 0, 0).astype(BF)
    down_grad = dot(hidden, y_own, 0, 0).astype(BF)

    row = jnp.arange(tokens.shape[0], dtype=jnp.int32)[:, None]
    input_grad = jnp.zeros(tokens.shape, F32)
    for s in range(CAP):
        input_grad = jnp.where((row == rows[s]) & live[s], back[s][None, :], input_grad)
    return (input_grad.astype(BF), gate_grad, up_grad, down_grad)


def solution(mesh):
    fine = Mesh(mesh.devices.reshape(SIZES), AXES)
    dp, fsdp = AXES[:2], AXES[2:]
    in_specs = (
        P(AXES, None),
        P(AXES, None),
        P(AXES),
        P(dp, fsdp, None),
        P(dp, None),
        P(fsdp, dp),
        P(fsdp, dp),
        P(dp, fsdp),
    )
    out_specs = (P(AXES, None), P(fsdp, dp), P(fsdp, dp), P(dp, fsdp))
    return jax.shard_map(shards, mesh=fine, in_specs=in_specs, out_specs=out_specs, check_vma=False)
```

time: 571 us -> 158 us (0.28)
  waiting for transfers between devices: 393 us -> 17.1 us
  blocking collectives: 89.8 us -> 65.4 us
  matrix products: 39.8 us -> 21 us
  starting transfers between devices: 7.47 us -> 20.9 us
  between operations: 14.2 us -> 1.62 us
    reduce_scatter x4 -> x0, waiting for transfers between devices: 255 us -> none  [the longest x1 85.1 us: shards(): lax.psum_scatter(gate_part, 'fsdp', scatter_dimension=1, tiled=True)]
    all_gather x3 -> x0, waiting for transfers between devices: 138 us -> none  [the longest x1 46.1 us: shards(): lax.all_gather(up_share, 'fsdp', axis=1, tiled=True)]
    all_gather x2 -> x0, blocking collectives: 62.7 us -> none  [the longest x1 33.2 us: shards(): lax.all_gather(local_x, 'dp', axis=0, tiled=True)]
    all_to_all x2, blocking collectives: 27 us -> 65.4 us  [the longest x1 33.3 us: shards(): share = lax.all_to_all(parts, ('x', 'zl'), 0, 0, tiled=True)]
    dot_general x8 -> x12, matrix products: 39.8 us -> 21 us  [dot(): lax.dot_general(a, b, (((ca,), (cb,)), ((), ())), preferred_element_type=...]
    all_to_all x1 -> x2, waiting for transfers between devices: 1.16 us -> 17.1 us  [the longest x1 9.7 us: shards(): lax.all_to_all(message, AXES, 0, 0, tiled=True).reshape(N_DEV * CAP, 768)]
    convert_element_type x3 -> x5, other arithmetic: 11.6 us -> 3.2 us  [the longest x1 2.19 us: shards(): return (input_grad.astype(BF), gate_grad, up_grad, down_grad)]
    all_to_all x1 -> x2, starting transfers between devices: 7.01 us -> 15.3 us  [the longest x1 11.5 us: shards(): lax.all_to_all(message, AXES, 0, 0, tiled=True).reshape(N_DEV * CAP, 768)]
  transfers between devices with their start and end apart: 8 -> 7, of which waited for: 8 -> 2; matrix products, arithmetic and copies ran while one was open for 5% -> 16% of each run, Pallas kernels for 0% -> 0%
where the time goes in v1:
time: 158 us; the launch traced here: 157 us
  blocking collectives  65.4 us (41%)
  matrix products  21 us (13%)
  starting transfers between devices  20.9 us (13%)
  other arithmetic  17.6 us (11%)
  waiting for transfers between devices  17.1 us (11%)
  local copies, waits for them, and re-layouts  13.7 us (9%)
  between operations  1.62 us (1%)
    all_to_all x1, blocking collectives, shards(): share = lax.all_to_all(parts, ('x', 'zl'), 0, 0, tiled=True)  33.3 us
    all_to_all x1, blocking collectives, shards(): lax.all_to_all(jnp.broadcast_to(values[None], (N_DP, GROUP, 3 * WIN)), ('...  32.1 us
    dot_general x12, matrix products, dot(): lax.dot_general(a, b, (((ca,), (cb,)), ((), ())), preferred_element_type=...  21 us
    all_to_all x1, starting transfers between devices, shards(): lax.all_to_all(message, AXES, 0, 0, tiled=True).reshape(N_DEV * CAP, 768)  11.5 us
    all_to_all x1, waiting for transfers between devices, shards(): lax.all_to_all(message, AXES, 0, 0, tiled=True).reshape(N_DEV * CAP, 768)  9.7 us
    all_to_all x1, waiting for transfers between devices, shards(): back = lax.all_to_all(back, AXES, 0, 0, tiled=True)  7.43 us
    and x2, other arithmetic, shards(): (row == rows[s]) & live[s]  5.02 us
    select_n x3, other arithmetic, window(): jnp.where(first, hi, lo)  4.99 us
  transfers between devices with their start and end apart: 7, of which 2 were waited for; matrix products, arithmetic and copies ran while one was open for 16% of the time, Pallas kernels for 0%

profile of v1, /device:TPU:1, one launch (start us, length us, event | category | flops | bytes accessed | tf_op | source)
XLA Modules:
  0.0 157.3 jit_solution(12256038205633738883)
XLA Ops:
  0.7 1.4 fusion.36
  2.1 1.2 constant_dynamic-slice_fusion
  3.3 0.6 iota_compare_fusion.3
  4.6 0.7 select_convert_fusion.2
  5.3 0.7 fusion.37
  5.9 0.6 gather_fusion.1
  6.5 0.1 reshape.149
  6.6 1.3 gather_fusion.2
  7.9 2.1 %gather_fusion = bf16[4,5120]{1,0:T(4,128)(2,1)S(1)} fusion(bf16[128,5120]{1,0:T(8,128)(2,1)} %param.8, s32[1024]{0:T(1024)S(1)} %pad_clamp_fusion), kind=kCustom, calls=%fused_computation | custom fusion | bytes 81936 | tf_op jit(solution)/shard_map/gather | solution.py:55
  10.0 0.1 gather.12
  10.1 0.1 broadcast_select_fusion.5
  10.2 0.1 select_convert_fusion.1
  10.3 0.1 broadcast_in_dim.120
  10.4 0.1 maximum_bitcast_fusion
  10.5 0.1 copy.15
  10.5 1.1 broadcast_in_dim.121
  11.6 11.5 %all-to-all-start = ((bf16[128,4,768]{2,1,0:T(4,128)(2,1)}), bf16[128,4,768]{2,1,0:T(4,128)(2,1)S(1)}, u32[]{:S(2)}, u32[]{:S(2)}) async-start(bf16[128,4,768]{2,1,0:T(4,128)(2,1)} %bitcast.7), calls=%async_computation | async-start | bytes 1572864 | tf_op jit(solution)/shard_map/all_to_all | solution.py:68
  23.1 2.8 %broadcast_select_fusion.4 = bf16[320,1664]{1,0:T(8,128)(2,1)} fusion(pred[]{:T(512)S(6)} %eq.65, bf16[320,3200]{1,0:T(8,128)(2,1)} %param.13), kind=kLoop, calls=%fused_computation.36 | loop fusion | flops 532480 | bytes 3194881 | tf_op jit(solution)/shard_map/jit(_where)/select_n | solution.py:43
  25.9 1.1 collective-permute-start.1
  27.0 1.1 broadcast_select_fusion.3
  28.1 1.1 broadcast_select_fusion.2
  29.2 0.8 collective-permute-start.3
  30.1 9.7 %all-to-all-done = bf16[128,4,768]{2,1,0:T(4,128)(2,1)S(1)} async-done(((bf16[128,4,768]{2,1,0:T(4,128)(2,1)}), bf16[128,4,768]{2,1,0:T(4,128)(2,1)S(1)}, u32[]{:S(2)}, u32[]{:S(2)}) %all-to-all-start) | async-done | bytes 786464 | tf_op jit(solution)/shard_map/all_to_all | solution.py:68
  39.8 0.2 reshape.145
  40.0 0.1 convert_reduce_fusion.2
  40.1 0.4 convolution_convert_fusion.4
  40.5 2.3 %fusion.11 = f32[256,1664]{1,0:T(8,128)S(1)} fusion(pred[]{:T(512)S(6)} %eq.65, bf16[320,3200]{1,0:T(8,128)(2,1)} %param.13, bf16[256,640]{1,0:T(8,128)(2,1)S(1)} %convolution_convert_fusion.4), kind=kOutput, calls=%fused_computation.30 | convolution fusion | flops 273162240 | bytes 4030465 | tf_op jit(solution)/shard_map/dot_general | solution.py:31
  42.9 0.4 collective-permute-start
  43.2 0.6 fusion.9
  43.9 0.6 copy-done.2
  44.4 0.7 fusion.7
  45.1 1.8 %fusion = bf16[256,1664]{1,0:T(8,128)(2,1)S(1)} fusion(f32[256,1664]{1,0:T(8,128)S(1)} %fusion.11, bf16[320,1664]{1,0:T(8,128)(2,1)} %collective-permute-done.1, bf16[256,640]{1,0:T(8,128)(2,1)S(1)} %collective-permute-done), kind=kOutput, calls=%fused_computation.11 | convolution fusion | flops 273481728 | bytes 3817472 | tf_op jit(solution)/shard_map/dot_general | solution.py:31
  47.0 1.8 %fusion.1 = bf16[256,1664]{1,0:T(8,128)(2,1)S(1)} fusion(f32[256,1664]{1,0:T(8,128)S(1)} %fusion.9, bf16[320,1664]{1,0:T(8,128)(2,1)} %collective-permute-done.2, bf16[256,640]{1,0:T(8,128)(2,1)S(1)} %collective-permute-done), kind=kOutput, calls=%fused_computation.12 | convolution fusion | flops 273481728 | bytes 3817472 | tf_op jit(solution)/shard_map/dot_general | solution.py:31
  48.8 1.9 %fusion.2 = bf16[256,1664]{1,0:T(8,128)(2,1)S(1)} fusion(f32[256,1664]{1,0:T(8,128)S(1)} %fusion.7, bf16[1664,320]{0,1:T(8,128)(2,1)} %collective-permute-done.3, bf16[256,640]{1,0:T(8,128)(2,1)S(1)} %collective-permute-done), kind=kOutput, calls=%fused_computation.13 | convolution fusion | flops 273481728 | bytes 3817472 | tf_op jit(solution)/shard_map/dot_general | solution.py:31
  50.8 0.2 pad_maximum_fusion
  51.0 33.3 %all_to_all.20 = bf16[8,32,4992]{2,1,0:T(8,128)(2,1)S(1)} all-to-all(bf16[8,32,4992]{2,1,0:T(8,128)(2,1)S(1)} %bitcast.31), channel_id=1, replica_groups=mesh['y'=4,'zh'=2,'x'=4,'zl'=2,'c'=2] {'x','zl'}, dimensions={0} | all-to-all | bytes 5111808 | tf_op jit(solution)/shard_map/all_to_all | solution.py:81
  84.2 0.4 convert_reduce_fusion
  84.6 0.1 multiply_convert_fusion.2
  84.8 0.2 broadcast_in_dim.122
  85.0 32.1 %all_to_all.21 = bf16[8,32,4992]{2,1,0:T(8,128)(2,1)S(1)} all-to-all(bf16[8,32,4992]{2,1,0:T(8,128)(2,1)S(1)} %broadcast_in_dim.122), channel_id=1, replica_groups=mesh['y'=4,'zh'=2,'x'=4,'zl'=2,'c'=2] {'x','zl'}, dimensions={0} | all-to-all | bytes 5111808 | tf_op jit(solution)/shard_map/all_to_all | solution.py:87
  117.1 3.2 %collective-permute-start.4 = (bf16[256,4992]{1,0:T(8,128)(2,1)S(1)}, bf16[256,4992]{1,0:T(8,128)(2,1)S(1)}, u32[]{:S(2)}, u32[]{:S(2)}) collective-permute-start(bf16[256,4992]{1,0:T(8,128)(2,1)S(1)} %bitcast.30), channel_id=1, source_target_pairs={{0,1},{1,0},{2,3},{3,2},{4,5},{5,4},{6,7},{7,6},{8,9},{9,8},{10,11... | collective-permute-start | bytes 7667720 | tf_op jit(solution)/shard_map/ppermute | solution.py:90
  120.4 0.7 fusion.46
  121.0 0.6 fusion.47
  121.6 2.5 %compare_and_fusion = (pred[128]{0:T(512)(128)(4,1)S(1)}, pred[128]{0:T(512)(128)(4,1)S(1)}) fusion(pred[]{:T(512)} %bitcast.17, s32[]{:T(128)} %bitcast.16, pred[]{:T(512)} %bitcast.15, s32[]{:T(128)} %bitcast.14), kind=kLoop, calls=%fused_computation.75 | loop fusion | flops 512 | bytes 266 | tf_op jit(solution)/shard_map/and | solution.py:114
  124.2 2.5 %compare_and_fusion.2 = (pred[128]{0:T(512)(128)(4,1)S(1)}, pred[128]{0:T(512)(128)(4,1)S(1)}) fusion(pred[]{:T(512)} %bitcast.13, s32[]{:T(128)} %bitcast.12, pred[]{:T(512)} %bitcast.2, s32[]{:T(128)} %bitcast), kind=kLoop, calls=%fused_computation.77 | loop fusion | flops 512 | bytes 266 | tf_op jit(solution)/shard_map/and | solution.py:114
  126.7 0.7 broadcast_select_fusion.1
  127.4 1.1 fusion.44
  128.5 1.1 fusion.45
  129.5 2.1 %convolution_convert_fusion.1 = bf16[320,3200]{1,0:T(8,128)(2,1)} fusion(bf16[256,1536]{1,0:T(8,128)(2,1)S(1)} %get-tuple-element.14, bf16[256,1664]{1,0:T(8,128)(2,1)S(1)} %get-tuple-element.11, bf16[256,640]{1,0:T(8,128)(2,1)S(1)} %convolution_convert_fusion.4), kind=kOutput, calls=%fused_computation.4 | convolution fusion | flops 528588800 | bytes 3883008 | tf_op jit(solution)/shard_map/dot_general | solution.py:31
  131.6 0.8 fusion.16
  132.3 3.4 %convolution_convert_fusion.3 = bf16[512,320]{0,1:T(8,128)(2,1)} fusion(f32[256,320]{0,1:T(8,128)S(1)} %fusion.16, bf16[320,3200]{1,0:T(8,128)(2,1)} %param.13, bf16[256,1536]{1,0:T(8,128)(2,1)S(1)} %get-tuple-element.15, bf16[256,1664]{1,0:T(8,128)(2,1)S(1)} %get-tuple-element.12, s32[512]{0:T(512)S(1)} %convert_reduce_fusion.2), kind=kOutput, calls=%fused_computation.22 | convolution fusion | flops 611909632 | bytes 4343808 | tf_op jit(solution)/shard_map/dot_general | solution.py:31
  135.7 1.2 copy.16
  136.9 0.9 reshape.148
  137.7 3.8 %all-to-all-start.3 = ((bf16[128,4,320]{2,1,0:T(4,128)(2,1)}), bf16[128,4,320]{2,1,0:T(4,128)(2,1)S(1)}, u32[]{:S(2)}, u32[]{:S(2)}) async-start(bf16[128,4,320]{2,1,0:T(4,128)(2,1)} %reshape.148), calls=%async_computation.3 | async-start | bytes 786432 | tf_op jit(solution)/shard_map/all_to_all | solution.py:103
  141.6 3.1 %convolution_convert_fusion.2 = bf16[320,3200]{1,0:T(8,128)(2,1)} fusion(bf16[256,1536]{1,0:T(8,128)(2,1)S(1)} %get-tuple-element.15, bf16[256,1664]{1,0:T(8,128)(2,1)S(1)} %get-tuple-element.12, bf16[256,640]{1,0:T(8,128)(2,1)} %copy-done.7), kind=kOutput, calls=%fused_computation.5 | convolution fusion | flops 528588800 | bytes 3883008 | tf_op jit(solution)/shard_map/dot_general | solution.py:31
  144.7 2.1 %convolution_convert_fusion = bf16[3200,320]{0,1:T(8,128)(2,1)} fusion(bf16[256,1536]{1,0:T(8,128)(2,1)S(1)} %copy-done.6, bf16[256,1664]{1,0:T(8,128)(2,1)S(1)} %copy-done.5, bf16[256,640]{1,0:T(8,128)(2,1)S(1)} %copy-done.8), kind=kOutput, calls=%fused_computation.3 | convolution fusion | flops 528588800 | bytes 3883008 | tf_op jit(solution)/shard_map/dot_general | solution.py:31
  146.9 7.4 %all-to-all-done.3 = bf16[128,4,320]{2,1,0:T(4,128)(2,1)S(1)} async-done(((bf16[128,4,320]{2,1,0:T(4,128)(2,1)}), bf16[128,4,320]{2,1,0:T(4,128)(2,1)S(1)}, u32[]{:S(2)}, u32[]{:S(2)}) %all-to-all-start.3) | async-done | bytes 327712 | tf_op jit(solution)/shard_map/all_to_all | solution.py:103
  154.3 0.2 convert_reduce_fusion.1
  154.5 0.3 slice_reduce_fusion.3
  154.8 0.1 broadcast_in_dim.123
  154.9 0.1 broadcast_in_dim.126
  155.0 0.1 broadcast_in_dim.129
  155.1 0.1 broadcast_in_dim.132
  155.1 2.2 %select_convert_fusion = bf16[128,5120]{1,0:T(8,128)(2,1)} fusion(bf16[5120]{0:T(1024)(128)(2,1)S(1)} %broadcast_in_dim.132, bf16[5120]{0:T(1024)(128)(2,1)S(1)} %broadcast_in_dim.129, bf16[5120]{0:T(1024)(128)(2,1)S(1)} %broadcast_in_dim.126, bf16[5120]{0:T(1024)(128)(2,1)S(1)} %broadcast_in_dim.123, pred[128]{0:T(512)(128)(4,1)S(1)} %get-tuple-element.27, ...), kind=kLoop, calls=%fused_computation.10 | loop fusion | flops 2621440 | bytes 1352192 | tf_op jit(solution)/shard_map/convert_element_type | solution.py:115
  (27 shorter events, 0.1 us)
Async XLA Ops:
  0.6 5.3 %copy-start = (bf16[128,5120]{1,0:T(8,128)(2,1)S(1)}, bf16[128,5120]{1,0:T(8,128)(2,1)}, u32[]{:S(2)}) copy-start(bf16[128,5120]{1,0:T(8,128)(2,1)} %param.9) | copy-start | bytes 3932164
  11.6 28.1 %all-to-all-start = ((bf16[128,4,768]{2,1,0:T(4,128)(2,1)}), bf16[128,4,768]{2,1,0:T(4,128)(2,1)S(1)}, u32[]{:S(2)}, u32[]{:S(2)}) async-start(bf16[128,4,768]{2,1,0:T(4,128)(2,1)} %bitcast.7), calls=%async_computation | async-start | bytes 1572864 | tf_op jit(solution)/shard_map/all_to_all | solution.py:68
  23.1 3.9 %copy-start.3 = (bf16[320,3200]{1,0:T(8,128)(2,1)S(1)}, bf16[320,3200]{1,0:T(8,128)(2,1)}, u32[]{:S(2)}) copy-start(bf16[320,3200]{1,0:T(8,128)(2,1)} %param.14) | copy-start | bytes 6144004
  25.9 2.2 %copy-start.1 = (bf16[3200,320]{0,1:T(8,128)(2,1)S(1)}, bf16[3200,320]{0,1:T(8,128)(2,1)}, u32[]{:S(2)}) copy-start(bf16[3200,320]{0,1:T(8,128)(2,1)} %param.15) | copy-start | bytes 6144004
  25.9 19.2 %collective-permute-start.1 = (bf16[320,1664]{1,0:T(8,128)(2,1)}, bf16[320,1664]{1,0:T(8,128)(2,1)}, u32[]{:S(2)}, u32[]{:S(2)}) collective-permute-start(bf16[320,1664]{1,0:T(8,128)(2,1)} %broadcast_select_fusion.4), channel_id=1, source_target_pairs={{0,1},{1,0},{2,3},{3,2},{4,5},{5,4},{6,7},{7,6},{8,9},{9,8},{10,11... | collective-permute-start | bytes 3194888 | tf_op jit(solution)/shard_map/ppermute | solution.py:43
  28.1 18.9 %collective-permute-start.2 = (bf16[320,1664]{1,0:T(8,128)(2,1)}, bf16[320,1664]{1,0:T(8,128)(2,1)}, u32[]{:S(2)}, u32[]{:S(2)}) collective-permute-start(bf16[320,1664]{1,0:T(8,128)(2,1)} %broadcast_select_fusion.3), channel_id=1, source_target_pairs={{0,1},{1,0},{2,3},{3,2},{4,5},{5,4},{6,7},{7,6},{8,9},{9,8},{10,11... | collective-permute-start | bytes 3194888 | tf_op jit(solution)/shard_map/ppermute | solution.py:43
  29.2 19.6 %collective-permute-start.3 = (bf16[1664,320]{0,1:T(8,128)(2,1)}, bf16[1664,320]{0,1:T(8,128)(2,1)}, u32[]{:S(2)}, u32[]{:S(2)}) collective-permute-start(bf16[1664,320]{0,1:T(8,128)(2,1)} %broadcast_select_fusion.2), channel_id=1, source_target_pairs={{0,1},{1,0},{2,3},{3,2},{4,5},{5,4},{6,7},{7,6},{8,9},{9,8},{10,11... | collective-permute-start | bytes 3194888 | tf_op jit(solution)/shard_map/ppermute | solution.py:43
  40.5 89.0 %copy-start.7 = (bf16[256,640]{1,0:T(8,128)(2,1)}, bf16[256,640]{1,0:T(8,128)(2,1)S(1)}, u32[]{:S(2)}) copy-start(bf16[256,640]{1,0:T(8,128)(2,1)S(1)} %convolution_convert_fusion.4) | copy-start | bytes 983044
  40.5 2.7 %copy-start.4 = (bf16[320,3200]{1,0:T(8,128)(2,1)S(1)}, bf16[320,3200]{1,0:T(8,128)(2,1)}, u32[]{:S(2)}) copy-start(bf16[320,3200]{1,0:T(8,128)(2,1)} %param.14) | copy-start | bytes 6144004
  42.9 1.6 %copy-start.2 = (bf16[3200,320]{0,1:T(8,128)(2,1)S(1)}, bf16[3200,320]{0,1:T(8,128)(2,1)}, u32[]{:S(2)}) copy-start(bf16[3200,320]{0,1:T(8,128)(2,1)} %param.15) | copy-start | bytes 6144004
  42.9 2.3 %collective-permute-start = (bf16[256,640]{1,0:T(8,128)(2,1)S(1)}, bf16[256,640]{1,0:T(8,128)(2,1)S(1)}, u32[]{:S(2)}, u32[]{:S(2)}) collective-permute-start(bf16[256,640]{1,0:T(8,128)(2,1)S(1)} %convolution_convert_fusion.4), channel_id=1, source_target_pairs={{0,1},{1,0},{2,3},{3,2},{4,5},{5,4},{6,7},{7,6},{8,9},{9,8},{10,11... | collective-permute-start | bytes 983048 | tf_op jit(solution)/shard_map/ppermute | solution.py:71
  85.0 35.4 %copy-start.9 = (s32[1,1,4]{2,1,0:T(1,128)S(1)}, s32[1,1,4]{2,1,0:T(1,128)}, u32[]{:S(2)}) copy-start(s32[1,1,4]{2,1,0:T(1,128)} %param.11) | copy-start | bytes 52
  117.1 9.5 %collective-permute-start.4 = (bf16[256,4992]{1,0:T(8,128)(2,1)S(1)}, bf16[256,4992]{1,0:T(8,128)(2,1)S(1)}, u32[]{:S(2)}, u32[]{:S(2)}) collective-permute-start(bf16[256,4992]{1,0:T(8,128)(2,1)S(1)} %bitcast.30), channel_id=1, source_target_pairs={{0,1},{1,0},{2,3},{3,2},{4,5},{5,4},{6,7},{7,6},{8,9},{9,8},{10,11... | collective-permute-start | bytes 7667720 | tf_op jit(solution)/shard_map/ppermute | solution.py:90
  137.7 16.6 %all-to-all-start.3 = ((bf16[128,4,320]{2,1,0:T(4,128)(2,1)}), bf16[128,4,320]{2,1,0:T(4,128)(2,1)S(1)}, u32[]{:S(2)}, u32[]{:S(2)}) async-start(bf16[128,4,320]{2,1,0:T(4,128)(2,1)} %reshape.148), calls=%async_computation.3 | async-start | bytes 786432 | tf_op jit(solution)/shard_map/all_to_all | solution.py:103
  141.6 3.1 %copy-start.5 = (bf16[256,1664]{1,0:T(8,128)(2,1)S(1)}, bf16[256,1664]{1,0:T(8,128)(2,1)}, u32[]{:S(2)}) copy-start(bf16[256,1664]{1,0:T(8,128)(2,1)} %get-tuple-element.10) | copy-start | bytes 2555908
  141.6 3.1 %copy-start.6 = (bf16[256,1536]{1,0:T(8,128)(2,1)S(1)}, bf16[256,1536]{1,0:T(8,128)(2,1)}, u32[]{:S(2)}) copy-start(bf16[256,1536]{1,0:T(8,128)(2,1)} %get-tuple-element.13) | copy-start | bytes 2359300
  141.6 3.1 %copy-start.8 = (bf16[256,640]{1,0:T(8,128)(2,1)S(1)}, bf16[256,640]{1,0:T(8,128)(2,1)}, u32[]{:S(2)}) copy-start(bf16[256,640]{1,0:T(8,128)(2,1)} %copy-done.7) | copy-start | bytes 983044

commit v2 on v1

v2 whole, which is shorter than its diff:
```python
import jax
import jax.numpy as jnp
from jax import lax
from jax.experimental import pallas as pl
from jax.experimental.pallas import tpu as pltpu
from jax.sharding import Mesh, PartitionSpec as P

AXES = ("y", "zh", "x", "zl", "c")
SIZES = (4, 2, 4, 2, 2)
N_DP, N_FSDP, N_DEV = 8, 16, 128
CAP = 4
GROUP = 32
LIVE = N_DP * GROUP
ROWS = 128
D = 5120
DL = 320
FL = 3200
WIN = 1664
HI = FL - WIN
TILE = WIN - HI
NA, NB = 768, 896
FAR = 512
MSG = 384
SWAP = [(0, 1), (1, 0)]
BF, F32 = jnp.bfloat16, jnp.float32
SMEM = pl.BlockSpec(memory_space=pltpu.SMEM)
VMEM = pl.BlockSpec(memory_space=pltpu.VMEM)
ANY = pl.BlockSpec(memory_space=pl.ANY)
ORDER = ((0, 0), (0, 1), (1, 0), (3, 0), (2, 0), (1, 1), (3, 1), (2, 1))


def limits(mib):
    return pltpu.CompilerParams(vmem_limit_bytes=mib * 2**20)


def cost(flops, moved):
    return pl.CostEstimate(flops=flops, bytes_accessed=moved, transcendentals=0)


def dot(a, b, ca, cb):
    return lax.dot_general(a, b, (((ca,), (cb,)), ((), ())), preferred_element_type=F32)


def along(t, step):
    return lax.ppermute(t, "x", [(i, (i + step) % 4) for i in range(4)])


def up(t):
    return along(t, 1)


def down(t):
    return along(t, 3)


def ring_y(t, step):
    return lax.ppermute(t, "y", [(i, (i + step) % 4) for i in range(4)])


def across(t):
    return lax.ppermute(t, "zl", SWAP)


def sibling(t):
    return lax.ppermute(t, "c", SWAP)


def call(kernel, shapes, operands, scratch=(), mib=24, estimate=None, smem=0, out_specs=None):
    return pl.pallas_call(
        kernel,
        out_shape=[jax.ShapeDtypeStruct(s, k) for s, k in shapes],
        in_specs=[SMEM] * smem + [VMEM] * (len(operands) - smem),
        out_specs=out_specs or [VMEM] * len(shapes),
        scratch_shapes=list(scratch),
        compiler_params=limits(mib),
        cost_estimate=estimate,
    )(*operands)


def message_kernel(index, chosen_in, counts_in, advantage_in, tokens, cotangent, out,
                   chosen, counts, advantage, x_rows, y_rows, small, big):
    first = [
        pltpu.make_async_copy(chosen_in, chosen, small.at[0]),
        pltpu.make_async_copy(counts_in, counts, small.at[1]),
        pltpu.make_async_copy(advantage_in, advantage, small.at[2]),
    ]
    for copy in first:
        copy.start()
    for copy in first:
        copy.wait()
    copies = []
    for s in range(CAP):
        block = pl.ds(pl.multiple_of(chosen[0, 0, s] // 16 * 16, 16), 16)
        here = pl.ds(s * 16, 16)
        copies.append(pltpu.make_async_copy(tokens.at[block], x_rows.at[here], big.at[s]))
        copies.append(pltpu.make_async_copy(cotangent.at[block], y_rows.at[here], big.at[CAP + s]))
    for copy in copies:
        copy.start()
    f = index[0]
    count = counts[0, f]
    before = jnp.int32(0)
    for j in range(N_FSDP):
        before = before + jnp.where(j < f, counts[0, j], 0)
    row = lax.broadcasted_iota(jnp.int32, (2 * CAP, CAP * 16), 0)
    lane = lax.broadcasted_iota(jnp.int32, (2 * CAP, CAP * 16), 1)
    line = lax.broadcasted_iota(jnp.int32, (2 * CAP, 1), 0)
    wide = lax.broadcasted_iota(jnp.int32, (2 * CAP, MSG - DL), 0)
    lane_of = lax.broadcasted_iota(jnp.int32, (2 * CAP, MSG - DL), 1)
    take_x = jnp.zeros((2 * CAP, CAP * 16), F32)
    take_y = jnp.zeros((2 * CAP, CAP * 16), F32)
    scale = jnp.zeros((2 * CAP, 1), F32)
    place = jnp.where(lane_of == 0, float(FAR), 0.0)
    for s in range(CAP):
        r = chosen[0, 0, s]
        one = jnp.where(s < count, 1.0, 0.0).astype(F32)
        at = r % 16 + s * 16
        take_x = jnp.where((row == s) & (lane == at), one, take_x)
        take_y = jnp.where((row == s + CAP) & (lane == at), one, take_y)
        scale = jnp.where(line == s + CAP, advantage[r], scale)
        spot = jnp.where(s < count, before + s, FAR).astype(F32)
        place = jnp.where((wide == s) & (lane_of == 0), spot, place)
        place = jnp.where((wide == s + CAP) & (lane_of == 0), spot + GROUP, place)
        slot = (f * CAP + s + 1).astype(F32)
        place = jnp.where((wide == s) & (lane_of == 1), slot, place)
    for copy in copies:
        copy.wait()
    x = dot(take_x.astype(BF), x_rows[...], 1, 0)
    y = dot(take_y.astype(BF), y_rows[...], 1, 0) * scale
    both = (x + y).astype(BF)
    place = place.astype(BF)
    for k in range(N_FSDP):
        out[k, :, 0:DL] = both[:, k * DL : (k + 1) * DL]
        out[k, :, DL:MSG] = place


def messages(*operands):
    return pl.pallas_call(
        message_kernel,
        out_shape=jax.ShapeDtypeStruct((N_FSDP, 2 * CAP, MSG), BF),
        in_specs=[SMEM] + [ANY] * 5,
        out_specs=VMEM,
        scratch_shapes=[
            pltpu.SMEM((1, 1, CAP), jnp.int32),
            pltpu.SMEM((1, N_FSDP), jnp.int32),
            pltpu.SMEM((ROWS,), F32),
            pltpu.VMEM((CAP * 16, D), BF),
            pltpu.VMEM((CAP * 16, D), BF),
            pltpu.SemaphoreType.DMA((3,)),
            pltpu.SemaphoreType.DMA((2 * CAP,)),
        ],
        compiler_params=limits(60),
    )(*operands)


def pack_kernel(lines, out):
    spot = lax.broadcasted_iota(jnp.int32, (N_FSDP * 2 * CAP, 2 * GROUP), 1)
    place = lines[:, DL : DL + 1].astype(jnp.int32)
    out[...] = dot(jnp.where(place == spot, 1.0, 0.0).astype(BF), lines[...], 0, 0).astype(BF)


FROM_Y = (0, 3, 1, 2)


def gather_rows(index, rows, order, x, y=None):
    for k, (dx, dz) in enumerate(order):
        i = (index[1] + dx) % 4 * 2 + (index[2] + dz) % 2
        here = slice(k * GROUP, (k + 1) * GROUP)
        x[here, :] = rows[i, 0:GROUP, :]
        if y is not None:
            y[here, :] = rows[i, GROUP : 2 * GROUP, :]


RELATIVE = tuple((dx, dz) for dx in range(4) for dz in range(2))


def products(index, own, sib, weights, lo, n, scratch, store):
    xo, yo, xs, ys, tail = scratch
    gather_rows(index, own, RELATIVE, xo, yo)
    gather_rows(index, sib, RELATIVE, xs, ys)
    for k in range(3):
        a, b = (xo, xs) if k < 2 else (yo, ys)
        ends = jnp.concatenate([a[:, 256:DL], b[:, 256:DL]], axis=1)
        mine, other = weights[2 * k], weights[2 * k + 1]
        tail[0 : DL - 256, 0:n] = mine[256:DL, lo : lo + n]
        tail[DL - 256 : 128, 0:n] = other[256:DL, lo : lo + n]
        for at in range(0, n, 256):
            to = min(at + 256, n)
            total = dot(a[:, 0:256], mine[0:256, lo + at : lo + to], 1, 0)
            total += dot(b[:, 0:256], other[0:256, lo + at : lo + to], 1, 0)
            total += dot(ends, tail[:, at:to], 1, 0)
            store(slice(k * n + at, k * n + to), total)


def kernel_b(index, own, sib, w0, w1, w2, w3, w4, w5, far, near, *scratch):
    def store(cols, total):
        for dx in range(4):
            here, near_at = slice(dx * GROUP, (dx + 1) * GROUP), 2 * dx * GROUP
            near[here, cols] = total[near_at : near_at + GROUP]
            far[here, cols] = total[near_at + GROUP : near_at + 2 * GROUP].astype(BF)

    products(index, own, sib, (w0, w1, w2, w3, w4, w5), NA, NB, scratch, store)


def kernel_a(index, own, sib, w0, w1, w2, w3, w4, w5, here, right, two, left, *scratch):
    def store(cols, total):
        here[:, cols] = total[0 : 2 * GROUP]
        for k, out in enumerate((right, two, left)):
            out[:, cols] = total[(k + 1) * 2 * GROUP : (k + 2) * 2 * GROUP].astype(BF)

    products(index, own, sib, (w0, w1, w2, w3, w4, w5), 0, NA, scratch, store)


def local_products(kernel, n, shapes, *operands):
    rows = pltpu.VMEM((LIVE, MSG), BF)
    return call(
        kernel,
        [((r, 3 * n), kind) for r, kind in shapes],
        operands,
        scratch=[rows] * 4 + [pltpu.VMEM((128, n), BF)],
        smem=1,
        estimate=cost(2 * LIVE * 2 * DL * 3 * n, 10 * 2**20),
    )


def sum_b_kernel(near, far, here, right, two, left):
    here[...] = near[0:GROUP] + far[0:GROUP].astype(F32)
    for k, out in enumerate((right, two, left)):
        rows = slice((k + 1) * GROUP, (k + 2) * GROUP)
        out[...] = (near[rows] + far[rows].astype(F32)).astype(BF)


def sum_a_kernel(mine, a, b, c, here, far):
    def total(rows):
        return mine[rows] + a[rows].astype(F32) + b[rows].astype(F32) + c[rows].astype(F32)

    here[...] = total(slice(0, GROUP))
    far[...] = total(slice(GROUP, 2 * GROUP)).astype(BF)


def swiglu_backward(gate_pre, up_pre, hidden_delta):
    sigma = jax.nn.sigmoid(gate_pre)
    active = gate_pre * sigma
    hidden = active * up_pre
    gate_delta = hidden_delta * up_pre * sigma * (1.0 + gate_pre * (1.0 - sigma))
    up_delta = hidden_delta * active
    return hidden, gate_delta, up_delta


def value_kernel(index, mine_a, far_a, mine_b, right, two, left, out):
    sums_a = mine_a[...] + far_a[...].astype(F32)
    sums_b = mine_b[...] + right[...].astype(F32) + two[...].astype(F32) + left[...].astype(F32)
    of_a = swiglu_backward(*[sums_a[:, k * NA : (k + 1) * NA] for k in range(3)])
    of_b = swiglu_backward(*[sums_b[:, k * NB : (k + 1) * NB] for k in range(3)])
    unit = lax.broadcasted_iota(jnp.int32, (GROUP, NA), 1)
    keep = (unit >= TILE) | (index[3] == 0)
    for k in range(3):
        out[:, k * WIN : k * WIN + NA] = jnp.where(keep, of_a[k], 0.0).astype(BF)
        out[:, k * WIN + NA : (k + 1) * WIN] = of_b[k].astype(BF)


def split_kernel(a, b, c, *outs):
    for k, (ref, out) in enumerate(zip((a, b, c), outs)):
        out[...] = ref[:, k * WIN : (k + 1) * WIN]


def back_product(value, gate, up_w):
    return dot(value[:, WIN : 2 * WIN], gate[...], 1, 1) + dot(value[:, 2 * WIN :], up_w[...], 1, 1)


def lay_kernel(*refs):
    blocks, (gate, up_w, value, out) = refs[:-4], refs[-4:]
    for k in range(3 + (len(blocks) == 4)):
        value[k * GROUP : (k + 1) * GROUP, :] = blocks[k][...]
    if len(blocks) > 4:
        for k in range(3):
            value[3 * GROUP :, k * WIN : (k + 1) * WIN] = blocks[3 + k][...]
    out[...] = back_product(value, gate, up_w)


def back_kernel(value, gate, up_w, out):
    out[...] = back_product(value, gate, up_w)


def back_products(blocks, gate_own, gate_sib, up_own, up_sib):
    rows = 4 * GROUP
    price = cost(2 * rows * DL * 2 * WIN, 4 * 2**20)
    value, other = call(
        lay_kernel,
        [((rows, 3 * WIN), BF), ((rows, DL), F32)],
        [*blocks, gate_sib, up_sib],
        estimate=price,
    )
    mine = call(back_kernel, [((rows, DL), F32)], [value, gate_own, up_own], estimate=price)[0]
    return value, mine, sibling(other)


def unpack_kernel(index, own, mine_e, other_e, mine_l, other_l, out):
    half = DL // 2
    parts = []
    for k, (dx, dz) in enumerate(ORDER):
        i = (index[1] + dx) % 4 * 2 + (index[2] + dz) % 2
        step = sum(jnp.where(i // 2 == j, FROM_Y[j], 0) for j in range(4))
        to = (index[4] + step) % 4 * 2 + (index[5] + i % 2) % 2
        slot = own[i, 0:GROUP, MSG - 128 : MSG].astype(F32)[:, DL + 1 - (MSG - 128) : DL + 2 - (MSG - 128)]
        slot = slot.astype(jnp.int32) - 1
        line = to * (N_FSDP * 2 * CAP) + slot // CAP * (2 * CAP) + slot % CAP
        parts.append(jnp.where(slot < 0, -2 * CAP, line).astype(F32))
    line = jnp.broadcast_to(jnp.concatenate(parts, axis=0), (LIVE, 128))
    line = jnp.transpose(line)[0:1, :].astype(jnp.int32)
    back = jnp.concatenate([mine_e[...] + other_e[...], mine_l[...] + other_l[...]]).astype(BF)
    at = lax.broadcasted_iota(jnp.int32, (2 * CAP * N_DEV, LIVE), 0)
    low = jnp.where(at == line, 1.0, 0.0).astype(BF)
    high = jnp.where(at == line + CAP, 1.0, 0.0).astype(BF)
    out[...] = (dot(low, back[:, :half], 1, 0) + dot(high, back[:, half:], 1, 0)).astype(BF)


def grad_kernel(index, own_in, early_in, late_in, early_other_in, late_other_in, gate_out, up_out,
                down_out, own, mine, other, x, y, gate, up_s, down_s, reads, sems):
    top, bottom = pl.ds(0, 4 * GROUP), pl.ds(4 * GROUP, 4 * GROUP)
    loads = [
        pltpu.make_async_copy(own_in, own, reads.at[0]),
        pltpu.make_async_copy(early_in, mine.at[top], reads.at[1]),
        pltpu.make_async_copy(late_in, mine.at[bottom], reads.at[2]),
        pltpu.make_async_copy(early_other_in, other.at[top], reads.at[3]),
        pltpu.make_async_copy(late_other_in, other.at[bottom], reads.at[4]),
    ]
    for copy in loads:
        copy.start()
    c = index[3]
    loads[0].wait()
    gather_rows(index, own, ORDER, x, y)
    for copy in loads[1:]:
        copy.wait()
    starts = [pl.multiple_of(c * HI, 128), pl.multiple_of((1 - c) * HI, 128)]
    spans = [(lo, min(lo + 512, WIN)) for lo in range(0, WIN, 512)]
    copies = []
    for k, (scratch, result) in enumerate(((gate, gate_out), (up_s, up_out), (down_s, down_out))):
        part = (k + 1) % 3
        rows = (x if k < 2 else y)[:, 0:DL]

        def product(ref, lo, hi):
            return dot(rows, ref[:, part * WIN + lo : part * WIN + hi], 0, 0).astype(BF)

        for start, ref in zip(starts, (mine, other)):
            for lo, hi in spans:
                scratch[:, pl.ds(start + lo, hi - lo)] = product(ref, lo, hi)

        @pl.when(c == 0)
        def _():
            scratch[:, HI:WIN] = product(mine, HI, WIN)

        @pl.when(c == 1)
        def _():
            scratch[:, HI:WIN] = product(other, HI, WIN)

        copies.append(pltpu.make_async_copy(scratch, result, sems.at[k]))
        copies[-1].start()
    for copy in copies:
        copy.wait()


def weight_grads(*operands):
    rows, grad = pltpu.VMEM((LIVE, MSG), BF), pltpu.VMEM((DL, FL), BF)
    values = pltpu.VMEM((LIVE, 3 * WIN), BF)
    return pl.pallas_call(
        grad_kernel,
        out_shape=[jax.ShapeDtypeStruct((DL, FL), BF)] * 3,
        in_specs=[SMEM] + [ANY] * 5,
        out_specs=[ANY] * 3,
        scratch_shapes=[
            pltpu.VMEM((N_DP, 2 * GROUP, MSG), BF),
            values, values, rows, rows, grad, grad, grad,
            pltpu.SemaphoreType.DMA((5,)),
            pltpu.SemaphoreType.DMA((3,)),
        ],
        compiler_params=limits(60),
        cost_estimate=cost(2 * LIVE * DL * FL * 3, 12 * 2**20),
    )(*operands)


def shards(tokens, cotangent, advantage, chosen, chosen_count, gate_weight, up_weight, down_weight):
    c = lax.axis_index("c")
    first = c == 0
    f_index = lax.axis_index(("x", "zl", "c"))
    place = [f_index, *[lax.axis_index(a) for a in ("x", "zl", "c", "y", "zh")]]
    index = jnp.stack(place).astype(jnp.int32)
    message = messages(index, chosen, chosen_count, advantage, tokens, cotangent)
    message, gate_weight, up_weight, down_weight, chosen, chosen_count = lax.optimization_barrier(
        (message, gate_weight, up_weight, down_weight, chosen, chosen_count)
    )
    got = lax.all_to_all(message, ("x", "zl", "c"), 0, 0, tiled=True)
    packed = call(pack_kernel, [((2 * GROUP, MSG), BF)], [got.reshape(N_FSDP * 2 * CAP, MSG)])[0]
    packed = jnp.stack([packed, lax.ppermute(packed, "zh", SWAP)])
    own = jnp.concatenate([packed, ring_y(packed, 1), ring_y(packed, 3), ring_y(packed, 2)])
    sib = sibling(own)

    def window(w):
        lo, hi = w[:, :WIN], w[:, HI:]
        return jnp.where(first, lo, hi), sibling(jnp.where(first, hi, lo))

    weights = [*window(gate_weight), *window(up_weight), *window(down_weight.T)]
    rows = chosen[0, 0]
    live = jnp.arange(CAP, dtype=jnp.int32) < chosen_count[0][f_index]
    owner = ((jnp.arange(ROWS, dtype=jnp.int32)[:, None] == rows[None, :]) & live[None, :]).astype(BF)

    far, near = local_products(
        kernel_b, NB, [(4 * GROUP, BF), (4 * GROUP, F32)], index, own, sib, *weights
    )
    own_a, near = lax.optimization_barrier((own, near))
    here_a, right, two, left = local_products(
        kernel_a, NA, [(2 * GROUP, F32)] + [(2 * GROUP, BF)] * 3, index, own_a, sib, *weights
    )
    far = across(far)
    right, left, two = up(right), down(left), along(two, 2)
    shape_a, shape_b = (GROUP, 3 * NA), (GROUP, 3 * NB)
    here_b, right_b, two_b, left_b = call(
        sum_b_kernel, [(shape_b, F32)] + [(shape_b, BF)] * 3, [near, far]
    )
    here_a, far_a = call(sum_a_kernel, [(shape_a, F32), (shape_a, BF)], [here_a, right, two, left])
    far_a = across(far_a)
    right_b, left_b, two_b = up(right_b), down(left_b), along(two_b, 2)
    v00 = call(
        value_kernel,
        [((GROUP, 3 * WIN), BF)],
        [index, here_a, far_a, here_b, right_b, two_b, left_b],
        smem=1,
    )[0]

    v01, v30, v10 = across(v00), up(v00), down(v00)
    v20, v11, v31 = down(v10), across(v10), up(v01)
    part = ((GROUP, WIN), BF)
    t20, t31, t11 = call(split_kernel, [part] * 3, [v20, v31, v11])
    v21 = [across(t20), up(t31), down(t11)]
    early, mine_e, other_e = back_products([v00, v01, v10, v30], *weights[:4])
    late, mine_l, other_l = back_products([v20, v11, v31, *v21], *weights[:4])
    early_other, late_other = sibling(early), sibling(late)

    back = call(
        unpack_kernel,
        [((2 * CAP * N_DEV, DL // 2), BF)],
        [index, own, mine_e, other_e, mine_l, other_l],
        smem=1,
        estimate=cost(8 * N_DEV * 2 * LIVE * DL, 2**20),
    )[0]
    back, early_other, late_other = lax.optimization_barrier((back, early_other, late_other))
    back = lax.all_to_all(back.reshape(N_DEV, 2 * CAP, DL // 2), AXES, 0, 0, tiled=True)

    gate_grad, up_grad, down_grad = weight_grads(index, own, early, late, early_other, late_other)

    back = jnp.sum(back.reshape(N_DP, N_FSDP, 2, CAP, DL // 2).astype(F32), axis=0).astype(BF)
    back = back.transpose(2, 0, 1, 3).reshape(CAP, D)
    input_grad = dot(owner, back, 1, 0).astype(BF)
    return (input_grad, gate_grad, up_grad, down_grad.T)


def solution(mesh):
    fine = Mesh(mesh.devices.reshape(SIZES), AXES)
    dp, fsdp = AXES[:2], AXES[2:]
    in_specs = (
        P(AXES, None),
        P(AXES, None),
        P(AXES),
        P(dp, fsdp, None),
        P(dp, None),
        P(fsdp, dp),
        P(fsdp, dp),
        P(dp, fsdp),
    )
    out_specs = (P(AXES, None), P(fsdp, dp), P(fsdp, dp), P(dp, fsdp))
    return jax.shard_map(shards, mesh=fine, in_specs=in_specs, out_specs=out_specs, check_vma=False)
```

time: 158 us -> 137 us (0.87)
  blocking collectives: 65.4 us -> 0 us
  starting transfers between devices: 20.9 us -> 52.5 us
  waiting for transfers between devices: 17.1 us -> 46.3 us
  Pallas kernels: 0 us -> 26.8 us
  matrix products: 21 us -> 1.53 us
  other arithmetic: 17.6 us -> 4.65 us
  local copies, waits for them, and re-layouts: 13.7 us -> 3.9 us
    all_to_all x2 -> x0, blocking collectives: 65.4 us -> none  [the longest x1 33.3 us: shards(): share = lax.all_to_all(parts, ('x', 'zl'), 0, 0, tiled=True)]
    ppermute x5 -> x29, waiting for transfers between devices: 0.01 us -> 41 us  [the longest x12 19.3 us: along(): return lax.ppermute(t, 'x', [(i, (i + step) % 4) for i in range(4)])]
    ppermute x5 -> x29, starting transfers between devices: 5.53 us -> 36.5 us  [the longest x12 14 us: along(): return lax.ppermute(t, 'x', [(i, (i + step) % 4) for i in range(4)])]
    pallas_call x0 -> x14, Pallas kernels: none -> 26.8 us  [the longest x12 15.1 us: call(): pl.pallas_call(kernel, out_shape=[jax.ShapeDtypeStruct(s, k) for s, k in...]
    dot_general x12 -> x1, matrix products: 21 us -> 1.53 us  [dot(): lax.dot_general(a, b, (((ca,), (cb,)), ((), ())), preferred_element_type=...]
    all_to_all x2, waiting for transfers between devices: 17.1 us -> 5.32 us  [the longest x1 4.98 us: shards(): lax.all_to_all(back.reshape(N_DEV, 2 * CAP, DL // 2), AXES, 0, 0, tiled=T...]
    and x2 -> x0, other arithmetic: 5.02 us -> none  [shards(): (row == rows[s]) & live[s]]
    gather x4 -> x0, local copies, waits for them, and re-layouts: 4.11 us -> none  [the longest x2 2.22 us: shards(): picked = jnp.where(live[:, None], tokens[rows], jnp.zeros((), BF))]
  transfers between devices with their start and end apart: 7 -> 31, of which waited for: 2 -> 16; matrix products, arithmetic and copies ran while one was open for 16% -> 4% of each run, Pallas kernels for 0% -> 14%
where the time goes in v2:
time: 137 us
  starting transfers between devices  52.5 us (38%)
  waiting for transfers between devices  46.3 us (34%)
  Pallas kernels  26.8 us (20%)
  other arithmetic  4.65 us (3%)
  local copies, waits for them, and re-layouts  3.9 us (3%)
  matrix products  1.53 us (1%)
    ppermute x12, waiting for transfers between devices, along(): return lax.ppermute(t, 'x', [(i, (i + step) % 4) for i in range(4)])  19.3 us
    pallas_call x12, Pallas kernels, call(): pl.pallas_call(kernel, out_shape=[jax.ShapeDtypeStruct(s, k) for s, k in...  15.1 us
    ppermute x12, starting transfers between devices, along(): return lax.ppermute(t, 'x', [(i, (i + step) % 4) for i in range(4)])  14 us
    ppermute x5, waiting for transfers between devices, across(): return lax.ppermute(t, 'zl', SWAP)  12.8 us
    ppermute x8, starting transfers between devices, sibling(): return lax.ppermute(t, 'c', SWAP)  10.2 us
    all_to_all x1, starting transfers between devices, shards(): lax.all_to_all(back.reshape(N_DEV, 2 * CAP, DL // 2), AXES, 0, 0, tiled=T...  8.82 us
    pallas_call x1, Pallas kernels, weight_grads(): pl.pallas_call(grad_kernel, out_shape=[jax.ShapeDtypeStruct((DL, FL), BF)...  7.75 us
    all_to_all x1, starting transfers between devices, shards(): got = lax.all_to_all(message, ('x', 'zl', 'c'), 0, 0, tiled=True)  7.18 us
  transfers between devices with their start and end apart: 31, of which 16 were waited for; matrix products, arithmetic and copies ran while one was open for 4% of the time, Pallas kernels for 14%

profile of v2, /device:TPU:1, one launch (start us, length us, event | category | flops | bytes accessed | tf_op | source)
XLA Modules:
  0.0 136.7 jit_solution(1605152307587083893)
XLA Ops:
  0.6 0.6 stack.36.index
  1.2 4.0 %shard_map.111 = bf16[16,8,384]{2,1,0:T(8,128)(2,1)} custom-call(s32[6]{0:T(128)} %stack.36.index, s32[1,1,4]{2,1,0:T(1,128)} %chosen_in.1, s32[1,16]{1,0:T(1,128)} %counts_in.1, f32[128]{0:T(128)} %advantage_in.1, bf16[128,5120]{1,0:T(8,128)(2,1)} %tokens.1, bf16[128,5120]{1,0:T(8,128)(2,1)} %cotangent.1), custom_call_target="tpu_custom_call" | custom-call | tf_op jit(solution)/shard_map/pallas_call | solution.py:137
  5.2 7.2 %all-to-all-start = ((bf16[16,8,384]{2,1,0:T(8,128)(2,1)}), bf16[16,8,384]{2,1,0:T(8,128)(2,1)S(1)}, u32[]{:S(2)}, u32[]{:S(2)}) async-start(bf16[16,8,384]{2,1,0:T(8,128)(2,1)} %shard_map.111), calls=%async_computation | async-start | bytes 196608 | tf_op jit(solution)/shard_map/all_to_all | solution.py:391
  12.4 1.2 broadcast_select_fusion.4
  13.7 0.7 copy-done.6
  14.4 1.2 broadcast_select_fusion.2
  15.7 0.7 copy-done.7
  16.3 1.5 %broadcast_select_fusion = (bf16[320,1664]{1,0:T(8,128)(2,1)}, bf16[320,1664]{1,0:T(8,128)(2,1)}) fusion(pred[]{:T(512)S(6)} %eq.22, bf16[320,3200]{1,0:T(8,128)(2,1)S(1)} %bitcast.24), kind=kLoop, calls=%fused_computation.1 | loop fusion | flops 1064960 | bytes 4259841 | tf_op jit(solution)/shard_map/jit(_where)/select_n | solution.py:399
  18.0 0.3 all-to-all-done
  18.3 0.3 shard_map.112
  18.6 3.4 %collective-permute-start = (bf16[64,384]{1,0:T(8,128)(2,1)S(1)}, bf16[64,384]{1,0:T(8,128)(2,1)S(1)}, u32[]{:S(2)}, u32[]{:S(2)}) collective-permute-start(bf16[64,384]{1,0:T(8,128)(2,1)S(1)} %shard_map.112), channel_id=1, source_target_pairs={{0,16},{16,0},{1,17},{17,1},{2,18},{18,2},{3,19},{19,3},{4,20},{20... | collective-permute-start | bytes 147464 | tf_op jit(solution)/shard_map/ppermute | solution.py:393
  22.0 1.5 %collective-permute-done = bf16[64,384]{1,0:T(8,128)(2,1)S(1)} collective-permute-done((bf16[64,384]{1,0:T(8,128)(2,1)S(1)}, bf16[64,384]{1,0:T(8,128)(2,1)S(1)}, u32[]{:S(2)}, u32[]{:S(2)}) %collective-permute-start) | collective-permute-done | bytes 49184 | tf_op jit(solution)/shard_map/ppermute | solution.py:393
  23.5 1.4 collective-permute-start.1
  24.8 1.5 %collective-permute-start.2 = (bf16[2,64,384]{2,1,0:T(8,128)(2,1)S(1)}, bf16[2,64,384]{2,1,0:T(8,128)(2,1)S(1)}, u32[]{:S(2)}, u32[]{:S(2)}) collective-permute-start(bf16[2,64,384]{2,1,0:T(8,128)(2,1)S(1)} %pad_maximum_fusion), channel_id=1, source_target_pairs={{0,96},{32,0},{64,32},{96,64},{1,97},{33,1},{65,33},{97,65},{2,98}... | collective-permute-start | bytes 294920 | tf_op jit(solution)/shard_map/ppermute | solution.py:57
  26.4 1.9 %collective-permute-done.1 = bf16[2,64,384]{2,1,0:T(8,128)(2,1)S(1)} collective-permute-done((bf16[2,64,384]{2,1,0:T(8,128)(2,1)S(1)}, bf16[2,64,384]{2,1,0:T(8,128)(2,1)S(1)}, u32[]{:S(2)}, u32[]{:S(2)}) %collective-permute-start.1) | collective-permute-done | bytes 98336 | tf_op jit(solution)/shard_map/ppermute | solution.py:57
  28.3 1.6 %collective-permute-start.3 = (bf16[2,64,384]{2,1,0:T(8,128)(2,1)S(1)}, bf16[2,64,384]{2,1,0:T(8,128)(2,1)S(1)}, u32[]{:S(2)}, u32[]{:S(2)}) collective-permute-start(bf16[2,64,384]{2,1,0:T(8,128)(2,1)S(1)} %pad_maximum_fusion), channel_id=1, source_target_pairs={{0,64},{32,96},{64,0},{96,32},{1,65},{33,97},{65,1},{97,33},{2,66}... | collective-permute-start | bytes 294920 | tf_op jit(solution)/shard_map/ppermute | solution.py:57
  30.0 3.3 %collective-permute-done.3 = bf16[2,64,384]{2,1,0:T(8,128)(2,1)S(1)} collective-permute-done((bf16[2,64,384]{2,1,0:T(8,128)(2,1)S(1)}, bf16[2,64,384]{2,1,0:T(8,128)(2,1)S(1)}, u32[]{:S(2)}, u32[]{:S(2)}) %collective-permute-start.3) | collective-permute-done | bytes 98336 | tf_op jit(solution)/shard_map/ppermute | solution.py:57
  33.3 3.7 %collective-permute-start.4 = (bf16[8,64,384]{2,1,0:T(8,128)(2,1)S(1)}, bf16[8,64,384]{2,1,0:T(8,128)(2,1)S(1)}, u32[]{:S(2)}, u32[]{:S(2)}) collective-permute-start(bf16[8,64,384]{2,1,0:T(8,128)(2,1)S(1)} %constant_dynamic-update-slice_fusion.own.own_in), channel_id=1, source_target_pairs={{0,1},{1,0},{2,3},{3,2},{4,5},{5,4},{6,7},{7,6},{8,9},{9,8},{10,11... | collective-permute-start | bytes 1179656 | tf_op jit(solution)/shard_map/ppermute | solution.py:65
  37.0 1.3 collective-permute-done.4.sib
  38.3 3.0 %shard_map.113 = (bf16[128,2688]{1,0:T(8,128)(2,1)S(1)}, f32[128,2688]{1,0:T(8,128)S(1)}) custom-call(s32[6]{0:T(128)S(1)} %copy-done.4, bf16[8,64,384]{2,1,0:T(8,128)(2,1)S(1)} %constant_dynamic-update-slice_fusion.own.own_in, bf16[8,64,384]{2,1,0:T(8,128)(2,1)S(1)} %collective-permute-done.4.sib, bf16[320,1664]{1,0:T(8,128)(2,1)S(1)} %get-tuple-element.75.w0.gate, ...), custom_call_target="tpu_custom_call" | custom-call | flops 880803840 | bytes 10485760 | tf_op jit(solution)/shard_map/pallas_call | solution.py:69
  41.3 1.0 collective-permute-start.12
  42.3 2.7 %shard_map.114 = (f32[64,2304]{1,0:T(8,128)S(1)}, bf16[64,2304]{1,0:T(8,128)(2,1)S(1)}, bf16[64,2304]{1,0:T(8,128)(2,1)S(1)}, bf16[64,2304]{1,0:T(8,128)(2,1)S(1)}) custom-call(s32[6]{0:T(128)S(1)} %copy-done.4, bf16[8,64,384]{2,1,0:T(8,128)(2,1)S(1)} %constant_dynamic-update-slice_fusion.own.own_in, bf16[8,64,384]{2,1,0:T(8,128)(2,1)S(1)} %collective-permute-done.4.sib, ...), custom_call_target="tpu_custom_call" | custom-call | flops 754974720 | bytes 10485760 | tf_op jit(solution)/shard_map/pallas_call | solution.py:69
  45.0 2.5 %collective-permute-start.10 = (bf16[64,2304]{1,0:T(8,128)(2,1)S(1)}, bf16[64,2304]{1,0:T(8,128)(2,1)S(1)}, u32[]{:S(2)}, u32[]{:S(2)}) collective-permute-start(bf16[64,2304]{1,0:T(8,128)(2,1)S(1)} %get-tuple-element.48), channel_id=1, source_target_pairs={{0,12},{4,0},{8,4},{12,8},{1,13},{5,1},{9,5},{13,9},{2,14},{6,2},{... | collective-permute-start | bytes 884744 | tf_op jit(solution)/shard_map/ppermute | solution.py:45
  47.5 1.8 %collective-permute-start.9 = (bf16[64,2304]{1,0:T(8,128)(2,1)S(1)}, bf16[64,2304]{1,0:T(8,128)(2,1)S(1)}, u32[]{:S(2)}, u32[]{:S(2)}) collective-permute-start(bf16[64,2304]{1,0:T(8,128)(2,1)S(1)} %get-tuple-element.47), channel_id=1, source_target_pairs={{0,8},{4,12},{8,0},{12,4},{1,9},{5,13},{9,1},{13,5},{2,10},{6,14},... | collective-permute-start | bytes 884744 | tf_op jit(solution)/shard_map/ppermute | solution.py:45
  49.3 8.8 %collective-permute-done.12.far = bf16[128,2688]{1,0:T(8,128)(2,1)S(1)} collective-permute-done((bf16[128,2688]{1,0:T(8,128)(2,1)S(1)}, bf16[128,2688]{1,0:T(8,128)(2,1)S(1)}, u32[]{:S(2)}, u32[]{:S(2)}) %collective-permute-start.12) | collective-permute-done | bytes 688160 | tf_op jit(solution)/shard_map/ppermute | solution.py:61
  58.2 1.2 collective-permute-start.13
  59.4 2.4 %collective-permute-start.14 = (bf16[32,2688]{1,0:T(8,128)(2,1)S(1)}, bf16[32,2688]{1,0:T(8,128)(2,1)S(1)}, u32[]{:S(2)}, u32[]{:S(2)}) collective-permute-start(bf16[32,2688]{1,0:T(8,128)(2,1)S(1)} %get-tuple-element.55), channel_id=1, source_target_pairs={{0,8},{4,12},{8,0},{12,4},{1,9},{5,13},{9,1},{13,5},{2,10},{6,14},... | collective-permute-start | bytes 516104 | tf_op jit(solution)/shard_map/ppermute | solution.py:45
  61.8 1.2 collective-permute-start.15
  63.0 0.1 shard_map.115
  63.1 1.0 collective-permute-start.11
  64.2 3.3 %collective-permute-done.11.far_a = bf16[32,2304]{1,0:T(8,128)(2,1)S(1)} collective-permute-done((bf16[32,2304]{1,0:T(8,128)(2,1)S(1)}, bf16[32,2304]{1,0:T(8,128)(2,1)S(1)}, u32[]{:S(2)}, u32[]{:S(2)}) %collective-permute-start.11) | collective-permute-done | bytes 147488 | tf_op jit(solution)/shard_map/ppermute | solution.py:61
  67.5 3.2 %collective-permute-done.13.right = bf16[32,2688]{1,0:T(8,128)(2,1)S(1)} collective-permute-done((bf16[32,2688]{1,0:T(8,128)(2,1)S(1)}, bf16[32,2688]{1,0:T(8,128)(2,1)S(1)}, u32[]{:S(2)}, u32[]{:S(2)}) %collective-permute-start.13) | collective-permute-done | bytes 172064 | tf_op jit(solution)/shard_map/ppermute | solution.py:45
  70.7 0.7 shard_map.117.refs_0_
  71.4 0.7 collective-permute-start.17
  72.1 0.9 collective-permute-start.16
  73.0 6.4 %collective-permute-done.17.refs_2_ = bf16[32,4992]{1,0:T(8,128)(2,1)S(1)} collective-permute-done((bf16[32,4992]{1,0:T(8,128)(2,1)S(1)}, bf16[32,4992]{1,0:T(8,128)(2,1)S(1)}, u32[]{:S(2)}, u32[]{:S(2)}) %collective-permute-start.17) | collective-permute-done | bytes 319520 | tf_op jit(solution)/shard_map/ppermute | solution.py:45
  79.4 1.4 collective-permute-start.20
  80.7 0.9 collective-permute-start.21
  81.6 0.2 collective-permute-start.18
  81.8 4.5 %collective-permute-done.20.a.refs_0_ = bf16[32,4992]{1,0:T(8,128)(2,1)S(1)} collective-permute-done((bf16[32,4992]{1,0:T(8,128)(2,1)S(1)}, bf16[32,4992]{1,0:T(8,128)(2,1)S(1)}, u32[]{:S(2)}, u32[]{:S(2)}) %collective-permute-start.20) | collective-permute-done | bytes 319520 | tf_op jit(solution)/shard_map/ppermute | solution.py:45
  86.3 0.6 collective-permute-done.21.c.refs_1_
  87.0 1.7 %collective-permute-done.22.b.refs_2_ = bf16[32,4992]{1,0:T(8,128)(2,1)S(1)} collective-permute-done((bf16[32,4992]{1,0:T(8,128)(2,1)S(1)}, bf16[32,4992]{1,0:T(8,128)(2,1)S(1)}, u32[]{:S(2)}, u32[]{:S(2)}) %collective-permute-start.22) | collective-permute-done | bytes 319520 | tf_op jit(solution)/shard_map/ppermute | solution.py:45
  88.7 0.7 collective-permute-start.23
  89.4 2.7 %collective-permute-start.25 = (bf16[32,1664]{1,0:T(8,128)(2,1)S(1)}, bf16[32,1664]{1,0:T(8,128)(2,1)S(1)}, u32[]{:S(2)}, u32[]{:S(2)}) collective-permute-start(bf16[32,1664]{1,0:T(8,128)(2,1)S(1)} %get-tuple-element.61), channel_id=1, source_target_pairs={{0,12},{4,0},{8,4},{12,8},{1,13},{5,1},{9,5},{13,9},{2,14},{6,2},{... | collective-permute-start | bytes 319496 | tf_op jit(solution)/shard_map/ppermute | solution.py:45
  92.0 3.6 %collective-permute-done.18.refs_3_ = bf16[32,4992]{1,0:T(8,128)(2,1)S(1)} collective-permute-done((bf16[32,4992]{1,0:T(8,128)(2,1)S(1)}, bf16[32,4992]{1,0:T(8,128)(2,1)S(1)}, u32[]{:S(2)}, u32[]{:S(2)}) %collective-permute-start.18) | collective-permute-done | bytes 319520 | tf_op jit(solution)/shard_map/ppermute | solution.py:45
  95.6 2.2 %shard_map.118 = (bf16[128,4992]{1,0:T(8,128)(2,1)S(1)}, f32[128,320]{1,0:T(8,128)S(1)}) custom-call(bf16[32,4992]{1,0:T(8,128)(2,1)S(1)} %shard_map.117.refs_0_, bf16[32,4992]{1,0:T(8,128)(2,1)S(1)} %collective-permute-done.16.refs_1_, bf16[32,4992]{1,0:T(8,128)(2,1)S(1)} %collective-permute-done.17.refs_2_, ...), custom_call_target="tpu_custom_call" | custom-call | flops 272629760 | bytes 4194304 | tf_op jit(solution)/shard_map/pallas_call | solution.py:69
  97.8 5.2 %collective-permute-start.27 = (bf16[128,4992]{1,0:T(8,128)(2,1)S(1)}, bf16[128,4992]{1,0:T(8,128)(2,1)S(1)}, u32[]{:S(2)}, u32[]{:S(2)}) collective-permute-start(bf16[128,4992]{1,0:T(8,128)(2,1)S(1)} %get-tuple-element.57.value.early_in), channel_id=1, source_target_pairs={{0,1},{1,0},{2,3},{3,2},{4,5},{5,4},{6,7},{7,6},{8,9},{9,8},{10,11... | collective-permute-start | bytes 3833864 | tf_op jit(solution)/shard_map/ppermute | solution.py:65
  103.0 2.1 %shard_map.121 = (bf16[128,4992]{1,0:T(8,128)(2,1)S(1)}, f32[128,320]{1,0:T(8,128)S(1)}) custom-call(bf16[32,4992]{1,0:T(8,128)(2,1)S(1)} %collective-permute-done.20.a.refs_0_, bf16[32,4992]{1,0:T(8,128)(2,1)S(1)} %collective-permute-done.21.c.refs_1_, bf16[32,4992]{1,0:T(8,128)(2,1)S(1)} %collective-permute-done.22.b.refs_2_, ...), custom_call_target="tpu_custom_call" | custom-call | flops 272629760 | bytes 4194304 | tf_op jit(solution)/shard_map/pallas_call | solution.py:69
  105.2 0.4 collective-permute-start.28
  105.6 0.2 collective-permute-start.19
  105.8 0.3 collective-permute-start.26
  106.1 0.9 shard_map.119.mine_e
  107.0 0.9 shard_map.122.mine_l
  107.9 0.6 collective-permute-done.19.other_e
  108.6 0.3 collective-permute-done.26.other_l
  108.8 2.0 %shard_map.123 = bf16[1024,160]{1,0:T(8,128)(2,1)} custom-call(s32[6]{0:T(128)S(1)} %copy-done.4, bf16[8,64,384]{2,1,0:T(8,128)(2,1)S(1)} %constant_dynamic-update-slice_fusion.own.own_in, f32[128,320]{1,0:T(8,128)S(1)} %shard_map.119.mine_e, f32[128,320]{1,0:T(8,128)S(1)} %collective-permute-done.19.other_e, f32[128,320]{1,0:T(8,128)S(1)} %shard_map.122.mine_l, ...), custom_call_target="tpu_custom_call" | custom-call | flops 167772160 | bytes 1048576 | tf_op jit(solution)/shard_map/pallas_call | solution.py:69
  110.9 1.0 copy-done.10
  111.9 8.8 %all-to-all-start.1 = ((bf16[128,8,160]{2,1,0:T(8,128)(2,1)}), bf16[128,8,160]{2,1,0:T(8,128)(2,1)S(1)}, u32[]{:S(2)}, u32[]{:S(2)}) async-start(bf16[128,8,160]{2,1,0:T(8,128)(2,1)} %bitcast.12), calls=%async_computation.1 | async-start | bytes 1048576 | tf_op jit(solution)/shard_map/all_to_all | solution.py:446
  120.8 0.6 constant_dynamic-slice_fusion
  121.4 0.6 iota_compare_fusion.1
  122.0 7.8 %shard_map.124 = (bf16[320,3200]{1,0:T(8,128)(2,1)}, bf16[320,3200]{1,0:T(8,128)(2,1)}, bf16[320,3200]{1,0:T(8,128)(2,1)}) custom-call(s32[6]{0:T(128)} %stack.36.index, bf16[8,64,384]{2,1,0:T(8,128)(2,1)} %copy-done.1, bf16[128,4992]{1,0:T(8,128)(2,1)} %copy-done.2, bf16[128,4992]{1,0:T(8,128)(2,1)} %copy-done.3, bf16[128,4992]{1,0:T(8,128)(2,1)} %copy-done.10, ...), custom_call_target="tpu_custom_call" | custom-call | flops 1572864000 | bytes 12582912 | tf_op jit(solution)/shard_map/pallas_call | solution.py:365
  129.8 5.0 %all-to-all-done.1 = bf16[128,8,160]{2,1,0:T(8,128)(2,1)S(1)} async-done(((bf16[128,8,160]{2,1,0:T(8,128)(2,1)}), bf16[128,8,160]{2,1,0:T(8,128)(2,1)S(1)}, u32[]{:S(2)}, u32[]{:S(2)}) %all-to-all-start.1) | async-done | bytes 327712 | tf_op jit(solution)/shard_map/all_to_all | solution.py:446
  135.0 0.1 reshape.30
  135.1 1.5 %convolution_convert_fusion = bf16[128,5120]{1,0:T(8,128)(2,1)} fusion(bf16[4,5120]{1,0:T(4,128)(2,1)S(1)} %reshape.30, s32[4]{0:T(128)S(1)} %bitcast.28, pred[4]{0:T(512)(128)(4,1)S(1)} %iota_compare_fusion.1), kind=kOutput, calls=%fused_computation | convolution fusion | flops 5899264 | bytes 1351700 | tf_op jit(solution)/shard_map/dot_general | solution.py:41
  (53 shorter events, 0.8 us)
Async XLA Ops:
  1.2 11.2 %copy-start.5 = (bf16[320,3200]{1,0:T(8,128)(2,1)S(1)}, bf16[320,3200]{1,0:T(8,128)(2,1)}, u32[]{:S(2)}) copy-start(bf16[320,3200]{1,0:T(8,128)(2,1)} %param.13) | copy-start | bytes 6144004
  5.2 13.1 %all-to-all-start = ((bf16[16,8,384]{2,1,0:T(8,128)(2,1)}), bf16[16,8,384]{2,1,0:T(8,128)(2,1)S(1)}, u32[]{:S(2)}, u32[]{:S(2)}) async-start(bf16[16,8,384]{2,1,0:T(8,128)(2,1)} %shard_map.111), calls=%async_computation | async-start | bytes 196608 | tf_op jit(solution)/shard_map/all_to_all | solution.py:391
  12.4 2.0 %copy-start.6 = (bf16[320,3200]{1,0:T(8,128)(2,1)S(1)}, bf16[320,3200]{1,0:T(8,128)(2,1)}, u32[]{:S(2)}) copy-start(bf16[320,3200]{1,0:T(8,128)(2,1)} %param.14) | copy-start | bytes 6144004
  13.6 24.7 %collective-permute-start.5 = (bf16[320,1664]{1,0:T(8,128)(2,1)}, bf16[320,1664]{1,0:T(8,128)(2,1)S(1)}, u32[]{:S(2)}, u32[]{:S(2)}) collective-permute-start(bf16[320,1664]{1,0:T(8,128)(2,1)} %get-tuple-element.74), channel_id=1, source_target_pairs={{0,1},{1,0},{2,3},{3,2},{4,5},{5,4},{6,7},{7,6},{8,9},{9,8},{10,11... | collective-permute-start | bytes 3194888 | tf_op jit(solution)/shard_map/ppermute | solution.py:65
  14.4 2.0 %copy-start.7 = (bf16[3200,320]{0,1:T(8,128)(2,1)S(1)}, bf16[3200,320]{0,1:T(8,128)(2,1)}, u32[]{:S(2)}) copy-start(bf16[3200,320]{0,1:T(8,128)(2,1)} %param.15) | copy-start | bytes 6144004
  15.6 22.8 %collective-permute-start.6 = (bf16[320,1664]{1,0:T(8,128)(2,1)}, bf16[320,1664]{1,0:T(8,128)(2,1)}, u32[]{:S(2)}, u32[]{:S(2)}) collective-permute-start(bf16[320,1664]{1,0:T(8,128)(2,1)} %get-tuple-element.72), channel_id=1, source_target_pairs={{0,1},{1,0},{2,3},{3,2},{4,5},{5,4},{6,7},{7,6},{8,9},{9,8},{10,11... | collective-permute-start | bytes 3194888 | tf_op jit(solution)/shard_map/ppermute | solution.py:65
  17.9 20.5 %copy-start.4 = (s32[6]{0:T(128)S(1)}, s32[6]{0:T(128)}, u32[]{:S(2)}) copy-start(s32[6]{0:T(128)} %stack.36.index) | copy-start | bytes 76
  17.9 20.4 %collective-permute-start.7 = (bf16[320,1664]{1,0:T(8,128)(2,1)}, bf16[320,1664]{1,0:T(8,128)(2,1)}, u32[]{:S(2)}, u32[]{:S(2)}) collective-permute-start(bf16[320,1664]{1,0:T(8,128)(2,1)} %get-tuple-element.70), channel_id=1, source_target_pairs={{0,1},{1,0},{2,3},{3,2},{4,5},{5,4},{6,7},{7,6},{8,9},{9,8},{10,11... | collective-permute-start | bytes 3194888 | tf_op jit(solution)/shard_map/ppermute | solution.py:65
  18.3 20.0 %copy-start = (bf16[320,1664]{1,0:T(8,128)(2,1)S(1)}, bf16[320,1664]{1,0:T(8,128)(2,1)}, u32[]{:S(2)}) copy-start(bf16[320,1664]{1,0:T(8,128)(2,1)} %get-tuple-element.71.w4) | copy-start | bytes 3194884
  18.6 4.9 %collective-permute-start = (bf16[64,384]{1,0:T(8,128)(2,1)S(1)}, bf16[64,384]{1,0:T(8,128)(2,1)S(1)}, u32[]{:S(2)}, u32[]{:S(2)}) collective-permute-start(bf16[64,384]{1,0:T(8,128)(2,1)S(1)} %shard_map.112), channel_id=1, source_target_pairs={{0,16},{16,0},{1,17},{17,1},{2,18},{18,2},{3,19},{19,3},{4,20},{20... | collective-permute-start | bytes 147464 | tf_op jit(solution)/shard_map/ppermute | solution.py:393
  23.5 4.8 %collective-permute-start.1 = (bf16[2,64,384]{2,1,0:T(8,128)(2,1)S(1)}, bf16[2,64,384]{2,1,0:T(8,128)(2,1)S(1)}, u32[]{:S(2)}, u32[]{:S(2)}) collective-permute-start(bf16[2,64,384]{2,1,0:T(8,128)(2,1)S(1)} %pad_maximum_fusion), channel_id=1, source_target_pairs={{0,32},{32,64},{64,96},{96,0},{1,33},{33,65},{65,97},{97,1},{2,34}... | collective-permute-start | bytes 294920 | tf_op jit(solution)/shard_map/ppermute | solution.py:57
  24.8 5.1 %collective-permute-start.2 = (bf16[2,64,384]{2,1,0:T(8,128)(2,1)S(1)}, bf16[2,64,384]{2,1,0:T(8,128)(2,1)S(1)}, u32[]{:S(2)}, u32[]{:S(2)}) collective-permute-start(bf16[2,64,384]{2,1,0:T(8,128)(2,1)S(1)} %pad_maximum_fusion), channel_id=1, source_target_pairs={{0,96},{32,0},{64,32},{96,64},{1,97},{33,1},{65,33},{97,65},{2,98}... | collective-permute-start | bytes 294920 | tf_op jit(solution)/shard_map/ppermute | solution.py:57
  28.3 5.0 %collective-permute-start.3 = (bf16[2,64,384]{2,1,0:T(8,128)(2,1)S(1)}, bf16[2,64,384]{2,1,0:T(8,128)(2,1)S(1)}, u32[]{:S(2)}, u32[]{:S(2)}) collective-permute-start(bf16[2,64,384]{2,1,0:T(8,128)(2,1)S(1)} %pad_maximum_fusion), channel_id=1, source_target_pairs={{0,64},{32,96},{64,0},{96,32},{1,65},{33,97},{65,1},{97,33},{2,66}... | collective-permute-start | bytes 294920 | tf_op jit(solution)/shard_map/ppermute | solution.py:57
  33.3 75.6 %copy-start.1 = (bf16[8,64,384]{2,1,0:T(8,128)(2,1)}, bf16[8,64,384]{2,1,0:T(8,128)(2,1)S(1)}, u32[]{:S(2)}) copy-start(bf16[8,64,384]{2,1,0:T(8,128)(2,1)S(1)} %constant_dynamic-update-slice_fusion.own.own_in) | copy-start | bytes 1179652
  33.3 5.0 %collective-permute-start.4 = (bf16[8,64,384]{2,1,0:T(8,128)(2,1)S(1)}, bf16[8,64,384]{2,1,0:T(8,128)(2,1)S(1)}, u32[]{:S(2)}, u32[]{:S(2)}) collective-permute-start(bf16[8,64,384]{2,1,0:T(8,128)(2,1)S(1)} %constant_dynamic-update-slice_fusion.own.own_in), channel_id=1, source_target_pairs={{0,1},{1,0},{2,3},{3,2},{4,5},{5,4},{6,7},{7,6},{8,9},{9,8},{10,11... | collective-permute-start | bytes 1179656 | tf_op jit(solution)/shard_map/ppermute | solution.py:65
  41.3 16.7 %collective-permute-start.12 = (bf16[128,2688]{1,0:T(8,128)(2,1)S(1)}, bf16[128,2688]{1,0:T(8,128)(2,1)S(1)}, u32[]{:S(2)}, u32[]{:S(2)}) collective-permute-start(bf16[128,2688]{1,0:T(8,128)(2,1)S(1)} %get-tuple-element.52), channel_id=1, source_target_pairs={{0,2},{2,0},{1,3},{3,1},{4,6},{6,4},{5,7},{7,5},{8,10},{10,8},{9,1... | collective-permute-start | bytes 2064392 | tf_op jit(solution)/shard_map/ppermute | solution.py:61
  45.0 16.8 %collective-permute-start.10 = (bf16[64,2304]{1,0:T(8,128)(2,1)S(1)}, bf16[64,2304]{1,0:T(8,128)(2,1)S(1)}, u32[]{:S(2)}, u32[]{:S(2)}) collective-permute-start(bf16[64,2304]{1,0:T(8,128)(2,1)S(1)} %get-tuple-element.48), channel_id=1, source_target_pairs={{0,12},{4,0},{8,4},{12,8},{1,13},{5,1},{9,5},{13,9},{2,14},{6,2},{... | collective-permute-start | bytes 884744 | tf_op jit(solution)/shard_map/ppermute | solution.py:45
  47.5 15.5 %collective-permute-start.8 = (bf16[64,2304]{1,0:T(8,128)(2,1)S(1)}, bf16[64,2304]{1,0:T(8,128)(2,1)S(1)}, u32[]{:S(2)}, u32[]{:S(2)}) collective-permute-start(bf16[64,2304]{1,0:T(8,128)(2,1)S(1)} %get-tuple-element.46), channel_id=1, source_target_pairs={{0,4},{4,8},{8,12},{12,0},{1,5},{5,9},{9,13},{13,1},{2,6},{6,10},{... | collective-permute-start | bytes 884744 | tf_op jit(solution)/shard_map/ppermute | solution.py:45
  47.5 15.5 %collective-permute-start.9 = (bf16[64,2304]{1,0:T(8,128)(2,1)S(1)}, bf16[64,2304]{1,0:T(8,128)(2,1)S(1)}, u32[]{:S(2)}, u32[]{:S(2)}) collective-permute-start(bf16[64,2304]{1,0:T(8,128)(2,1)S(1)} %get-tuple-element.47), channel_id=1, source_target_pairs={{0,8},{4,12},{8,0},{12,4},{1,9},{5,13},{9,1},{13,5},{2,10},{6,14},... | collective-permute-start | bytes 884744 | tf_op jit(solution)/shard_map/ppermute | solution.py:45
  58.2 12.5 %collective-permute-start.13 = (bf16[32,2688]{1,0:T(8,128)(2,1)S(1)}, bf16[32,2688]{1,0:T(8,128)(2,1)S(1)}, u32[]{:S(2)}, u32[]{:S(2)}) collective-permute-start(bf16[32,2688]{1,0:T(8,128)(2,1)S(1)} %get-tuple-element.54), channel_id=1, source_target_pairs={{0,4},{4,8},{8,12},{12,0},{1,5},{5,9},{9,13},{13,1},{2,6},{6,10},{... | collective-permute-start | bytes 516104 | tf_op jit(solution)/shard_map/ppermute | solution.py:45
  59.4 11.3 %collective-permute-start.14 = (bf16[32,2688]{1,0:T(8,128)(2,1)S(1)}, bf16[32,2688]{1,0:T(8,128)(2,1)S(1)}, u32[]{:S(2)}, u32[]{:S(2)}) collective-permute-start(bf16[32,2688]{1,0:T(8,128)(2,1)S(1)} %get-tuple-element.55), channel_id=1, source_target_pairs={{0,8},{4,12},{8,0},{12,4},{1,9},{5,13},{9,1},{13,5},{2,10},{6,14},... | collective-permute-start | bytes 516104 | tf_op jit(solution)/shard_map/ppermute | solution.py:45
  61.8 8.9 %collective-permute-start.15 = (bf16[32,2688]{1,0:T(8,128)(2,1)S(1)}, bf16[32,2688]{1,0:T(8,128)(2,1)S(1)}, u32[]{:S(2)}, u32[]{:S(2)}) collective-permute-start(bf16[32,2688]{1,0:T(8,128)(2,1)S(1)} %get-tuple-element.56), channel_id=1, source_target_pairs={{0,12},{4,0},{8,4},{12,8},{1,13},{5,1},{9,5},{13,9},{2,14},{6,2},{... | collective-permute-start | bytes 516104 | tf_op jit(solution)/shard_map/ppermute | solution.py:45
  63.1 4.4 %collective-permute-start.11 = (bf16[32,2304]{1,0:T(8,128)(2,1)S(1)}, bf16[32,2304]{1,0:T(8,128)(2,1)S(1)}, u32[]{:S(2)}, u32[]{:S(2)}) collective-permute-start(bf16[32,2304]{1,0:T(8,128)(2,1)S(1)} %get-tuple-element.50), channel_id=1, source_target_pairs={{0,2},{2,0},{1,3},{3,1},{4,6},{6,4},{5,7},{7,5},{8,10},{10,8},{9,1... | collective-permute-start | bytes 442376 | tf_op jit(solution)/shard_map/ppermute | solution.py:61
  71.4 8.0 %collective-permute-start.17 = (bf16[32,4992]{1,0:T(8,128)(2,1)S(1)}, bf16[32,4992]{1,0:T(8,128)(2,1)S(1)}, u32[]{:S(2)}, u32[]{:S(2)}) collective-permute-start(bf16[32,4992]{1,0:T(8,128)(2,1)S(1)} %shard_map.117.refs_0_), channel_id=1, source_target_pairs={{0,12},{4,0},{8,4},{12,8},{1,13},{5,1},{9,5},{13,9},{2,14},{6,2},{... | collective-permute-start | bytes 958472 | tf_op jit(solution)/shard_map/ppermute | solution.py:45
  72.1 9.5 %collective-permute-start.16 = (bf16[32,4992]{1,0:T(8,128)(2,1)S(1)}, bf16[32,4992]{1,0:T(8,128)(2,1)S(1)}, u32[]{:S(2)}, u32[]{:S(2)}) collective-permute-start(bf16[32,4992]{1,0:T(8,128)(2,1)S(1)} %shard_map.117.refs_0_), channel_id=1, source_target_pairs={{0,2},{2,0},{1,3},{3,1},{4,6},{6,4},{5,7},{7,5},{8,10},{10,8},{9,1... | collective-permute-start | bytes 958472 | tf_op jit(solution)/shard_map/ppermute | solution.py:61
  79.4 7.0 %collective-permute-start.20 = (bf16[32,4992]{1,0:T(8,128)(2,1)S(1)}, bf16[32,4992]{1,0:T(8,128)(2,1)S(1)}, u32[]{:S(2)}, u32[]{:S(2)}) collective-permute-start(bf16[32,4992]{1,0:T(8,128)(2,1)S(1)} %collective-permute-done.17.refs_2_), channel_id=1, source_target_pairs={{0,12},{4,0},{8,4},{12,8},{1,13},{5,1},{9,5},{13,9},{2,14},{6,2},{... | collective-permute-start | bytes 958472 | tf_op jit(solution)/shard_map/ppermute | solution.py:45
  80.7 6.2 %collective-permute-start.21 = (bf16[32,4992]{1,0:T(8,128)(2,1)S(1)}, bf16[32,4992]{1,0:T(8,128)(2,1)S(1)}, u32[]{:S(2)}, u32[]{:S(2)}) collective-permute-start(bf16[32,4992]{1,0:T(8,128)(2,1)S(1)} %collective-permute-done.17.refs_2_), channel_id=1, source_target_pairs={{0,2},{2,0},{1,3},{3,1},{4,6},{6,4},{5,7},{7,5},{8,10},{10,8},{9,1... | collective-permute-start | bytes 958472 | tf_op jit(solution)/shard_map/ppermute | solution.py:61
  81.6 7.0 %collective-permute-start.22 = (bf16[32,4992]{1,0:T(8,128)(2,1)S(1)}, bf16[32,4992]{1,0:T(8,128)(2,1)S(1)}, u32[]{:S(2)}, u32[]{:S(2)}) collective-permute-start(bf16[32,4992]{1,0:T(8,128)(2,1)S(1)} %collective-permute-done.16.refs_1_), channel_id=1, source_target_pairs={{0,4},{4,8},{8,12},{12,0},{1,5},{5,9},{9,13},{13,1},{2,6},{6,10},{... | collective-permute-start | bytes 958472 | tf_op jit(solution)/shard_map/ppermute | solution.py:45
  81.6 14.0 %collective-permute-start.18 = (bf16[32,4992]{1,0:T(8,128)(2,1)S(1)}, bf16[32,4992]{1,0:T(8,128)(2,1)S(1)}, u32[]{:S(2)}, u32[]{:S(2)}) collective-permute-start(bf16[32,4992]{1,0:T(8,128)(2,1)S(1)} %shard_map.117.refs_0_), channel_id=1, source_target_pairs={{0,4},{4,8},{8,12},{12,0},{1,5},{5,9},{9,13},{13,1},{2,6},{6,10},{... | collective-permute-start | bytes 958472 | tf_op jit(solution)/shard_map/ppermute | solution.py:45
  88.7 14.3 %collective-permute-start.23 = (bf16[32,1664]{1,0:T(8,128)(2,1)S(1)}, bf16[32,1664]{1,0:T(8,128)(2,1)S(1)}, u32[]{:S(2)}, u32[]{:S(2)}) collective-permute-start(bf16[32,1664]{1,0:T(8,128)(2,1)S(1)} %get-tuple-element.59), channel_id=1, source_target_pairs={{0,2},{2,0},{1,3},{3,1},{4,6},{6,4},{5,7},{7,5},{8,10},{10,8},{9,1... | collective-permute-start | bytes 319496 | tf_op jit(solution)/shard_map/ppermute | solution.py:61
  89.4 13.7 %collective-permute-start.24 = (bf16[32,1664]{1,0:T(8,128)(2,1)S(1)}, bf16[32,1664]{1,0:T(8,128)(2,1)S(1)}, u32[]{:S(2)}, u32[]{:S(2)}) collective-permute-start(bf16[32,1664]{1,0:T(8,128)(2,1)S(1)} %get-tuple-element.60), channel_id=1, source_target_pairs={{0,4},{4,8},{8,12},{12,0},{1,5},{5,9},{9,13},{13,1},{2,6},{6,10},{... | collective-permute-start | bytes 319496 | tf_op jit(solution)/shard_map/ppermute | solution.py:45
  89.4 13.7 %collective-permute-start.25 = (bf16[32,1664]{1,0:T(8,128)(2,1)S(1)}, bf16[32,1664]{1,0:T(8,128)(2,1)S(1)}, u32[]{:S(2)}, u32[]{:S(2)}) collective-permute-start(bf16[32,1664]{1,0:T(8,128)(2,1)S(1)} %get-tuple-element.61), channel_id=1, source_target_pairs={{0,12},{4,0},{8,4},{12,8},{1,13},{5,1},{9,5},{13,9},{2,14},{6,2},{... | collective-permute-start | bytes 319496 | tf_op jit(solution)/shard_map/ppermute | solution.py:45
  97.8 8.4 %copy-start.2 = (bf16[128,4992]{1,0:T(8,128)(2,1)}, bf16[128,4992]{1,0:T(8,128)(2,1)S(1)}, u32[]{:S(2)}) copy-start(bf16[128,4992]{1,0:T(8,128)(2,1)S(1)} %get-tuple-element.57.value.early_in) | copy-start | bytes 3833860
  97.8 13.1 %collective-permute-start.27 = (bf16[128,4992]{1,0:T(8,128)(2,1)S(1)}, bf16[128,4992]{1,0:T(8,128)(2,1)S(1)}, u32[]{:S(2)}, u32[]{:S(2)}) collective-permute-start(bf16[128,4992]{1,0:T(8,128)(2,1)S(1)} %get-tuple-element.57.value.early_in), channel_id=1, source_target_pairs={{0,1},{1,0},{2,3},{3,2},{4,5},{5,4},{6,7},{7,6},{8,9},{9,8},{10,11... | collective-permute-start | bytes 3833864 | tf_op jit(solution)/shard_map/ppermute | solution.py:65
  105.2 1.8 %copy-start.3 = (bf16[128,4992]{1,0:T(8,128)(2,1)}, bf16[128,4992]{1,0:T(8,128)(2,1)S(1)}, u32[]{:S(2)}) copy-start(bf16[128,4992]{1,0:T(8,128)(2,1)S(1)} %get-tuple-element.62.value.late_in) | copy-start | bytes 3833860
  105.2 5.7 %collective-permute-start.28 = (bf16[128,4992]{1,0:T(8,128)(2,1)S(1)}, bf16[128,4992]{1,0:T(8,128)(2,1)S(1)}, u32[]{:S(2)}, u32[]{:S(2)}) collective-permute-start(bf16[128,4992]{1,0:T(8,128)(2,1)S(1)} %get-tuple-element.62.value.late_in), channel_id=1, source_target_pairs={{0,1},{1,0},{2,3},{3,2},{4,5},{5,4},{6,7},{7,6},{8,9},{9,8},{10,11... | collective-permute-start | bytes 3833864 | tf_op jit(solution)/shard_map/ppermute | solution.py:65
  105.6 2.9 %collective-permute-start.19 = (f32[128,320]{1,0:T(8,128)S(1)}, f32[128,320]{1,0:T(8,128)S(1)}, u32[]{:S(2)}, u32[]{:S(2)}) collective-permute-start(f32[128,320]{1,0:T(8,128)S(1)} %get-tuple-element.58), channel_id=1, source_target_pairs={{0,1},{1,0},{2,3},{3,2},{4,5},{5,4},{6,7},{7,6},{8,9},{9,8},{10,11... | collective-permute-start | bytes 491528 | tf_op jit(solution)/shard_map/ppermute | solution.py:65
  105.8 3.0 %collective-permute-start.26 = (f32[128,320]{1,0:T(8,128)S(1)}, f32[128,320]{1,0:T(8,128)S(1)}, u32[]{:S(2)}, u32[]{:S(2)}) collective-permute-start(f32[128,320]{1,0:T(8,128)S(1)} %get-tuple-element.63), channel_id=1, source_target_pairs={{0,1},{1,0},{2,3},{3,2},{4,5},{5,4},{6,7},{7,6},{8,9},{9,8},{10,11... | collective-permute-start | bytes 491528 | tf_op jit(solution)/shard_map/ppermute | solution.py:65
  107.9 12.8 %copy-start.9 = (s32[1,16]{1,0:T(1,128)S(1)}, s32[1,16]{1,0:T(1,128)}, u32[]{:S(2)}) copy-start(s32[1,16]{1,0:T(1,128)} %counts_in.1) | copy-start | bytes 196
  110.9 1.1 copy-start.10
  111.9 10.1 %copy-start.11 = (bf16[128,4992]{1,0:T(8,128)(2,1)}, bf16[128,4992]{1,0:T(8,128)(2,1)S(1)}, u32[]{:S(2)}) copy-start(bf16[128,4992]{1,0:T(8,128)(2,1)S(1)} %collective-permute-done.28.late_other_in) | copy-start | bytes 3833860
  111.9 22.8 %all-to-all-start.1 = ((bf16[128,8,160]{2,1,0:T(8,128)(2,1)}), bf16[128,8,160]{2,1,0:T(8,128)(2,1)S(1)}, u32[]{:S(2)}, u32[]{:S(2)}) async-start(bf16[128,8,160]{2,1,0:T(8,128)(2,1)} %bitcast.12), calls=%async_computation.1 | async-start | bytes 1048576 | tf_op jit(solution)/shard_map/all_to_all | solution.py:446
  122.0 13.1 %copy-start.8 = (s32[1,1,4]{2,1,0:T(1,128)S(1)}, s32[1,1,4]{2,1,0:T(1,128)}, u32[]{:S(2)}) copy-start(s32[1,1,4]{2,1,0:T(1,128)} %chosen_in.1) | copy-start | bytes 52

commit v3 on v2

--- a/solution.py
+++ b/solution.py
@@ -53,10 +53,6 @@
     return along(t, 3)
 
 
-def ring_y(t, step):
-    return lax.ppermute(t, "y", [(i, (i + step) % 4) for i in range(4)])
-
-
 def across(t):
     return lax.ppermute(t, "zl", SWAP)
 
@@ -65,7 +61,7 @@
     return lax.ppermute(t, "c", SWAP)
 
 
-def call(kernel, shapes, operands, scratch=(), mib=24, estimate=None, smem=0, out_specs=None):
+def call(kernel, shapes, operands, scratch=(), mib=16, estimate=None, smem=0, out_specs=None):
     return pl.pallas_call(
         kernel,
         out_shape=[jax.ShapeDtypeStruct(s, k) for s, k in shapes],
@@ -77,7 +73,7 @@
     )(*operands)
 
 
-def message_kernel(index, chosen_in, counts_in, advantage_in, tokens, cotangent, out,
+def message_kernel(chosen_in, counts_in, advantage_in, tokens, cotangent, out, owner,
                    chosen, counts, advantage, x_rows, y_rows, small, big):
     first = [
         pltpu.make_async_copy(chosen_in, chosen, small.at[0]),
@@ -96,7 +92,7 @@
         copies.append(pltpu.make_async_copy(cotangent.at[block], y_rows.at[here], big.at[CAP + s]))
     for copy in copies:
         copy.start()
-    f = index[0]
+    f = lax.axis_index(("x", "zl", "c"))
     count = counts[0, f]
     before = jnp.int32(0)
     for j in range(N_FSDP):
@@ -122,6 +118,12 @@
         place = jnp.where((wide == s + CAP) & (lane_of == 0), spot + GROUP, place)
         slot = (f * CAP + s + 1).astype(F32)
         place = jnp.where((wide == s) & (lane_of == 1), slot, place)
+    mark = jnp.zeros((2 * CAP, ROWS), F32)
+    row = lax.broadcasted_iota(jnp.int32, (2 * CAP, ROWS), 0)
+    lane = lax.broadcasted_iota(jnp.int32, (2 * CAP, ROWS), 1)
+    for s in range(CAP):
+        mark = jnp.where((row == s) & (lane == chosen[0, 0, s]) & (s < count), 1.0, mark)
+    owner[...] = mark.astype(BF)
     for copy in copies:
         copy.wait()
     x = dot(take_x.astype(BF), x_rows[...], 1, 0)
@@ -136,9 +138,12 @@
 def messages(*operands):
     return pl.pallas_call(
         message_kernel,
-        out_shape=jax.ShapeDtypeStruct((N_FSDP, 2 * CAP, MSG), BF),
-        in_specs=[SMEM] + [ANY] * 5,
-        out_specs=VMEM,
+        out_shape=[
+            jax.ShapeDtypeStruct((N_FSDP, 2 * CAP, MSG), BF),
+            jax.ShapeDtypeStruct((2 * CAP, ROWS), BF),
+        ],
+        in_specs=[ANY] * 5,
+        out_specs=[VMEM] * 2,
         scratch_shapes=[
             pltpu.SMEM((1, 1, CAP), jnp.int32),
             pltpu.SMEM((1, N_FSDP), jnp.int32),
@@ -155,10 +160,9 @@
 def pack_kernel(lines, out):
     spot = lax.broadcasted_iota(jnp.int32, (N_FSDP * 2 * CAP, 2 * GROUP), 1)
     place = lines[:, DL : DL + 1].astype(jnp.int32)
-    out[...] = dot(jnp.where(place == spot, 1.0, 0.0).astype(BF), lines[...], 0, 0).astype(BF)
-
-
-FROM_Y = (0, 3, 1, 2)
+    rows = dot(jnp.where(place == spot, 1.0, 0.0).astype(BF), lines[...], 0, 0).astype(BF)
+    for i in range(N_DP):
+        out[i] = rows
 
 
 def gather_rows(index, rows, order, x, y=None):
@@ -258,79 +262,86 @@
         out[:, k * WIN + NA : (k + 1) * WIN] = of_b[k].astype(BF)
 
 
-def split_kernel(a, b, c, *outs):
-    for k, (ref, out) in enumerate(zip((a, b, c), outs)):
-        out[...] = ref[:, k * WIN : (k + 1) * WIN]
-
-
-def back_product(value, gate, up_w):
-    return dot(value[:, WIN : 2 * WIN], gate[...], 1, 1) + dot(value[:, 2 * WIN :], up_w[...], 1, 1)
-
-
-def lay_kernel(*refs):
-    blocks, (gate, up_w, value, out) = refs[:-4], refs[-4:]
-    for k in range(3 + (len(blocks) == 4)):
-        value[k * GROUP : (k + 1) * GROUP, :] = blocks[k][...]
-    if len(blocks) > 4:
-        for k in range(3):
-            value[3 * GROUP :, k * WIN : (k + 1) * WIN] = blocks[3 + k][...]
-    out[...] = back_product(value, gate, up_w)
-
-
-def back_kernel(value, gate, up_w, out):
-    out[...] = back_product(value, gate, up_w)
-
-
-def back_products(blocks, gate_own, gate_sib, up_own, up_sib):
+def back_kernel(*refs):
+    blocks, (go, gs, uo, us, value, mine, other) = refs[:4], refs[4:]
+    for k, block in enumerate(blocks):
+        value[k * GROUP : (k + 1) * GROUP, :] = block[...]
+    gate, up_w = value[:, WIN : 2 * WIN], value[:, 2 * WIN :]
+    other[...] = dot(gate, gs[...], 1, 1) + dot(up_w, us[...], 1, 1)
+    mine[...] = dot(gate, go[...], 1, 1) + dot(up_w, uo[...], 1, 1)
+
+
+def back_products(blocks, weights):
     rows = 4 * GROUP
-    price = cost(2 * rows * DL * 2 * WIN, 4 * 2**20)
-    value, other = call(
-        lay_kernel,
-        [((rows, 3 * WIN), BF), ((rows, DL), F32)],
-        [*blocks, gate_sib, up_sib],
-        estimate=price,
-    )
-    mine = call(back_kernel, [((rows, DL), F32)], [value, gate_own, up_own], estimate=price)[0]
-    return value, mine, sibling(other)
-
-
-def unpack_kernel(index, own, mine_e, other_e, mine_l, other_l, out):
-    half = DL // 2
+    return call(
+        back_kernel,
+        [((rows, 3 * WIN), BF), ((rows, DL), F32), ((rows, DL), F32)],
+        [*blocks, *weights],
+        estimate=cost(2 * rows * DL * 4 * WIN, 6 * 2**20),
+    )
+
+
+def line_kernel(index, own, out):
     parts = []
-    for k, (dx, dz) in enumerate(ORDER):
+    lane = DL + 1 - (MSG - 128)
+    for dx, dz in ORDER:
         i = (index[1] + dx) % 4 * 2 + (index[2] + dz) % 2
-        step = sum(jnp.where(i // 2 == j, FROM_Y[j], 0) for j in range(4))
-        to = (index[4] + step) % 4 * 2 + (index[5] + i % 2) % 2
-        slot = own[i, 0:GROUP, MSG - 128 : MSG].astype(F32)[:, DL + 1 - (MSG - 128) : DL + 2 - (MSG - 128)]
-        slot = slot.astype(jnp.int32) - 1
-        line = to * (N_FSDP * 2 * CAP) + slot // CAP * (2 * CAP) + slot % CAP
-        parts.append(jnp.where(slot < 0, -2 * CAP, line).astype(F32))
-    line = jnp.broadcast_to(jnp.concatenate(parts, axis=0), (LIVE, 128))
-    line = jnp.transpose(line)[0:1, :].astype(jnp.int32)
-    back = jnp.concatenate([mine_e[...] + other_e[...], mine_l[...] + other_l[...]]).astype(BF)
-    at = lax.broadcasted_iota(jnp.int32, (2 * CAP * N_DEV, LIVE), 0)
-    low = jnp.where(at == line, 1.0, 0.0).astype(BF)
-    high = jnp.where(at == line + CAP, 1.0, 0.0).astype(BF)
-    out[...] = (dot(low, back[:, :half], 1, 0) + dot(high, back[:, half:], 1, 0)).astype(BF)
-
-
-def grad_kernel(index, own_in, early_in, late_in, early_other_in, late_other_in, gate_out, up_out,
-                down_out, own, mine, other, x, y, gate, up_s, down_s, reads, sems):
+        slot = own[i, 0:GROUP, MSG - 128 : MSG].astype(F32)[:, lane : lane + 1].astype(jnp.int32) - 1
+        device = slot // CAP
+        line = i * (N_FSDP // 2 * 2 * CAP) + device // 2 * (2 * CAP) + slot % CAP
+        core = jnp.where(slot < 0, -1, device % 2)
+        parts.append(jnp.concatenate([jnp.where(core == k, line, -2 * CAP) for k in range(2)], axis=1))
+    lines = jnp.concatenate(parts, axis=0).astype(F32)
+    lines = jnp.concatenate([lines, jnp.zeros((LIVE, 126), F32)], axis=1)
+    out[...] = jnp.transpose(lines)[0:8, :].astype(jnp.int32)
+
+
+def unpack(index, core, lines, mine_e, other_e, mine_l, other_l):
+    c = index[3]
+    line = jnp.where(core == 0, lines[0:1, :], lines[1:2, :])
+    mine = jnp.concatenate([mine_e[...], mine_l[...]])
+    other = jnp.concatenate([other_e[...], other_l[...]])
+    at = lax.broadcasted_iota(jnp.int32, (CAP * N_DEV, LIVE), 0)
+    low = jnp.where(at == jnp.where(c == 0, line, line + CAP), 1.0, 0.0).astype(BF)
+    high = jnp.where(at == jnp.where(c == 0, line + CAP, line), 1.0, 0.0).astype(BF)
+    return dot(low, mine.astype(BF), 1, 0) + dot(high, other.astype(BF), 1, 0)
+
+
+def unpack_send_kernel(index, lines, mine_e, other_e, mine_l, other_l, out):
+    out[...] = unpack(index, 1 - index[3], lines, mine_e, other_e, mine_l, other_l).astype(BF)
+
+
+def unpack_keep_kernel(index, lines, mine_e, other_e, mine_l, other_l, sent, out):
+    kept = unpack(index, index[3], lines, mine_e, other_e, mine_l, other_l)
+    out[...] = (kept + sent[...].astype(F32)).astype(BF)
+
+
+def owner_kernel(owner, back, out):
+    n = N_FSDP // 2
+    for k in range(n):
+        total = back[k].astype(F32)
+        for i in range(1, N_DP):
+            total = total + back[i * n + k].astype(F32)
+        total = total.astype(BF)
+        for core in range(2):
+            cols = slice((2 * k + core) * DL, (2 * k + core + 1) * DL)
+            rows = slice(core * CAP, (core + 1) * CAP)
+            out[:, cols] = dot(owner[0:CAP, :], total[rows, :], 0, 0).astype(BF)
+
+
+def grad_kernel(index, own, early_in, late_in, early_other_in, late_other_in, gate_out, up_out,
+                down_out, mine, other, x, y, gate, up_s, down_s, reads, sems):
     top, bottom = pl.ds(0, 4 * GROUP), pl.ds(4 * GROUP, 4 * GROUP)
     loads = [
-        pltpu.make_async_copy(own_in, own, reads.at[0]),
-        pltpu.make_async_copy(early_in, mine.at[top], reads.at[1]),
-        pltpu.make_async_copy(late_in, mine.at[bottom], reads.at[2]),
-        pltpu.make_async_copy(early_other_in, other.at[top], reads.at[3]),
-        pltpu.make_async_copy(late_other_in, other.at[bottom], reads.at[4]),
+        pltpu.make_async_copy(early_in, mine.at[top], reads.at[0]),
+        pltpu.make_async_copy(late_in, mine.at[bottom], reads.at[1]),
+        pltpu.make_async_copy(early_other_in, other.at[top], reads.at[2]),
+        pltpu.make_async_copy(late_other_in, other.at[bottom], reads.at[3]),
     ]
     for copy in loads:
         copy.start()
     c = index[3]
-    loads[0].wait()
     gather_rows(index, own, ORDER, x, y)
-    for copy in loads[1:]:
-        copy.wait()
     starts = [pl.multiple_of(c * HI, 128), pl.multiple_of((1 - c) * HI, 128)]
     spans = [(lo, min(lo + 512, WIN)) for lo in range(0, WIN, 512)]
     copies = []
@@ -341,7 +352,10 @@
         def product(ref, lo, hi):
             return dot(rows, ref[:, part * WIN + lo : part * WIN + hi], 0, 0).astype(BF)
 
-        for start, ref in zip(starts, (mine, other)):
+        for start, ref, first in zip(starts, (mine, other), (0, 2)):
+            if k == 0:
+                loads[first].wait()
+                loads[first + 1].wait()
             for lo, hi in spans:
                 scratch[:, pl.ds(start + lo, hi - lo)] = product(ref, lo, hi)
 
@@ -365,12 +379,11 @@
     return pl.pallas_call(
         grad_kernel,
         out_shape=[jax.ShapeDtypeStruct((DL, FL), BF)] * 3,
-        in_specs=[SMEM] + [ANY] * 5,
+        in_specs=[SMEM, VMEM] + [ANY] * 4,
         out_specs=[ANY] * 3,
         scratch_shapes=[
-            pltpu.VMEM((N_DP, 2 * GROUP, MSG), BF),
             values, values, rows, rows, grad, grad, grad,
-            pltpu.SemaphoreType.DMA((5,)),
+            pltpu.SemaphoreType.DMA((4,)),
             pltpu.SemaphoreType.DMA((3,)),
         ],
         compiler_params=limits(60),
@@ -379,29 +392,31 @@
 
 
 def shards(tokens, cotangent, advantage, chosen, chosen_count, gate_weight, up_weight, down_weight):
-    c = lax.axis_index("c")
-    first = c == 0
-    f_index = lax.axis_index(("x", "zl", "c"))
-    place = [f_index, *[lax.axis_index(a) for a in ("x", "zl", "c", "y", "zh")]]
+    place = [lax.axis_index(a) for a in ("c", "x", "zl", "c")]
     index = jnp.stack(place).astype(jnp.int32)
-    message = messages(index, chosen, chosen_count, advantage, tokens, cotangent)
-    message, gate_weight, up_weight, down_weight, chosen, chosen_count = lax.optimization_barrier(
-        (message, gate_weight, up_weight, down_weight, chosen, chosen_count)
-    )
-    got = lax.all_to_all(message, ("x", "zl", "c"), 0, 0, tiled=True)
-    packed = call(pack_kernel, [((2 * GROUP, MSG), BF)], [got.reshape(N_FSDP * 2 * CAP, MSG)])[0]
-    packed = jnp.stack([packed, lax.ppermute(packed, "zh", SWAP)])
-    own = jnp.concatenate([packed, ring_y(packed, 1), ring_y(packed, 3), ring_y(packed, 2)])
-    sib = sibling(own)
+    message, owner = messages(chosen, chosen_count, advantage, tokens, cotangent)
+    message, gate_weight, up_weight, down_weight = lax.optimization_barrier(
+        (message, gate_weight, up_weight, down_weight)
+    )
+    first = lax.axis_index("c") == 0
 
     def window(w):
         lo, hi = w[:, :WIN], w[:, HI:]
-        return jnp.where(first, lo, hi), sibling(jnp.where(first, hi, lo))
-
-    weights = [*window(gate_weight), *window(up_weight), *window(down_weight.T)]
-    rows = chosen[0, 0]
-    live = jnp.arange(CAP, dtype=jnp.int32) < chosen_count[0][f_index]
-    owner = ((jnp.arange(ROWS, dtype=jnp.int32)[:, None] == rows[None, :]) & live[None, :]).astype(BF)
+        return jnp.where(first, lo, hi), jnp.where(first, hi, lo)
+
+    mine, halves = [], []
+    for w in (gate_weight, up_weight, down_weight.T):
+        if halves:
+            w, halves[-1] = lax.optimization_barrier((w, halves[-1]))
+        a, b = window(w)
+        mine.append(a)
+        halves.append(b)
+    got = lax.all_to_all(message, ("x", "zl", "c"), 0, 0, tiled=True)
+    got, *halves = lax.optimization_barrier((got, *halves))
+    weights = [w for pair in zip(mine, map(sibling, halves)) for w in pair]
+    packed = call(pack_kernel, [((N_DP, 2 * GROUP, MSG), BF)], [got.reshape(N_FSDP * 2 * CAP, MSG)])[0]
+    own = lax.all_to_all(packed, ("y", "zh"), 0, 0, tiled=True)
+    sib = sibling(own)
 
     far, near = local_products(
         kernel_b, NB, [(4 * GROUP, BF), (4 * GROUP, F32)], index, own, sib, *weights
@@ -426,30 +441,29 @@
         smem=1,
     )[0]
 
-    v01, v30, v10 = across(v00), up(v00), down(v00)
-    v20, v11, v31 = down(v10), across(v10), up(v01)
-    part = ((GROUP, WIN), BF)
-    t20, t31, t11 = call(split_kernel, [part] * 3, [v20, v31, v11])
-    v21 = [across(t20), up(t31), down(t11)]
-    early, mine_e, other_e = back_products([v00, v01, v10, v30], *weights[:4])
-    late, mine_l, other_l = back_products([v20, v11, v31, *v21], *weights[:4])
-    early_other, late_other = sibling(early), sibling(late)
-
-    back = call(
-        unpack_kernel,
-        [((2 * CAP * N_DEV, DL // 2), BF)],
-        [index, own, mine_e, other_e, mine_l, other_l],
-        smem=1,
-        estimate=cost(8 * N_DEV * 2 * LIVE * DL, 2**20),
-    )[0]
-    back, early_other, late_other = lax.optimization_barrier((back, early_other, late_other))
-    back = lax.all_to_all(back.reshape(N_DEV, 2 * CAP, DL // 2), AXES, 0, 0, tiled=True)
+    v01, v30, v10 = lax.optimization_barrier((across(v00), up(v00), down(v00)))
+    early, mine_e, other_e = back_products([v00, v01, v10, v30], weights[:4])
+    lines = call(line_kernel, [((8, LIVE), jnp.int32)], [index, own], smem=1)[0]
+    v20, v11, v31, early, lines = lax.optimization_barrier(
+        (down(v10), across(v10), up(v01), early, lines)
+    )
+    v21, mine_e, other_e = lax.optimization_barrier((across(v20), mine_e, other_e))
+    late, mine_l, other_l = back_products([v20, v11, v31, v21], weights[:4])
+    early_other = sibling(early)
+
+    backs = [index, lines, mine_e, other_e, mine_l, other_l]
+    shape, price = (CAP * N_DEV, DL), cost(2 * CAP * N_DEV * LIVE * DL, 2**20)
+    sent = call(unpack_send_kernel, [(shape, BF)], backs, smem=1, estimate=price)[0]
+    sent, late = lax.optimization_barrier((sibling(sent), late))
+    late_other = sibling(late)
+    back = call(unpack_keep_kernel, [(shape, BF)], [*backs, sent], smem=1, estimate=price)[0]
+    back, early_other = lax.optimization_barrier((back, early_other))
+    back = lax.all_to_all(back.reshape(N_DEV // 2, 2 * CAP, DL), AXES[:4], 0, 0, tiled=True)
 
     gate_grad, up_grad, down_grad = weight_grads(index, own, early, late, early_other, late_other)
 
-    back = jnp.sum(back.reshape(N_DP, N_FSDP, 2, CAP, DL // 2).astype(F32), axis=0).astype(BF)
-    back = back.transpose(2, 0, 1, 3).reshape(CAP, D)
-    input_grad = dot(owner, back, 1, 0).astype(BF)
+    back, down_grad = lax.optimization_barrier((back, down_grad))
+    input_grad = call(owner_kernel, [((ROWS, D), BF)], [owner, back])[0]
     return (input_grad, gate_grad, up_grad, down_grad.T)
 
 

time: 137 us -> 130 us (0.949)
  blocking collectives: 0 us -> 16.6 us
  waiting for transfers between devices: 46.3 us -> 33.1 us
  starting transfers between devices: 52.5 us -> 39.8 us
  Pallas kernels: 26.8 us -> 30.6 us
  matrix products: 1.53 us -> 0 us
    all_to_all x0 -> x1, blocking collectives: none -> 16.6 us  [shards(): own = lax.all_to_all(packed, ('y', 'zh'), 0, 0, tiled=True)]
    ppermute x12 -> x10, waiting for transfers between devices: 19.3 us -> 10 us  [along(): return lax.ppermute(t, 'x', [(i, (i + step) % 4) for i in range(4)])]
    ppermute x4 -> x0, starting transfers between devices: 7.91 us -> none  [the longest x3 4.53 us: ring_y(): return lax.ppermute(t, 'y', [(i, (i + step) % 4) for i in range(4)])]
    ppermute x4 -> x0, waiting for transfers between devices: 6.66 us -> none  [the longest x3 5.19 us: ring_y(): return lax.ppermute(t, 'y', [(i, (i + step) % 4) for i in range(4)])]
    pallas_call x12, Pallas kernels: 15.1 us -> 19.8 us  [call(): pl.pallas_call(kernel, out_shape=[jax.ShapeDtypeStruct(s, k) for s, k in...]
    ppermute x5, waiting for transfers between devices: 12.8 us -> 17.1 us  [across(): return lax.ppermute(t, 'zl', SWAP)]
    ppermute x8 -> x7, starting transfers between devices: 10.2 us -> 7.74 us  [sibling(): return lax.ppermute(t, 'c', SWAP)]
    all_to_all x1, waiting for transfers between devices: 4.98 us -> 2.58 us  [shards(): lax.all_to_all(back.reshape(N_DEV // 2, 2 * CAP, DL), AXES[:4], 0, 0, til...]
  transfers between devices with their start and end apart: 31 -> 24, of which waited for: 16 -> 11; matrix products, arithmetic and copies ran while one was open for 4% -> 3% of each run, Pallas kernels for 14% -> 13%
where the time goes in v3:
time: 130 us; the launch traced here: 129 us
  starting transfers between devices  39.8 us (31%)
  waiting for transfers between devices  33.1 us (25%)
  Pallas kernels  30.6 us (24%)
  blocking collectives  16.6 us (13%)
  other arithmetic  3.97 us (3%)
  local copies, waits for them, and re-layouts  3.84 us (3%)
    pallas_call x12, Pallas kernels, call(): pl.pallas_call(kernel, out_shape=[jax.ShapeDtypeStruct(s, k) for s, k in...  19.8 us
    ppermute x5, waiting for transfers between devices, across(): return lax.ppermute(t, 'zl', SWAP)  17.1 us
    all_to_all x1, blocking collectives, shards(): own = lax.all_to_all(packed, ('y', 'zh'), 0, 0, tiled=True)  16.6 us
    ppermute x10, starting transfers between devices, along(): return lax.ppermute(t, 'x', [(i, (i + step) % 4) for i in range(4)])  15.4 us
    ppermute x10, waiting for transfers between devices, along(): return lax.ppermute(t, 'x', [(i, (i + step) % 4) for i in range(4)])  10 us
    ppermute x7, starting transfers between devices, sibling(): return lax.ppermute(t, 'c', SWAP)  7.74 us
    pallas_call x1, Pallas kernels, weight_grads(): pl.pallas_call(grad_kernel, out_shape=[jax.ShapeDtypeStruct((DL, FL), BF)...  7.54 us
    all_to_all x1, starting transfers between devices, shards(): lax.all_to_all(back.reshape(N_DEV // 2, 2 * CAP, DL), AXES[:4], 0, 0, til...  7.28 us
  transfers between devices with their start and end apart: 24, of which 11 were waited for; matrix products, arithmetic and copies ran while one was open for 3% of the time, Pallas kernels for 13%

profile of v3, /device:TPU:1, one launch (start us, length us, event | category | flops | bytes accessed | tf_op | source)
XLA Modules:
  0.0 128.8 jit_solution(4982378020114504006)
XLA Ops:
  0.6 3.3 %shard_map.111 = (bf16[16,8,384]{2,1,0:T(8,128)(2,1)}, bf16[8,128]{1,0:T(8,128)(2,1)}) custom-call(s32[1,1,4]{2,1,0:T(1,128)} %chosen_in.1, s32[1,16]{1,0:T(1,128)} %counts_in.1, f32[128]{0:T(128)} %advantage_in.1, bf16[128,5120]{1,0:T(8,128)(2,1)} %tokens.1, bf16[128,5120]{1,0:T(8,128)(2,1)} %cotangent.1), custom_call_target="tpu_custom_call" | custom-call | tf_op jit(solution)/shard_map/pallas_call | solution.py:139
  4.0 7.2 %all-to-all-start = ((bf16[16,8,384]{2,1,0:T(8,128)(2,1)}), bf16[16,8,384]{2,1,0:T(8,128)(2,1)S(1)}, u32[]{:S(2)}, u32[]{:S(2)}) async-start(bf16[16,8,384]{2,1,0:T(8,128)(2,1)} %get-tuple-element.60), calls=%async_computation | async-start | bytes 196608 | tf_op jit(solution)/shard_map/all_to_all | solution.py:414
  11.1 0.0 copy-start.5
  11.2 1.2 broadcast_select_fusion.2
  12.3 0.8 copy-done.5
  13.1 1.2 broadcast_select_fusion.1
  14.3 0.8 copy-done.6
  15.1 1.5 %broadcast_select_fusion = (bf16[320,1664]{1,0:T(8,128)(2,1)}, bf16[320,1664]{1,0:T(8,128)(2,1)}) fusion(pred[]{:T(512)S(6)} %eq.3, bf16[320,3200]{1,0:T(8,128)(2,1)S(1)} %bitcast.8), kind=kLoop, calls=%fused_computation | loop fusion | flops 1064960 | bytes 4259841 | tf_op jit(solution)/shard_map/jit(_where)/select_n | solution.py:405
  16.6 0.5 all-to-all-done
  17.1 0.5 collective-permute-start.1
  17.6 0.0 collective-permute-start.2
  17.6 0.5 collective-permute-start.3
  18.1 0.3 shard_map.112
  18.3 16.6 %all_to_all.15.own = bf16[8,64,384]{2,1,0:T(8,128)(2,1)} all-to-all(bf16[8,64,384]{2,1,0:T(8,128)(2,1)S(1)} %shard_map.112), channel_id=1, replica_groups=mesh['y'=4,'zh'=2,'x'=4,'zl'=2,'c'=2] {'y','zh'}, dimensions={0} | all-to-all | bytes 786432 | tf_op jit(solution)/shard_map/all_to_all | solution.py:418
  35.0 1.5 %collective-permute-start = (bf16[8,64,384]{2,1,0:T(8,128)(2,1)}, bf16[8,64,384]{2,1,0:T(8,128)(2,1)}, u32[]{:S(2)}, u32[]{:S(2)}) collective-permute-start(bf16[8,64,384]{2,1,0:T(8,128)(2,1)} %all_to_all.15.own), channel_id=1, source_target_pairs={{0,1},{1,0},{2,3},{3,2},{4,5},{5,4},{6,7},{7,6},{8,9},{9,8},{10,11... | collective-permute-start | bytes 1179656 | tf_op jit(solution)/shard_map/ppermute | solution.py:61
  36.4 0.1 pad_add_fusion.index
  36.5 1.6 %collective-permute-done.sib = bf16[8,64,384]{2,1,0:T(8,128)(2,1)} collective-permute-done((bf16[8,64,384]{2,1,0:T(8,128)(2,1)}, bf16[8,64,384]{2,1,0:T(8,128)(2,1)}, u32[]{:S(2)}, u32[]{:S(2)}) %collective-permute-start) | collective-permute-done | bytes 393248 | tf_op jit(solution)/shard_map/ppermute | solution.py:61
  38.1 0.0 collective-permute-done.3.w5
  38.1 0.0 copy-start
  38.1 1.2 copy-done
  39.4 3.2 %shard_map.113 = (bf16[128,2688]{1,0:T(8,128)(2,1)S(1)}, f32[128,2688]{1,0:T(8,128)S(1)}) custom-call(s32[4]{0:T(128)S(1)} %pad_add_fusion.index, bf16[8,64,384]{2,1,0:T(8,128)(2,1)} %all_to_all.15.own, bf16[8,64,384]{2,1,0:T(8,128)(2,1)} %collective-permute-done.sib, bf16[320,1664]{1,0:T(8,128)(2,1)S(1)} %get-tuple-element.116.w0.refs_4_, ...), custom_call_target="tpu_custom_call" | custom-call | flops 880803840 | bytes 10485760 | tf_op jit(solution)/shard_map/pallas_call | solution.py:65
  42.6 0.3 collective-permute-start.8
  42.9 2.9 %shard_map.114 = (f32[64,2304]{1,0:T(8,128)S(1)}, bf16[64,2304]{1,0:T(8,128)(2,1)S(1)}, bf16[64,2304]{1,0:T(8,128)(2,1)S(1)}, bf16[64,2304]{1,0:T(8,128)(2,1)S(1)}) custom-call(s32[4]{0:T(128)S(1)} %pad_add_fusion.index, bf16[8,64,384]{2,1,0:T(8,128)(2,1)} %all_to_all.15.own, bf16[8,64,384]{2,1,0:T(8,128)(2,1)} %collective-permute-done.sib, ...), custom_call_target="tpu_custom_call" | custom-call | flops 754974720 | bytes 10485760 | tf_op jit(solution)/shard_map/pallas_call | solution.py:65
  45.8 1.3 collective-permute-start.4
  47.1 2.4 %collective-permute-start.5 = (bf16[64,2304]{1,0:T(8,128)(2,1)S(1)}, bf16[64,2304]{1,0:T(8,128)(2,1)S(1)}, u32[]{:S(2)}, u32[]{:S(2)}) collective-permute-start(bf16[64,2304]{1,0:T(8,128)(2,1)S(1)} %get-tuple-element.76), channel_id=1, source_target_pairs={{0,8},{4,12},{8,0},{12,4},{1,9},{5,13},{9,1},{13,5},{2,10},{6,14},... | collective-permute-start | bytes 884744 | tf_op jit(solution)/shard_map/ppermute | solution.py:45
  49.5 1.2 collective-permute-start.6
  50.7 8.7 %collective-permute-done.8.far = bf16[128,2688]{1,0:T(8,128)(2,1)S(1)} collective-permute-done((bf16[128,2688]{1,0:T(8,128)(2,1)S(1)}, bf16[128,2688]{1,0:T(8,128)(2,1)S(1)}, u32[]{:S(2)}, u32[]{:S(2)}) %collective-permute-start.8) | collective-permute-done | bytes 688160 | tf_op jit(solution)/shard_map/ppermute | solution.py:57
  59.3 0.1 shard_map.116
  59.5 0.9 collective-permute-start.9
  60.3 2.4 %collective-permute-start.10 = (bf16[32,2688]{1,0:T(8,128)(2,1)S(1)}, bf16[32,2688]{1,0:T(8,128)(2,1)S(1)}, u32[]{:S(2)}, u32[]{:S(2)}) collective-permute-start(bf16[32,2688]{1,0:T(8,128)(2,1)S(1)} %get-tuple-element.84), channel_id=1, source_target_pairs={{0,8},{4,12},{8,0},{12,4},{1,9},{5,13},{9,1},{13,5},{2,10},{6,14},... | collective-permute-start | bytes 516104 | tf_op jit(solution)/shard_map/ppermute | solution.py:45
  62.7 1.2 collective-permute-start.11
  63.9 0.0 collective-permute-done.5.b
  63.9 0.0 collective-permute-done.6.c
  63.9 0.1 shard_map.115
  64.1 0.7 collective-permute-start.7
  64.7 3.6 %collective-permute-done.7.far_a = bf16[32,2304]{1,0:T(8,128)(2,1)S(1)} collective-permute-done((bf16[32,2304]{1,0:T(8,128)(2,1)S(1)}, bf16[32,2304]{1,0:T(8,128)(2,1)S(1)}, u32[]{:S(2)}, u32[]{:S(2)}) %collective-permute-start.7) | collective-permute-done | bytes 147488 | tf_op jit(solution)/shard_map/ppermute | solution.py:57
  68.3 1.3 collective-permute-done.10.two
  69.6 0.7 shard_map.117.refs_0_
  70.4 3.2 %collective-permute-start.14 = (bf16[32,4992]{1,0:T(8,128)(2,1)S(1)}, bf16[32,4992]{1,0:T(8,128)(2,1)S(1)}, u32[]{:S(2)}, u32[]{:S(2)}) collective-permute-start(bf16[32,4992]{1,0:T(8,128)(2,1)S(1)} %shard_map.117.refs_0_), channel_id=1, source_target_pairs={{0,12},{4,0},{8,4},{12,8},{1,13},{5,1},{9,5},{13,9},{2,14},{6,2},{... | collective-permute-start | bytes 958472 | tf_op jit(solution)/shard_map/ppermute | solution.py:45
  73.6 0.0 collective-permute-start.13
  73.6 0.3 collective-permute-start.12
  73.9 6.1 %collective-permute-done.14.refs_2_ = bf16[32,4992]{1,0:T(8,128)(2,1)S(1)} collective-permute-done((bf16[32,4992]{1,0:T(8,128)(2,1)S(1)}, bf16[32,4992]{1,0:T(8,128)(2,1)S(1)}, u32[]{:S(2)}, u32[]{:S(2)}) %collective-permute-start.14) | collective-permute-done | bytes 319520 | tf_op jit(solution)/shard_map/ppermute | solution.py:45
  80.0 2.1 %collective-permute-done.13.refs_3_ = bf16[32,4992]{1,0:T(8,128)(2,1)S(1)} collective-permute-done((bf16[32,4992]{1,0:T(8,128)(2,1)S(1)}, bf16[32,4992]{1,0:T(8,128)(2,1)S(1)}, u32[]{:S(2)}, u32[]{:S(2)}) %collective-permute-start.13) | collective-permute-done | bytes 319520 | tf_op jit(solution)/shard_map/ppermute | solution.py:45
  82.1 0.0 collective-permute-done.12.refs_1_
  82.1 0.2 collective-permute-start.17
  82.3 0.0 collective-permute-start.16
  82.3 2.7 %collective-permute-start.15 = (bf16[32,4992]{1,0:T(8,128)(2,1)S(1)}, bf16[32,4992]{1,0:T(8,128)(2,1)S(1)}, u32[]{:S(2)}, u32[]{:S(2)}) collective-permute-start(bf16[32,4992]{1,0:T(8,128)(2,1)S(1)} %collective-permute-done.14.refs_2_), channel_id=1, source_target_pairs={{0,12},{4,0},{8,4},{12,8},{1,13},{5,1},{9,5},{13,9},{2,14},{6,2},{... | collective-permute-start | bytes 958472 | tf_op jit(solution)/shard_map/ppermute | solution.py:45
  85.0 1.4 %shard_map.119.lines = s32[8,256]{1,0:T(8,128)S(1)} custom-call(s32[4]{0:T(128)S(1)} %pad_add_fusion.index, bf16[8,64,384]{2,1,0:T(8,128)(2,1)} %all_to_all.15.own), custom_call_target="tpu_custom_call" | custom-call | tf_op jit(solution)/shard_map/pallas_call | solution.py:65
  86.4 2.8 %shard_map.118 = (bf16[128,4992]{1,0:T(8,128)(2,1)S(1)}, f32[128,320]{1,0:T(8,128)S(1)}, f32[128,320]{1,0:T(8,128)S(1)}) custom-call(bf16[32,4992]{1,0:T(8,128)(2,1)S(1)} %shard_map.117.refs_0_, bf16[32,4992]{1,0:T(8,128)(2,1)S(1)} %collective-permute-done.12.refs_1_, bf16[32,4992]{1,0:T(8,128)(2,1)S(1)} %collective-permute-done.14.refs_2_, ...), custom_call_target="tpu_custom_call" | custom-call | flops 545259520 | bytes 6291456 | tf_op jit(solution)/shard_map/pallas_call | solution.py:65
  89.2 0.5 collective-permute-done.17.refs_2_
  89.7 1.0 collective-permute-start.18
  90.7 4.8 %collective-permute-done.18.refs_3_ = bf16[32,4992]{1,0:T(8,128)(2,1)S(1)} collective-permute-done((bf16[32,4992]{1,0:T(8,128)(2,1)S(1)}, bf16[32,4992]{1,0:T(8,128)(2,1)S(1)}, u32[]{:S(2)}, u32[]{:S(2)}) %collective-permute-start.18) | collective-permute-done | bytes 319520 | tf_op jit(solution)/shard_map/ppermute | solution.py:57
  95.5 3.7 %shard_map.120 = (bf16[128,4992]{1,0:T(8,128)(2,1)}, f32[128,320]{1,0:T(8,128)S(1)}, f32[128,320]{1,0:T(8,128)S(1)}) custom-call(bf16[32,4992]{1,0:T(8,128)(2,1)S(1)} %collective-permute-done.15.refs_0_, bf16[32,4992]{1,0:T(8,128)(2,1)S(1)} %collective-permute-done.16.refs_1_, bf16[32,4992]{1,0:T(8,128)(2,1)S(1)} %collective-permute-done.17.refs_2_, ...), custom_call_target="tpu_custom_call" | custom-call | flops 545259520 | bytes 6291456 | tf_op jit(solution)/shard_map/pallas_call | solution.py:65
  99.3 1.0 shard_map.121
  100.2 4.8 %collective-permute-start.19 = (bf16[512,320]{1,0:T(8,128)(2,1)S(1)}, bf16[512,320]{1,0:T(8,128)(2,1)S(1)}, u32[]{:S(2)}, u32[]{:S(2)}) collective-permute-start(bf16[512,320]{1,0:T(8,128)(2,1)S(1)} %shard_map.121), channel_id=1, source_target_pairs={{0,1},{1,0},{2,3},{3,2},{4,5},{5,4},{6,7},{7,6},{8,9},{9,8},{10,11... | collective-permute-start | bytes 983048 | tf_op jit(solution)/shard_map/ppermute | solution.py:61
  105.0 0.1 collective-permute-start.20
  105.1 1.2 collective-permute-done.19.sent
  106.4 0.4 collective-permute-start.21
  106.8 1.7 %shard_map.122 = bf16[512,320]{1,0:T(8,128)(2,1)} custom-call(s32[4]{0:T(128)S(1)} %pad_add_fusion.index, s32[8,256]{1,0:T(8,128)S(1)} %shard_map.119.lines, f32[128,320]{1,0:T(8,128)S(1)} %get-tuple-element.94.mine_e, f32[128,320]{1,0:T(8,128)S(1)} %get-tuple-element.95.other_e, f32[128,320]{1,0:T(8,128)S(1)} %get-tuple-element.99.mine_l, ...), custom_call_target="tpu_custom_call" | custom-call | flops 83886080 | bytes 1048576 | tf_op jit(solution)/shard_map/pallas_call | solution.py:65
  108.5 7.3 %all-to-all-start.2 = ((bf16[64,8,320]{2,1,0:T(8,128)(2,1)}), bf16[64,8,320]{2,1,0:T(8,128)(2,1)S(1)}, u32[]{:S(2)}, u32[]{:S(2)}) async-start(bf16[64,8,320]{2,1,0:T(8,128)(2,1)} %bitcast.5), calls=%async_computation.2 | async-start | bytes 786432 | tf_op jit(solution)/shard_map/all_to_all | solution.py:461
  115.8 1.0 copy-done.8
  116.9 7.5 %shard_map.123 = (bf16[320,3200]{1,0:T(8,128)(2,1)}, bf16[320,3200]{1,0:T(8,128)(2,1)}, bf16[320,3200]{1,0:T(8,128)(2,1)}) custom-call(s32[4]{0:T(128)} %copy-done.1, bf16[8,64,384]{2,1,0:T(8,128)(2,1)} %all_to_all.15.own, bf16[128,4992]{1,0:T(8,128)(2,1)} %copy-done.3, bf16[128,4992]{1,0:T(8,128)(2,1)} %get-tuple-element.105.late_in, ...), custom_call_target="tpu_custom_call" | custom-call | flops 1572864000 | bytes 12582912 | tf_op jit(solution)/shard_map/pallas_call | solution.py:379
  124.4 2.6 %all-to-all-done.2.back = bf16[64,8,320]{2,1,0:T(8,128)(2,1)S(1)} async-done(((bf16[64,8,320]{2,1,0:T(8,128)(2,1)}), bf16[64,8,320]{2,1,0:T(8,128)(2,1)S(1)}, u32[]{:S(2)}, u32[]{:S(2)}) %all-to-all-start.2) | async-done | bytes 327712 | tf_op jit(solution)/shard_map/all_to_all | solution.py:461
  127.0 1.7 %shard_map.124 = bf16[128,5120]{1,0:T(8,128)(2,1)} custom-call(bf16[8,128]{1,0:T(8,128)(2,1)S(1)} %copy-done.2, bf16[64,8,320]{2,1,0:T(8,128)(2,1)S(1)} %all-to-all-done.2.back), custom_call_target="tpu_custom_call" | custom-call | tf_op jit(solution)/shard_map/pallas_call | solution.py:65
  (21 shorter events, 0.0 us)
Async XLA Ops:
  0.6 10.5 %copy-start.4 = (bf16[320,3200]{1,0:T(8,128)(2,1)S(1)}, bf16[320,3200]{1,0:T(8,128)(2,1)}, u32[]{:S(2)}) copy-start(bf16[320,3200]{1,0:T(8,128)(2,1)} %param.13) | copy-start | bytes 6144004
  4.0 13.1 %all-to-all-start = ((bf16[16,8,384]{2,1,0:T(8,128)(2,1)}), bf16[16,8,384]{2,1,0:T(8,128)(2,1)S(1)}, u32[]{:S(2)}, u32[]{:S(2)}) async-start(bf16[16,8,384]{2,1,0:T(8,128)(2,1)} %get-tuple-element.60), calls=%async_computation | async-start | bytes 196608 | tf_op jit(solution)/shard_map/all_to_all | solution.py:414
  11.1 2.0 %copy-start.5 = (bf16[320,3200]{1,0:T(8,128)(2,1)S(1)}, bf16[320,3200]{1,0:T(8,128)(2,1)}, u32[]{:S(2)}) copy-start(bf16[320,3200]{1,0:T(8,128)(2,1)} %param.14) | copy-start | bytes 6144004
  13.1 2.0 %copy-start.6 = (bf16[3200,320]{0,1:T(8,128)(2,1)S(1)}, bf16[3200,320]{0,1:T(8,128)(2,1)}, u32[]{:S(2)}) copy-start(bf16[3200,320]{0,1:T(8,128)(2,1)} %param.15) | copy-start | bytes 6144004
  17.1 21.1 %collective-permute-start.1 = (bf16[320,1664]{1,0:T(8,128)(2,1)}, bf16[320,1664]{1,0:T(8,128)(2,1)S(1)}, u32[]{:S(2)}, u32[]{:S(2)}) collective-permute-start(bf16[320,1664]{1,0:T(8,128)(2,1)} %get-tuple-element.69), channel_id=1, source_target_pairs={{0,1},{1,0},{2,3},{3,2},{4,5},{5,4},{6,7},{7,6},{8,9},{9,8},{10,11... | collective-permute-start | bytes 3194888 | tf_op jit(solution)/shard_map/ppermute | solution.py:61
  17.6 20.6 %collective-permute-start.2 = (bf16[320,1664]{1,0:T(8,128)(2,1)}, bf16[320,1664]{1,0:T(8,128)(2,1)}, u32[]{:S(2)}, u32[]{:S(2)}) collective-permute-start(bf16[320,1664]{1,0:T(8,128)(2,1)} %get-tuple-element.70), channel_id=1, source_target_pairs={{0,1},{1,0},{2,3},{3,2},{4,5},{5,4},{6,7},{7,6},{8,9},{9,8},{10,11... | collective-permute-start | bytes 3194888 | tf_op jit(solution)/shard_map/ppermute | solution.py:61
  17.6 20.6 %collective-permute-start.3 = (bf16[320,1664]{1,0:T(8,128)(2,1)}, bf16[320,1664]{1,0:T(8,128)(2,1)}, u32[]{:S(2)}, u32[]{:S(2)}) collective-permute-start(bf16[320,1664]{1,0:T(8,128)(2,1)} %get-tuple-element.71), channel_id=1, source_target_pairs={{0,1},{1,0},{2,3},{3,2},{4,5},{5,4},{6,7},{7,6},{8,9},{9,8},{10,11... | collective-permute-start | bytes 3194888 | tf_op jit(solution)/shard_map/ppermute | solution.py:61
  35.0 3.2 %collective-permute-start = (bf16[8,64,384]{2,1,0:T(8,128)(2,1)}, bf16[8,64,384]{2,1,0:T(8,128)(2,1)}, u32[]{:S(2)}, u32[]{:S(2)}) collective-permute-start(bf16[8,64,384]{2,1,0:T(8,128)(2,1)} %all_to_all.15.own), channel_id=1, source_target_pairs={{0,1},{1,0},{2,3},{3,2},{4,5},{5,4},{6,7},{7,6},{8,9},{9,8},{10,11... | collective-permute-start | bytes 1179656 | tf_op jit(solution)/shard_map/ppermute | solution.py:61
  36.5 70.3 %copy-start.1 = (s32[4]{0:T(128)}, s32[4]{0:T(128)S(1)}, u32[]{:S(2)}) copy-start(s32[4]{0:T(128)S(1)} %pad_add_fusion.index) | copy-start | bytes 52
  38.1 1.2 copy-start
  42.6 16.7 %collective-permute-start.8 = (bf16[128,2688]{1,0:T(8,128)(2,1)S(1)}, bf16[128,2688]{1,0:T(8,128)(2,1)S(1)}, u32[]{:S(2)}, u32[]{:S(2)}) collective-permute-start(bf16[128,2688]{1,0:T(8,128)(2,1)S(1)} %get-tuple-element.81), channel_id=1, source_target_pairs={{0,2},{2,0},{1,3},{3,1},{4,6},{6,4},{5,7},{7,5},{8,10},{10,8},{9,1... | collective-permute-start | bytes 2064392 | tf_op jit(solution)/shard_map/ppermute | solution.py:57
  45.8 16.9 %collective-permute-start.4 = (bf16[64,2304]{1,0:T(8,128)(2,1)S(1)}, bf16[64,2304]{1,0:T(8,128)(2,1)S(1)}, u32[]{:S(2)}, u32[]{:S(2)}) collective-permute-start(bf16[64,2304]{1,0:T(8,128)(2,1)S(1)} %get-tuple-element.75), channel_id=1, source_target_pairs={{0,4},{4,8},{8,12},{12,0},{1,5},{5,9},{9,13},{13,1},{2,6},{6,10},{... | collective-permute-start | bytes 884744 | tf_op jit(solution)/shard_map/ppermute | solution.py:45
  47.1 16.8 %collective-permute-start.5 = (bf16[64,2304]{1,0:T(8,128)(2,1)S(1)}, bf16[64,2304]{1,0:T(8,128)(2,1)S(1)}, u32[]{:S(2)}, u32[]{:S(2)}) collective-permute-start(bf16[64,2304]{1,0:T(8,128)(2,1)S(1)} %get-tuple-element.76), channel_id=1, source_target_pairs={{0,8},{4,12},{8,0},{12,4},{1,9},{5,13},{9,1},{13,5},{2,10},{6,14},... | collective-permute-start | bytes 884744 | tf_op jit(solution)/shard_map/ppermute | solution.py:45
  49.5 14.4 %collective-permute-start.6 = (bf16[64,2304]{1,0:T(8,128)(2,1)S(1)}, bf16[64,2304]{1,0:T(8,128)(2,1)S(1)}, u32[]{:S(2)}, u32[]{:S(2)}) collective-permute-start(bf16[64,2304]{1,0:T(8,128)(2,1)S(1)} %get-tuple-element.77), channel_id=1, source_target_pairs={{0,12},{4,0},{8,4},{12,8},{1,13},{5,1},{9,5},{13,9},{2,14},{6,2},{... | collective-permute-start | bytes 884744 | tf_op jit(solution)/shard_map/ppermute | solution.py:45
  59.5 8.9 %collective-permute-start.9 = (bf16[32,2688]{1,0:T(8,128)(2,1)S(1)}, bf16[32,2688]{1,0:T(8,128)(2,1)S(1)}, u32[]{:S(2)}, u32[]{:S(2)}) collective-permute-start(bf16[32,2688]{1,0:T(8,128)(2,1)S(1)} %get-tuple-element.83), channel_id=1, source_target_pairs={{0,4},{4,8},{8,12},{12,0},{1,5},{5,9},{9,13},{13,1},{2,6},{6,10},{... | collective-permute-start | bytes 516104 | tf_op jit(solution)/shard_map/ppermute | solution.py:45
  60.3 9.3 %collective-permute-start.10 = (bf16[32,2688]{1,0:T(8,128)(2,1)S(1)}, bf16[32,2688]{1,0:T(8,128)(2,1)S(1)}, u32[]{:S(2)}, u32[]{:S(2)}) collective-permute-start(bf16[32,2688]{1,0:T(8,128)(2,1)S(1)} %get-tuple-element.84), channel_id=1, source_target_pairs={{0,8},{4,12},{8,0},{12,4},{1,9},{5,13},{9,1},{13,5},{2,10},{6,14},... | collective-permute-start | bytes 516104 | tf_op jit(solution)/shard_map/ppermute | solution.py:45
  62.7 6.9 %collective-permute-start.11 = (bf16[32,2688]{1,0:T(8,128)(2,1)S(1)}, bf16[32,2688]{1,0:T(8,128)(2,1)S(1)}, u32[]{:S(2)}, u32[]{:S(2)}) collective-permute-start(bf16[32,2688]{1,0:T(8,128)(2,1)S(1)} %get-tuple-element.85), channel_id=1, source_target_pairs={{0,12},{4,0},{8,4},{12,8},{1,13},{5,1},{9,5},{13,9},{2,14},{6,2},{... | collective-permute-start | bytes 516104 | tf_op jit(solution)/shard_map/ppermute | solution.py:45
  64.1 4.3 %collective-permute-start.7 = (bf16[32,2304]{1,0:T(8,128)(2,1)S(1)}, bf16[32,2304]{1,0:T(8,128)(2,1)S(1)}, u32[]{:S(2)}, u32[]{:S(2)}) collective-permute-start(bf16[32,2304]{1,0:T(8,128)(2,1)S(1)} %get-tuple-element.79), channel_id=1, source_target_pairs={{0,2},{2,0},{1,3},{3,1},{4,6},{6,4},{5,7},{7,5},{8,10},{10,8},{9,1... | collective-permute-start | bytes 442376 | tf_op jit(solution)/shard_map/ppermute | solution.py:57
  70.4 9.6 %collective-permute-start.14 = (bf16[32,4992]{1,0:T(8,128)(2,1)S(1)}, bf16[32,4992]{1,0:T(8,128)(2,1)S(1)}, u32[]{:S(2)}, u32[]{:S(2)}) collective-permute-start(bf16[32,4992]{1,0:T(8,128)(2,1)S(1)} %shard_map.117.refs_0_), channel_id=1, source_target_pairs={{0,12},{4,0},{8,4},{12,8},{1,13},{5,1},{9,5},{13,9},{2,14},{6,2},{... | collective-permute-start | bytes 958472 | tf_op jit(solution)/shard_map/ppermute | solution.py:45
  73.6 8.5 %collective-permute-start.13 = (bf16[32,4992]{1,0:T(8,128)(2,1)S(1)}, bf16[32,4992]{1,0:T(8,128)(2,1)S(1)}, u32[]{:S(2)}, u32[]{:S(2)}) collective-permute-start(bf16[32,4992]{1,0:T(8,128)(2,1)S(1)} %shard_map.117.refs_0_), channel_id=1, source_target_pairs={{0,4},{4,8},{8,12},{12,0},{1,5},{5,9},{9,13},{13,1},{2,6},{6,10},{... | collective-permute-start | bytes 958472 | tf_op jit(solution)/shard_map/ppermute | solution.py:45
  73.6 8.5 %collective-permute-start.12 = (bf16[32,4992]{1,0:T(8,128)(2,1)S(1)}, bf16[32,4992]{1,0:T(8,128)(2,1)S(1)}, u32[]{:S(2)}, u32[]{:S(2)}) collective-permute-start(bf16[32,4992]{1,0:T(8,128)(2,1)S(1)} %shard_map.117.refs_0_), channel_id=1, source_target_pairs={{0,2},{2,0},{1,3},{3,1},{4,6},{6,4},{5,7},{7,5},{8,10},{10,8},{9,1... | collective-permute-start | bytes 958472 | tf_op jit(solution)/shard_map/ppermute | solution.py:57
  82.1 7.6 %collective-permute-start.17 = (bf16[32,4992]{1,0:T(8,128)(2,1)S(1)}, bf16[32,4992]{1,0:T(8,128)(2,1)S(1)}, u32[]{:S(2)}, u32[]{:S(2)}) collective-permute-start(bf16[32,4992]{1,0:T(8,128)(2,1)S(1)} %collective-permute-done.12.refs_1_), channel_id=1, source_target_pairs={{0,4},{4,8},{8,12},{12,0},{1,5},{5,9},{9,13},{13,1},{2,6},{6,10},{... | collective-permute-start | bytes 958472 | tf_op jit(solution)/shard_map/ppermute | solution.py:45
  82.3 7.4 %collective-permute-start.16 = (bf16[32,4992]{1,0:T(8,128)(2,1)S(1)}, bf16[32,4992]{1,0:T(8,128)(2,1)S(1)}, u32[]{:S(2)}, u32[]{:S(2)}) collective-permute-start(bf16[32,4992]{1,0:T(8,128)(2,1)S(1)} %collective-permute-done.14.refs_2_), channel_id=1, source_target_pairs={{0,2},{2,0},{1,3},{3,1},{4,6},{6,4},{5,7},{7,5},{8,10},{10,8},{9,1... | collective-permute-start | bytes 958472 | tf_op jit(solution)/shard_map/ppermute | solution.py:57
  82.3 7.4 %collective-permute-start.15 = (bf16[32,4992]{1,0:T(8,128)(2,1)S(1)}, bf16[32,4992]{1,0:T(8,128)(2,1)S(1)}, u32[]{:S(2)}, u32[]{:S(2)}) collective-permute-start(bf16[32,4992]{1,0:T(8,128)(2,1)S(1)} %collective-permute-done.14.refs_2_), channel_id=1, source_target_pairs={{0,12},{4,0},{8,4},{12,8},{1,13},{5,1},{9,5},{13,9},{2,14},{6,2},{... | collective-permute-start | bytes 958472 | tf_op jit(solution)/shard_map/ppermute | solution.py:45
  89.1 15.9 %copy-start.3 = (bf16[128,4992]{1,0:T(8,128)(2,1)}, bf16[128,4992]{1,0:T(8,128)(2,1)S(1)}, u32[]{:S(2)}) copy-start(bf16[128,4992]{1,0:T(8,128)(2,1)S(1)} %get-tuple-element.103.early_in) | copy-start | bytes 3833860
  89.7 5.8 %collective-permute-start.18 = (bf16[32,4992]{1,0:T(8,128)(2,1)S(1)}, bf16[32,4992]{1,0:T(8,128)(2,1)S(1)}, u32[]{:S(2)}, u32[]{:S(2)}) collective-permute-start(bf16[32,4992]{1,0:T(8,128)(2,1)S(1)} %collective-permute-done.15.refs_0_), channel_id=1, source_target_pairs={{0,2},{2,0},{1,3},{3,1},{4,6},{6,4},{5,7},{7,5},{8,10},{10,8},{9,1... | collective-permute-start | bytes 958472 | tf_op jit(solution)/shard_map/ppermute | solution.py:57
  100.2 6.1 %collective-permute-start.19 = (bf16[512,320]{1,0:T(8,128)(2,1)S(1)}, bf16[512,320]{1,0:T(8,128)(2,1)S(1)}, u32[]{:S(2)}, u32[]{:S(2)}) collective-permute-start(bf16[512,320]{1,0:T(8,128)(2,1)S(1)} %shard_map.121), channel_id=1, source_target_pairs={{0,1},{1,0},{2,3},{3,2},{4,5},{5,4},{6,7},{7,6},{8,9},{9,8},{10,11... | collective-permute-start | bytes 983048 | tf_op jit(solution)/shard_map/ppermute | solution.py:61
  105.0 3.5 %collective-permute-start.20 = (bf16[128,4992]{1,0:T(8,128)(2,1)S(1)}, bf16[128,4992]{1,0:T(8,128)(2,1)S(1)}, u32[]{:S(2)}, u32[]{:S(2)}) collective-permute-start(bf16[128,4992]{1,0:T(8,128)(2,1)S(1)} %get-tuple-element.103.early_in), channel_id=1, source_target_pairs={{0,1},{1,0},{2,3},{3,2},{4,5},{5,4},{6,7},{7,6},{8,9},{9,8},{10,11... | collective-permute-start | bytes 3833864 | tf_op jit(solution)/shard_map/ppermute | solution.py:61
  106.4 9.4 %collective-permute-start.21 = (bf16[128,4992]{1,0:T(8,128)(2,1)}, bf16[128,4992]{1,0:T(8,128)(2,1)S(1)}, u32[]{:S(2)}, u32[]{:S(2)}) collective-permute-start(bf16[128,4992]{1,0:T(8,128)(2,1)} %get-tuple-element.105.late_in), channel_id=1, source_target_pairs={{0,1},{1,0},{2,3},{3,2},{4,5},{5,4},{6,7},{7,6},{8,9},{9,8},{10,11... | collective-permute-start | bytes 3833864 | tf_op jit(solution)/shard_map/ppermute | solution.py:61
  108.5 7.3 %copy-start.7 = (bf16[128,4992]{1,0:T(8,128)(2,1)}, bf16[128,4992]{1,0:T(8,128)(2,1)S(1)}, u32[]{:S(2)}) copy-start(bf16[128,4992]{1,0:T(8,128)(2,1)S(1)} %collective-permute-done.20.early_other_in) | copy-start | bytes 3833860
  108.5 18.5 %all-to-all-start.2 = ((bf16[64,8,320]{2,1,0:T(8,128)(2,1)}), bf16[64,8,320]{2,1,0:T(8,128)(2,1)S(1)}, u32[]{:S(2)}, u32[]{:S(2)}) async-start(bf16[64,8,320]{2,1,0:T(8,128)(2,1)} %bitcast.5), calls=%async_computation.2 | async-start | bytes 786432 | tf_op jit(solution)/shard_map/all_to_all | solution.py:461
  115.8 11.2 %copy-start.2 = (bf16[8,128]{1,0:T(8,128)(2,1)S(1)}, bf16[8,128]{1,0:T(8,128)(2,1)}, u32[]{:S(2)}) copy-start(bf16[8,128]{1,0:T(8,128)(2,1)} %get-tuple-element.58.owner) | copy-start | bytes 6148
  115.8 1.0 copy-start.8

commit v4 on v3

--- a/solution.py
+++ b/solution.py
@@ -105,7 +105,8 @@
     take_x = jnp.zeros((2 * CAP, CAP * 16), F32)
     take_y = jnp.zeros((2 * CAP, CAP * 16), F32)
     scale = jnp.zeros((2 * CAP, 1), F32)
-    place = jnp.where(lane_of == 0, float(FAR), 0.0)
+    d = lax.axis_index(("y", "zh"))
+    place = jnp.where(lane_of < 2, float(FAR), 0.0)
     for s in range(CAP):
         r = chosen[0, 0, s]
         one = jnp.where(s < count, 1.0, 0.0).astype(F32)
@@ -113,11 +114,11 @@
         take_x = jnp.where((row == s) & (lane == at), one, take_x)
         take_y = jnp.where((row == s + CAP) & (lane == at), one, take_y)
         scale = jnp.where(line == s + CAP, advantage[r], scale)
-        spot = jnp.where(s < count, before + s, FAR).astype(F32)
+        spot = jnp.where(s < count, d * GROUP + before + s, FAR).astype(F32)
         place = jnp.where((wide == s) & (lane_of == 0), spot, place)
-        place = jnp.where((wide == s + CAP) & (lane_of == 0), spot + GROUP, place)
+        place = jnp.where((wide == s + CAP) & (lane_of == 1), spot, place)
         slot = (f * CAP + s + 1).astype(F32)
-        place = jnp.where((wide == s) & (lane_of == 1), slot, place)
+        place = jnp.where((wide == s) & (lane_of == 2), slot, place)
     mark = jnp.zeros((2 * CAP, ROWS), F32)
     row = lax.broadcasted_iota(jnp.int32, (2 * CAP, ROWS), 0)
     lane = lax.broadcasted_iota(jnp.int32, (2 * CAP, ROWS), 1)
@@ -131,15 +132,17 @@
     both = (x + y).astype(BF)
     place = place.astype(BF)
     for k in range(N_FSDP):
-        out[k, :, 0:DL] = both[:, k * DL : (k + 1) * DL]
-        out[k, :, DL:MSG] = place
+        part = both[:, k * DL : (k + 1) * DL]
+        for i in range(N_DP):
+            out[i * N_FSDP + k, :, 0:DL] = part
+            out[i * N_FSDP + k, :, DL:MSG] = place
 
 
 def messages(*operands):
     return pl.pallas_call(
         message_kernel,
         out_shape=[
-            jax.ShapeDtypeStruct((N_FSDP, 2 * CAP, MSG), BF),
+            jax.ShapeDtypeStruct((N_DEV, 2 * CAP, MSG), BF),
             jax.ShapeDtypeStruct((2 * CAP, ROWS), BF),
         ],
         in_specs=[ANY] * 5,
@@ -158,11 +161,14 @@
 
 
 def pack_kernel(lines, out):
-    spot = lax.broadcasted_iota(jnp.int32, (N_FSDP * 2 * CAP, 2 * GROUP), 1)
-    place = lines[:, DL : DL + 1].astype(jnp.int32)
-    rows = dot(jnp.where(place == spot, 1.0, 0.0).astype(BF), lines[...], 0, 0).astype(BF)
-    for i in range(N_DP):
-        out[i] = rows
+    places = jnp.transpose(lines[:, MSG - 128 : MSG].astype(F32)).astype(jnp.int32)
+    spot = lax.broadcasted_iota(jnp.int32, (LIVE, N_DEV * 2 * CAP), 0)
+    for k in range(2):
+        at = DL - (MSG - 128) + k
+        pack = jnp.where(places[at : at + 1, :] == spot, 1.0, 0.0).astype(BF)
+        rows = dot(pack, lines[...], 1, 0).astype(BF)
+        for i in range(N_DP):
+            out[i, k * GROUP : (k + 1) * GROUP, :] = rows[i * GROUP : (i + 1) * GROUP]
 
 
 def gather_rows(index, rows, order, x, y=None):
@@ -195,12 +201,16 @@
             store(slice(k * n + at, k * n + to), total)
 
 
-def kernel_b(index, own, sib, w0, w1, w2, w3, w4, w5, far, near, *scratch):
+def kernel_b(index, own, sib, w0, w1, w2, w3, w4, w5, far0, far, near, *scratch):
     def store(cols, total):
         for dx in range(4):
             here, near_at = slice(dx * GROUP, (dx + 1) * GROUP), 2 * dx * GROUP
             near[here, cols] = total[near_at : near_at + GROUP]
-            far[here, cols] = total[near_at + GROUP : near_at + 2 * GROUP].astype(BF)
+            away = total[near_at + GROUP : near_at + 2 * GROUP].astype(BF)
+            if dx:
+                far[(dx - 1) * GROUP : dx * GROUP, cols] = away
+            else:
+                far0[:, cols] = away
 
     products(index, own, sib, (w0, w1, w2, w3, w4, w5), NA, NB, scratch, store)
 
@@ -226,11 +236,10 @@
     )
 
 
-def sum_b_kernel(near, far, here, right, two, left):
-    here[...] = near[0:GROUP] + far[0:GROUP].astype(F32)
+def sum_b_kernel(near, far, right, two, left):
     for k, out in enumerate((right, two, left)):
         rows = slice((k + 1) * GROUP, (k + 2) * GROUP)
-        out[...] = (near[rows] + far[rows].astype(F32)).astype(BF)
+        out[...] = (near[rows] + far[k * GROUP : (k + 1) * GROUP].astype(F32)).astype(BF)
 
 
 def sum_a_kernel(mine, a, b, c, here, far):
@@ -250,9 +259,9 @@
     return hidden, gate_delta, up_delta
 
 
-def value_kernel(index, mine_a, far_a, mine_b, right, two, left, out):
+def value_kernel(index, mine_a, far_a, near, far0, right, two, left, out):
     sums_a = mine_a[...] + far_a[...].astype(F32)
-    sums_b = mine_b[...] + right[...].astype(F32) + two[...].astype(F32) + left[...].astype(F32)
+    sums_b = near[0:GROUP] + far0[...].astype(F32) + right[...].astype(F32) + two[...].astype(F32) + left[...].astype(F32)
     of_a = swiglu_backward(*[sums_a[:, k * NA : (k + 1) * NA] for k in range(3)])
     of_b = swiglu_backward(*[sums_b[:, k * NB : (k + 1) * NB] for k in range(3)])
     unit = lax.broadcasted_iota(jnp.int32, (GROUP, NA), 1)
@@ -262,28 +271,36 @@
         out[:, k * WIN + NA : (k + 1) * WIN] = of_b[k].astype(BF)
 
 
+def lay_kernel(*refs):
+    for k, block in enumerate(refs[:-1]):
+        refs[-1][k * GROUP : (k + 1) * GROUP, :] = block[...]
+
+
+def laid(blocks):
+    rows = len(blocks) * GROUP
+    return call(lay_kernel, [((rows, 3 * WIN), BF)], blocks, estimate=cost(0, 4 * 2**20))[0]
+
+
 def back_kernel(*refs):
-    blocks, (go, gs, uo, us, value, mine, other) = refs[:4], refs[4:]
-    for k, block in enumerate(blocks):
-        value[k * GROUP : (k + 1) * GROUP, :] = block[...]
+    value, (go, gs, uo, us, mine, other) = refs[0], refs[1:]
     gate, up_w = value[:, WIN : 2 * WIN], value[:, 2 * WIN :]
     other[...] = dot(gate, gs[...], 1, 1) + dot(up_w, us[...], 1, 1)
     mine[...] = dot(gate, go[...], 1, 1) + dot(up_w, uo[...], 1, 1)
 
 
-def back_products(blocks, weights):
-    rows = 4 * GROUP
+def back_products(value, weights):
+    rows = value.shape[0]
     return call(
         back_kernel,
-        [((rows, 3 * WIN), BF), ((rows, DL), F32), ((rows, DL), F32)],
-        [*blocks, *weights],
+        [((rows, DL), F32)] * 2,
+        [value, *weights],
         estimate=cost(2 * rows * DL * 4 * WIN, 6 * 2**20),
     )
 
 
 def line_kernel(index, own, out):
     parts = []
-    lane = DL + 1 - (MSG - 128)
+    lane = DL + 2 - (MSG - 128)
     for dx, dz in ORDER:
         i = (index[1] + dx) % 4 * 2 + (index[2] + dz) % 2
         slot = own[i, 0:GROUP, MSG - 128 : MSG].astype(F32)[:, lane : lane + 1].astype(jnp.int32) - 1
@@ -296,24 +313,27 @@
     out[...] = jnp.transpose(lines)[0:8, :].astype(jnp.int32)
 
 
-def unpack(index, core, lines, mine_e, other_e, mine_l, other_l):
+def unpack(index, core, lines, parts):
     c = index[3]
     line = jnp.where(core == 0, lines[0:1, :], lines[1:2, :])
-    mine = jnp.concatenate([mine_e[...], mine_l[...]])
-    other = jnp.concatenate([other_e[...], other_l[...]])
+    mine = jnp.concatenate([part[...] for part in parts[0::2]])
+    other = jnp.concatenate([part[...] for part in parts[1::2]])
     at = lax.broadcasted_iota(jnp.int32, (CAP * N_DEV, LIVE), 0)
     low = jnp.where(at == jnp.where(c == 0, line, line + CAP), 1.0, 0.0).astype(BF)
     high = jnp.where(at == jnp.where(c == 0, line + CAP, line), 1.0, 0.0).astype(BF)
     return dot(low, mine.astype(BF), 1, 0) + dot(high, other.astype(BF), 1, 0)
 
 
-def unpack_send_kernel(index, lines, mine_e, other_e, mine_l, other_l, out):
-    out[...] = unpack(index, 1 - index[3], lines, mine_e, other_e, mine_l, other_l).astype(BF)
-
-
-def unpack_keep_kernel(index, lines, mine_e, other_e, mine_l, other_l, sent, out):
-    kept = unpack(index, index[3], lines, mine_e, other_e, mine_l, other_l)
-    out[...] = (kept + sent[...].astype(F32)).astype(BF)
+def unpack_send_kernel(index, lines, *refs):
+    refs[-1][...] = unpack(index, 1 - index[3], lines, refs[:-1]).astype(BF)
+
+
+def unpack_keep_kernel(index, lines, *refs):
+    refs[-1][...] = unpack(index, index[3], lines, refs[:-1])
+
+
+def add_kernel(kept, sent, out):
+    out[...] = (kept[...] + sent[...].astype(F32)).astype(BF)
 
 
 def owner_kernel(owner, back, out):
@@ -400,64 +420,65 @@
     )
     first = lax.axis_index("c") == 0
 
-    def window(w):
-        lo, hi = w[:, :WIN], w[:, HI:]
-        return jnp.where(first, lo, hi), jnp.where(first, hi, lo)
-
-    mine, halves = [], []
-    for w in (gate_weight, up_weight, down_weight.T):
+    def half(w, which):
+        return jnp.where(which, w[:, :WIN], w[:, HI:])
+
+    full = [gate_weight, up_weight, down_weight.T]
+    halves = []
+    for w in full:
         if halves:
             w, halves[-1] = lax.optimization_barrier((w, halves[-1]))
-        a, b = window(w)
-        mine.append(a)
-        halves.append(b)
-    got = lax.all_to_all(message, ("x", "zl", "c"), 0, 0, tiled=True)
-    got, *halves = lax.optimization_barrier((got, *halves))
-    weights = [w for pair in zip(mine, map(sibling, halves)) for w in pair]
-    packed = call(pack_kernel, [((N_DP, 2 * GROUP, MSG), BF)], [got.reshape(N_FSDP * 2 * CAP, MSG)])[0]
-    own = lax.all_to_all(packed, ("y", "zh"), 0, 0, tiled=True)
+        halves.append(half(w, ~first))
+    got = lax.all_to_all(message, AXES, 0, 0, tiled=True)
+    got = lax.optimization_barrier((got, *halves))[0]
+    own = call(pack_kernel, [((N_DP, 2 * GROUP, MSG), BF)], [got.reshape(N_DEV * 2 * CAP, MSG)])[0]
+    own, *full = lax.optimization_barrier((own, *full))
+    weights = [w for f, h in zip(full, halves) for w in (half(f, first), sibling(h))]
     sib = sibling(own)
 
-    far, near = local_products(
-        kernel_b, NB, [(4 * GROUP, BF), (4 * GROUP, F32)], index, own, sib, *weights
+    far0, far, near = local_products(
+        kernel_b, NB, [(GROUP, BF), (3 * GROUP, BF), (4 * GROUP, F32)], index, own, sib, *weights
     )
     own_a, near = lax.optimization_barrier((own, near))
     here_a, right, two, left = local_products(
         kernel_a, NA, [(2 * GROUP, F32)] + [(2 * GROUP, BF)] * 3, index, own_a, sib, *weights
     )
-    far = across(far)
+    far0, far = across(far0), across(far)
     right, left, two = up(right), down(left), along(two, 2)
     shape_a, shape_b = (GROUP, 3 * NA), (GROUP, 3 * NB)
-    here_b, right_b, two_b, left_b = call(
-        sum_b_kernel, [(shape_b, F32)] + [(shape_b, BF)] * 3, [near, far]
-    )
+    right_b, two_b, left_b = call(sum_b_kernel, [(shape_b, BF)] * 3, [near, far])
     here_a, far_a = call(sum_a_kernel, [(shape_a, F32), (shape_a, BF)], [here_a, right, two, left])
     far_a = across(far_a)
     right_b, left_b, two_b = up(right_b), down(left_b), along(two_b, 2)
     v00 = call(
         value_kernel,
         [((GROUP, 3 * WIN), BF)],
-        [index, here_a, far_a, here_b, right_b, two_b, left_b],
+        [index, here_a, far_a, near, far0, right_b, two_b, left_b],
         smem=1,
     )[0]
 
     v01, v30, v10 = lax.optimization_barrier((across(v00), up(v00), down(v00)))
-    early, mine_e, other_e = back_products([v00, v01, v10, v30], weights[:4])
+    early = laid([v00, v01, v10, v30])
+    backs = back_products(early, weights[:4])
     lines = call(line_kernel, [((8, LIVE), jnp.int32)], [index, own], smem=1)[0]
     v20, v11, v31, early, lines = lax.optimization_barrier(
         (down(v10), across(v10), up(v01), early, lines)
     )
-    v21, mine_e, other_e = lax.optimization_barrier((across(v20), mine_e, other_e))
-    late, mine_l, other_l = back_products([v20, v11, v31, v21], weights[:4])
+    v21 = across(v20)
+    backs += back_products(laid([v20, v11, v31]), weights[:4])
+    v21, *backs = lax.optimization_barrier((v21, *backs))
+    backs += back_products(v21, weights[:4])
     early_other = sibling(early)
 
-    backs = [index, lines, mine_e, other_e, mine_l, other_l]
+    backs = [index, lines, *backs]
     shape, price = (CAP * N_DEV, DL), cost(2 * CAP * N_DEV * LIVE * DL, 2**20)
     sent = call(unpack_send_kernel, [(shape, BF)], backs, smem=1, estimate=price)[0]
-    sent, late = lax.optimization_barrier((sibling(sent), late))
+    v20, v21, sent = lax.optimization_barrier((v20, v21, sent))
+    late = laid([v20, v11, v31, v21])
+    kept = call(unpack_keep_kernel, [(shape, F32)], backs, smem=1, estimate=price)[0]
+    sent, late, kept = lax.optimization_barrier((sibling(sent), late, kept))
     late_other = sibling(late)
-    back = call(unpack_keep_kernel, [(shape, BF)], [*backs, sent], smem=1, estimate=price)[0]
-    back, early_other = lax.optimization_barrier((back, early_other))
+    back = call(add_kernel, [(shape, BF)], [kept, sent])[0]
     back = lax.all_to_all(back.reshape(N_DEV // 2, 2 * CAP, DL), AXES[:4], 0, 0, tiled=True)
 
     gate_grad, up_grad, down_grad = weight_grads(index, own, early, late, early_other, late_other)

time: 130 us -> 123 us (0.946)
  blocking collectives: 16.6 us -> 0 us
  waiting for transfers between devices: 33.1 us -> 42.4 us
  starting transfers between devices: 39.8 us -> 42.8 us
  Pallas kernels: 30.6 us -> 27.9 us
  other arithmetic: 3.97 us -> 6.06 us
  local copies, waits for them, and re-layouts: 3.84 us -> 2.03 us
    all_to_all x1 -> x0, blocking collectives: 16.6 us -> none  [shards(): own = lax.all_to_all(packed, ('y', 'zh'), 0, 0, tiled=True)]
    all_to_all x1, waiting for transfers between devices: 0.45 us -> 9.94 us  [shards(): got = lax.all_to_all(message, AXES, 0, 0, tiled=True)]
    ppermute x10, waiting for transfers between devices: 10 us -> 18 us  [along(): return lax.ppermute(t, 'x', [(i, (i + step) % 4) for i in range(4)])]
    ppermute x5 -> x6, waiting for transfers between devices: 17.1 us -> 10.7 us  [across(): return lax.ppermute(t, 'zl', SWAP)]
    all_to_all x1, starting transfers between devices: 7.18 us -> 11.5 us  [shards(): got = lax.all_to_all(message, AXES, 0, 0, tiled=True)]
    ppermute x5 -> x6, starting transfers between devices: 2.21 us -> 5.97 us  [across(): return lax.ppermute(t, 'zl', SWAP)]
    ppermute x10, starting transfers between devices: 15.4 us -> 12.2 us  [along(): return lax.ppermute(t, 'x', [(i, (i + step) % 4) for i in range(4)])]
    pallas_call x12 -> x17, Pallas kernels: 19.8 us -> 16.8 us  [call(): pl.pallas_call(kernel, out_shape=[jax.ShapeDtypeStruct(s, k) for s, k in...]
  transfers between devices with their start and end apart: 24 -> 25, of which waited for: 11 -> 13; matrix products, arithmetic and copies ran while one was open for 3% -> 5% of each run, Pallas kernels for 13% -> 14%
where the time goes in v4:
time: 123 us; the launch traced here: 122 us
  starting transfers between devices  42.8 us (35%)
  waiting for transfers between devices  42.4 us (34%)
  Pallas kernels  27.9 us (23%)
  other arithmetic  6.06 us (5%)
  local copies, waits for them, and re-layouts  2.03 us (2%)
    ppermute x10, waiting for transfers between devices, along(): return lax.ppermute(t, 'x', [(i, (i + step) % 4) for i in range(4)])  18 us
    pallas_call x17, Pallas kernels, call(): pl.pallas_call(kernel, out_shape=[jax.ShapeDtypeStruct(s, k) for s, k in...  16.8 us
    ppermute x10, starting transfers between devices, along(): return lax.ppermute(t, 'x', [(i, (i + step) % 4) for i in range(4)])  12.2 us
    all_to_all x1, starting transfers between devices, shards(): got = lax.all_to_all(message, AXES, 0, 0, tiled=True)  11.5 us
    ppermute x6, waiting for transfers between devices, across(): return lax.ppermute(t, 'zl', SWAP)  10.7 us
    all_to_all x1, waiting for transfers between devices, shards(): got = lax.all_to_all(message, AXES, 0, 0, tiled=True)  9.94 us
    pallas_call x1, Pallas kernels, weight_grads(): pl.pallas_call(grad_kernel, out_shape=[jax.ShapeDtypeStruct((DL, FL), BF)...  7.55 us
    ppermute x7, starting transfers between devices, sibling(): return lax.ppermute(t, 'c', SWAP)  6.61 us
  transfers between devices with their start and end apart: 25, of which 13 were waited for; matrix products, arithmetic and copies ran while one was open for 5% of the time, Pallas kernels for 14%

profile of v4, /device:TPU:1, one launch (start us, length us, event | category | flops | bytes accessed | tf_op | source)
XLA Modules:
  0.0 122.1 jit_solution(9645742266794663001)
XLA Ops:
  0.6 0.0 copy-start.7
  0.6 3.6 %shard_map.111 = (bf16[128,8,384]{2,1,0:T(8,128)(2,1)}, bf16[8,128]{1,0:T(8,128)(2,1)}) custom-call(s32[1,1,4]{2,1,0:T(1,128)} %chosen_in.1, s32[1,16]{1,0:T(1,128)} %counts_in.1, f32[128]{0:T(128)} %advantage_in.1, bf16[128,5120]{1,0:T(8,128)(2,1)} %tokens.1, bf16[128,5120]{1,0:T(8,128)(2,1)} %cotangent.1), custom_call_target="tpu_custom_call" | custom-call | tf_op jit(solution)/shard_map/pallas_call | solution.py:142
  4.2 11.5 %all-to-all-start = ((bf16[128,8,384]{2,1,0:T(8,128)(2,1)}), bf16[128,8,384]{2,1,0:T(8,128)(2,1)S(1)}, u32[]{:S(2)}, u32[]{:S(2)}) async-start(bf16[128,8,384]{2,1,0:T(8,128)(2,1)} %get-tuple-element.65), calls=%async_computation | async-start | bytes 1572864 | tf_op jit(solution)/shard_map/all_to_all | solution.py:432
  15.8 0.0 copy-start.6
  15.8 1.1 slice_select_fusion.5
  16.9 0.8 copy-done.6
  17.7 1.1 slice_select_fusion.4
  18.8 0.9 copy-done.5
  19.7 1.1 slice_select_fusion.3
  20.8 1.1 collective-permute-start.3
  21.9 0.5 collective-permute-start.1
  22.4 0.1 pad_add_fusion.index
  22.5 9.9 %all-to-all-done = bf16[128,8,384]{2,1,0:T(8,128)(2,1)S(1)} async-done(((bf16[128,8,384]{2,1,0:T(8,128)(2,1)}), bf16[128,8,384]{2,1,0:T(8,128)(2,1)S(1)}, u32[]{:S(2)}, u32[]{:S(2)}) %all-to-all-start) | async-done | bytes 786464 | tf_op jit(solution)/shard_map/all_to_all | solution.py:432
  32.4 0.8 shard_map.112.own
  33.2 0.4 collective-permute-start
  33.6 2.6 %slice_select_fusion = (bf16[320,1664]{1,0:T(8,128)(2,1)S(1)}, bf16[320,1664]{1,0:T(8,128)(2,1)S(1)}) fusion(bf16[320,3200]{1,0:T(8,128)(2,1)} %bitcast.8, pred[]{:T(512)S(6)} %eq.3, bf16[320,3200]{1,0:T(8,128)(2,1)} %param.14), kind=kLoop, calls=%fused_computation | loop fusion | flops 1064960 | bytes 6389761 | tf_op jit(solution)/shard_map/jit(_where)/select_n | solution.py:424
  36.1 0.3 copy-done.8
  36.4 0.1 slice_select_fusion.2.w0.refs_1_
  36.6 2.7 %shard_map.113 = (bf16[32,2688]{1,0:T(8,128)(2,1)S(1)}, bf16[96,2688]{1,0:T(8,128)(2,1)S(1)}, f32[128,2688]{1,0:T(8,128)S(1)}) custom-call(s32[4]{0:T(128)S(1)} %pad_add_fusion.index, bf16[8,64,384]{2,1,0:T(8,128)(2,1)S(1)} %shard_map.112.own, bf16[8,64,384]{2,1,0:T(8,128)(2,1)S(1)} %collective-permute-done.sib, ...), custom_call_target="tpu_custom_call" | custom-call | flops 880803840 | bytes 10485760 | tf_op jit(solution)/shard_map/pallas_call | solution.py:65
  39.3 0.6 collective-permute-start.9
  39.9 2.4 %shard_map.114 = (f32[64,2304]{1,0:T(8,128)S(1)}, bf16[64,2304]{1,0:T(8,128)(2,1)S(1)}, bf16[64,2304]{1,0:T(8,128)(2,1)S(1)}, bf16[64,2304]{1,0:T(8,128)(2,1)S(1)}) custom-call(s32[4]{0:T(128)S(1)} %pad_add_fusion.index, bf16[8,64,384]{2,1,0:T(8,128)(2,1)S(1)} %shard_map.112.own, bf16[8,64,384]{2,1,0:T(8,128)(2,1)S(1)} %collective-permute-done.sib, ...), custom_call_target="tpu_custom_call" | custom-call | flops 754974720 | bytes 10485760 | tf_op jit(solution)/shard_map/pallas_call | solution.py:65
  42.3 0.3 collective-permute-start.4
  42.6 1.8 %collective-permute-start.5 = (bf16[64,2304]{1,0:T(8,128)(2,1)S(1)}, bf16[64,2304]{1,0:T(8,128)(2,1)S(1)}, u32[]{:S(2)}, u32[]{:S(2)}) collective-permute-start(bf16[64,2304]{1,0:T(8,128)(2,1)S(1)} %get-tuple-element.82), channel_id=1, source_target_pairs={{0,8},{4,12},{8,0},{12,4},{1,9},{5,13},{9,1},{13,5},{2,10},{6,14},... | collective-permute-start | bytes 884744 | tf_op jit(solution)/shard_map/ppermute | solution.py:45
  44.3 1.2 collective-permute-start.6
  45.5 1.4 %collective-permute-start.8 = (bf16[32,2688]{1,0:T(8,128)(2,1)S(1)}, bf16[32,2688]{1,0:T(8,128)(2,1)S(1)}, u32[]{:S(2)}, u32[]{:S(2)}) collective-permute-start(bf16[32,2688]{1,0:T(8,128)(2,1)S(1)} %get-tuple-element.87), channel_id=1, source_target_pairs={{0,2},{2,0},{1,3},{3,1},{4,6},{6,4},{5,7},{7,5},{8,10},{10,8},{9,1... | collective-permute-start | bytes 516104 | tf_op jit(solution)/shard_map/ppermute | solution.py:57
  47.0 5.5 %collective-permute-done.9.far = bf16[96,2688]{1,0:T(8,128)(2,1)S(1)} collective-permute-done((bf16[96,2688]{1,0:T(8,128)(2,1)S(1)}, bf16[96,2688]{1,0:T(8,128)(2,1)S(1)}, u32[]{:S(2)}, u32[]{:S(2)}) %collective-permute-start.9) | collective-permute-done | bytes 516128 | tf_op jit(solution)/shard_map/ppermute | solution.py:57
  52.5 0.1 shard_map.116
  52.6 0.1 collective-permute-start.10
  52.7 2.7 %collective-permute-start.11 = (bf16[32,2688]{1,0:T(8,128)(2,1)S(1)}, bf16[32,2688]{1,0:T(8,128)(2,1)S(1)}, u32[]{:S(2)}, u32[]{:S(2)}) collective-permute-start(bf16[32,2688]{1,0:T(8,128)(2,1)S(1)} %get-tuple-element.90), channel_id=1, source_target_pairs={{0,8},{4,12},{8,0},{12,4},{1,9},{5,13},{9,1},{13,5},{2,10},{6,14},... | collective-permute-start | bytes 516104 | tf_op jit(solution)/shard_map/ppermute | solution.py:45
  55.4 2.4 %collective-permute-done.5.b = bf16[64,2304]{1,0:T(8,128)(2,1)S(1)} collective-permute-done((bf16[64,2304]{1,0:T(8,128)(2,1)S(1)}, bf16[64,2304]{1,0:T(8,128)(2,1)S(1)}, u32[]{:S(2)}, u32[]{:S(2)}) %collective-permute-start.5) | collective-permute-done | bytes 294944 | tf_op jit(solution)/shard_map/ppermute | solution.py:45
  57.8 1.2 collective-permute-done.6.c
  59.0 0.1 shard_map.115
  59.1 1.1 collective-permute-start.7
  60.2 3.3 %collective-permute-done.7.far_a = bf16[32,2304]{1,0:T(8,128)(2,1)S(1)} collective-permute-done((bf16[32,2304]{1,0:T(8,128)(2,1)S(1)}, bf16[32,2304]{1,0:T(8,128)(2,1)S(1)}, u32[]{:S(2)}, u32[]{:S(2)}) %collective-permute-start.7) | collective-permute-done | bytes 147488 | tf_op jit(solution)/shard_map/ppermute | solution.py:57
  63.5 0.4 collective-permute-done.10.right
  63.9 1.7 %collective-permute-done.12.left = bf16[32,2688]{1,0:T(8,128)(2,1)S(1)} collective-permute-done((bf16[32,2688]{1,0:T(8,128)(2,1)S(1)}, bf16[32,2688]{1,0:T(8,128)(2,1)S(1)}, u32[]{:S(2)}, u32[]{:S(2)}) %collective-permute-start.12) | collective-permute-done | bytes 172064 | tf_op jit(solution)/shard_map/ppermute | solution.py:45
  65.6 0.8 shard_map.117.refs_0_
  66.4 3.5 %collective-permute-start.15 = (bf16[32,4992]{1,0:T(8,128)(2,1)S(1)}, bf16[32,4992]{1,0:T(8,128)(2,1)S(1)}, u32[]{:S(2)}, u32[]{:S(2)}) collective-permute-start(bf16[32,4992]{1,0:T(8,128)(2,1)S(1)} %shard_map.117.refs_0_), channel_id=1, source_target_pairs={{0,12},{4,0},{8,4},{12,8},{1,13},{5,1},{9,5},{13,9},{2,14},{6,2},{... | collective-permute-start | bytes 958472 | tf_op jit(solution)/shard_map/ppermute | solution.py:45
  69.9 1.0 collective-permute-start.13
  70.8 5.3 %collective-permute-done.15.refs_2_ = bf16[32,4992]{1,0:T(8,128)(2,1)S(1)} collective-permute-done((bf16[32,4992]{1,0:T(8,128)(2,1)S(1)}, bf16[32,4992]{1,0:T(8,128)(2,1)S(1)}, u32[]{:S(2)}, u32[]{:S(2)}) %collective-permute-start.15) | collective-permute-done | bytes 319520 | tf_op jit(solution)/shard_map/ppermute | solution.py:45
  76.2 3.1 %collective-permute-done.14.refs_3_ = bf16[32,4992]{1,0:T(8,128)(2,1)S(1)} collective-permute-done((bf16[32,4992]{1,0:T(8,128)(2,1)S(1)}, bf16[32,4992]{1,0:T(8,128)(2,1)S(1)}, u32[]{:S(2)}, u32[]{:S(2)}) %collective-permute-start.14) | collective-permute-done | bytes 319520 | tf_op jit(solution)/shard_map/ppermute | solution.py:45
  79.3 1.0 collective-permute-start.17
  80.2 2.7 %collective-permute-start.16 = (bf16[32,4992]{1,0:T(8,128)(2,1)S(1)}, bf16[32,4992]{1,0:T(8,128)(2,1)S(1)}, u32[]{:S(2)}, u32[]{:S(2)}) collective-permute-start(bf16[32,4992]{1,0:T(8,128)(2,1)S(1)} %collective-permute-done.15.refs_2_), channel_id=1, source_target_pairs={{0,12},{4,0},{8,4},{12,8},{1,13},{5,1},{9,5},{13,9},{2,14},{6,2},{... | collective-permute-start | bytes 958472 | tf_op jit(solution)/shard_map/ppermute | solution.py:45
  82.9 0.9 shard_map.119.lines
  83.8 0.1 shard_map.118.refs_0_.early_in
  83.9 3.8 %collective-permute-done.18.refs_2_ = bf16[32,4992]{1,0:T(8,128)(2,1)S(1)} collective-permute-done((bf16[32,4992]{1,0:T(8,128)(2,1)S(1)}, bf16[32,4992]{1,0:T(8,128)(2,1)S(1)}, u32[]{:S(2)}, u32[]{:S(2)}) %collective-permute-start.18) | collective-permute-done | bytes 319520 | tf_op jit(solution)/shard_map/ppermute | solution.py:45
  87.7 1.0 collective-permute-start.19
  88.7 1.5 %shard_map.120 = (f32[128,320]{1,0:T(8,128)S(1)}, f32[128,320]{1,0:T(8,128)S(1)}) custom-call(bf16[128,4992]{1,0:T(8,128)(2,1)S(1)} %shard_map.118.refs_0_.early_in, bf16[320,1664]{1,0:T(8,128)(2,1)S(1)} %slice_select_fusion.2.w0.refs_1_, bf16[320,1664]{1,0:T(8,128)(2,1)S(1)} %collective-permute-done.1.w1.refs_2_, ...), custom_call_target="tpu_custom_call" | custom-call | flops 545259520 | bytes 6291456 | tf_op jit(solution)/shard_map/pallas_call | solution.py:65
  90.2 0.1 shard_map.121.refs_0_
  90.3 1.5 %shard_map.122 = (f32[96,320]{1,0:T(8,128)S(1)}, f32[96,320]{1,0:T(8,128)S(1)}) custom-call(bf16[96,4992]{1,0:T(8,128)(2,1)S(1)} %shard_map.121.refs_0_, bf16[320,1664]{1,0:T(8,128)(2,1)S(1)} %slice_select_fusion.2.w0.refs_1_, bf16[320,1664]{1,0:T(8,128)(2,1)S(1)} %collective-permute-done.1.w1.refs_2_, bf16[320,1664]{1,0:T(8,128)(2,1)S(1)} %get-tuple-element.123.w2.refs_3_, ...), custom_call_target="tpu_custom_call" | custom-call | flops 408944640 | bytes 6291456 | tf_op jit(solution)/shard_map/pallas_call | solution.py:65
  91.7 1.8 %collective-permute-done.19.refs_0_.refs_3_ = bf16[32,4992]{1,0:T(8,128)(2,1)S(1)} collective-permute-done((bf16[32,4992]{1,0:T(8,128)(2,1)S(1)}, bf16[32,4992]{1,0:T(8,128)(2,1)S(1)}, u32[]{:S(2)}, u32[]{:S(2)}) %collective-permute-start.19) | collective-permute-done | bytes 319520 | tf_op jit(solution)/shard_map/ppermute | solution.py:57
  93.6 1.3 %shard_map.123 = (f32[32,320]{1,0:T(8,128)S(1)}, f32[32,320]{1,0:T(8,128)S(1)}) custom-call(bf16[32,4992]{1,0:T(8,128)(2,1)S(1)} %collective-permute-done.19.refs_0_.refs_3_, bf16[320,1664]{1,0:T(8,128)(2,1)S(1)} %slice_select_fusion.2.w0.refs_1_, bf16[320,1664]{1,0:T(8,128)(2,1)S(1)} %collective-permute-done.1.w1.refs_2_, ...), custom_call_target="tpu_custom_call" | custom-call | flops 136314880 | bytes 6291456 | tf_op jit(solution)/shard_map/pallas_call | solution.py:65
  94.8 1.0 shard_map.124
  95.8 4.2 %collective-permute-start.20 = (bf16[512,320]{1,0:T(8,128)(2,1)S(1)}, bf16[512,320]{1,0:T(8,128)(2,1)S(1)}, u32[]{:S(2)}, u32[]{:S(2)}) collective-permute-start(bf16[512,320]{1,0:T(8,128)(2,1)S(1)} %shard_map.124), channel_id=1, source_target_pairs={{0,1},{1,0},{2,3},{3,2},{4,5},{5,4},{6,7},{7,6},{8,9},{9,8},{10,11... | collective-permute-start | bytes 983048 | tf_op jit(solution)/shard_map/ppermute | solution.py:61
  100.0 0.1 collective-permute-start.21
  100.1 0.1 shard_map.125.late_in
  100.2 1.0 shard_map.126.kept
  101.2 0.2 collective-permute-done.20.sent
  101.4 0.4 collective-permute-start.22
  101.7 0.8 shard_map.127
  102.6 6.6 %all-to-all-start.1 = ((bf16[64,8,320]{2,1,0:T(8,128)(2,1)}), bf16[64,8,320]{2,1,0:T(8,128)(2,1)S(1)}, u32[]{:S(2)}, u32[]{:S(2)}) async-start(bf16[64,8,320]{2,1,0:T(8,128)(2,1)} %bitcast.5), calls=%async_computation.1 | async-start | bytes 786432 | tf_op jit(solution)/shard_map/all_to_all | solution.py:482
  109.2 7.6 %shard_map.128 = (bf16[320,3200]{1,0:T(8,128)(2,1)}, bf16[320,3200]{1,0:T(8,128)(2,1)}, bf16[320,3200]{1,0:T(8,128)(2,1)}) custom-call(s32[4]{0:T(128)} %copy-done.3, bf16[8,64,384]{2,1,0:T(8,128)(2,1)} %copy-done, bf16[128,4992]{1,0:T(8,128)(2,1)} %copy-done.1, bf16[128,4992]{1,0:T(8,128)(2,1)} %copy-done.2, ...), custom_call_target="tpu_custom_call" | custom-call | flops 1572864000 | bytes 12582912 | tf_op jit(solution)/shard_map/pallas_call | solution.py:399
  116.7 3.6 %all-to-all-done.1.back = bf16[64,8,320]{2,1,0:T(8,128)(2,1)S(1)} async-done(((bf16[64,8,320]{2,1,0:T(8,128)(2,1)}), bf16[64,8,320]{2,1,0:T(8,128)(2,1)S(1)}, u32[]{:S(2)}, u32[]{:S(2)}) %all-to-all-start.1) | async-done | bytes 327712 | tf_op jit(solution)/shard_map/all_to_all | solution.py:482
  120.3 1.7 %shard_map.129 = bf16[128,5120]{1,0:T(8,128)(2,1)} custom-call(bf16[8,128]{1,0:T(8,128)(2,1)S(1)} %copy-done.4, bf16[64,8,320]{2,1,0:T(8,128)(2,1)S(1)} %all-to-all-done.1.back), custom_call_target="tpu_custom_call" | custom-call | tf_op jit(solution)/shard_map/pallas_call | solution.py:65
  (29 shorter events, 0.1 us)
Async XLA Ops:
  0.6 15.1 %copy-start.7 = (bf16[320,3200]{1,0:T(8,128)(2,1)S(1)}, bf16[320,3200]{1,0:T(8,128)(2,1)}, u32[]{:S(2)}) copy-start(bf16[320,3200]{1,0:T(8,128)(2,1)} %param.13) | copy-start | bytes 6144004
  4.2 28.1 %all-to-all-start = ((bf16[128,8,384]{2,1,0:T(8,128)(2,1)}), bf16[128,8,384]{2,1,0:T(8,128)(2,1)S(1)}, u32[]{:S(2)}, u32[]{:S(2)}) async-start(bf16[128,8,384]{2,1,0:T(8,128)(2,1)} %get-tuple-element.65), calls=%async_computation | async-start | bytes 1572864 | tf_op jit(solution)/shard_map/all_to_all | solution.py:432
  15.8 2.0 %copy-start.6 = (bf16[320,3200]{1,0:T(8,128)(2,1)S(1)}, bf16[320,3200]{1,0:T(8,128)(2,1)}, u32[]{:S(2)}) copy-start(bf16[320,3200]{1,0:T(8,128)(2,1)} %param.14) | copy-start | bytes 6144004
  17.7 2.0 %copy-start.5 = (bf16[3200,320]{0,1:T(8,128)(2,1)S(1)}, bf16[3200,320]{0,1:T(8,128)(2,1)}, u32[]{:S(2)}) copy-start(bf16[3200,320]{0,1:T(8,128)(2,1)} %param.15) | copy-start | bytes 6144004
  20.8 15.8 %collective-permute-start.3 = (bf16[320,1664]{1,0:T(8,128)(2,1)}, bf16[320,1664]{1,0:T(8,128)(2,1)}, u32[]{:S(2)}, u32[]{:S(2)}) collective-permute-start(bf16[320,1664]{1,0:T(8,128)(2,1)} %slice_select_fusion.3), channel_id=1, source_target_pairs={{0,1},{1,0},{2,3},{3,2},{4,5},{5,4},{6,7},{7,6},{8,9},{9,8},{10,11... | collective-permute-start | bytes 3194888 | tf_op jit(solution)/shard_map/ppermute | solution.py:61
  21.9 14.7 %collective-permute-start.2 = (bf16[320,1664]{1,0:T(8,128)(2,1)}, bf16[320,1664]{1,0:T(8,128)(2,1)S(1)}, u32[]{:S(2)}, u32[]{:S(2)}) collective-permute-start(bf16[320,1664]{1,0:T(8,128)(2,1)} %slice_select_fusion.4), channel_id=1, source_target_pairs={{0,1},{1,0},{2,3},{3,2},{4,5},{5,4},{6,7},{7,6},{8,9},{9,8},{10,11... | collective-permute-start | bytes 3194888 | tf_op jit(solution)/shard_map/ppermute | solution.py:61
  21.9 14.7 %collective-permute-start.1 = (bf16[320,1664]{1,0:T(8,128)(2,1)}, bf16[320,1664]{1,0:T(8,128)(2,1)S(1)}, u32[]{:S(2)}, u32[]{:S(2)}) collective-permute-start(bf16[320,1664]{1,0:T(8,128)(2,1)} %slice_select_fusion.5), channel_id=1, source_target_pairs={{0,1},{1,0},{2,3},{3,2},{4,5},{5,4},{6,7},{7,6},{8,9},{9,8},{10,11... | collective-permute-start | bytes 3194888 | tf_op jit(solution)/shard_map/ppermute | solution.py:61
  22.5 77.8 %copy-start.3 = (s32[4]{0:T(128)}, s32[4]{0:T(128)S(1)}, u32[]{:S(2)}) copy-start(s32[4]{0:T(128)S(1)} %pad_add_fusion.index) | copy-start | bytes 52
  33.2 49.7 %copy-start = (bf16[8,64,384]{2,1,0:T(8,128)(2,1)}, bf16[8,64,384]{2,1,0:T(8,128)(2,1)S(1)}, u32[]{:S(2)}) copy-start(bf16[8,64,384]{2,1,0:T(8,128)(2,1)S(1)} %shard_map.112.own) | copy-start | bytes 1179652
  33.2 3.4 %collective-permute-start = (bf16[8,64,384]{2,1,0:T(8,128)(2,1)S(1)}, bf16[8,64,384]{2,1,0:T(8,128)(2,1)S(1)}, u32[]{:S(2)}, u32[]{:S(2)}) collective-permute-start(bf16[8,64,384]{2,1,0:T(8,128)(2,1)S(1)} %shard_map.112.own), channel_id=1, source_target_pairs={{0,1},{1,0},{2,3},{3,2},{4,5},{5,4},{6,7},{7,6},{8,9},{9,8},{10,11... | collective-permute-start | bytes 1179656 | tf_op jit(solution)/shard_map/ppermute | solution.py:61
  33.6 2.9 %copy-start.8 = (bf16[320,3200]{1,0:T(8,128)(2,1)S(1)}, bf16[320,3200]{1,0:T(8,128)(2,1)}, u32[]{:S(2)}) copy-start(bf16[320,3200]{1,0:T(8,128)(2,1)} %param.13) | copy-start | bytes 6144004
  39.3 13.2 %collective-permute-start.9 = (bf16[96,2688]{1,0:T(8,128)(2,1)S(1)}, bf16[96,2688]{1,0:T(8,128)(2,1)S(1)}, u32[]{:S(2)}, u32[]{:S(2)}) collective-permute-start(bf16[96,2688]{1,0:T(8,128)(2,1)S(1)} %get-tuple-element.88), channel_id=1, source_target_pairs={{0,2},{2,0},{1,3},{3,1},{4,6},{6,4},{5,7},{7,5},{8,10},{10,8},{9,1... | collective-permute-start | bytes 1548296 | tf_op jit(solution)/shard_map/ppermute | solution.py:57
  42.3 10.4 %collective-permute-start.4 = (bf16[64,2304]{1,0:T(8,128)(2,1)S(1)}, bf16[64,2304]{1,0:T(8,128)(2,1)S(1)}, u32[]{:S(2)}, u32[]{:S(2)}) collective-permute-start(bf16[64,2304]{1,0:T(8,128)(2,1)S(1)} %get-tuple-element.81), channel_id=1, source_target_pairs={{0,4},{4,8},{8,12},{12,0},{1,5},{5,9},{9,13},{13,1},{2,6},{6,10},{... | collective-permute-start | bytes 884744 | tf_op jit(solution)/shard_map/ppermute | solution.py:45
  42.6 15.2 %collective-permute-start.5 = (bf16[64,2304]{1,0:T(8,128)(2,1)S(1)}, bf16[64,2304]{1,0:T(8,128)(2,1)S(1)}, u32[]{:S(2)}, u32[]{:S(2)}) collective-permute-start(bf16[64,2304]{1,0:T(8,128)(2,1)S(1)} %get-tuple-element.82), channel_id=1, source_target_pairs={{0,8},{4,12},{8,0},{12,4},{1,9},{5,13},{9,1},{13,5},{2,10},{6,14},... | collective-permute-start | bytes 884744 | tf_op jit(solution)/shard_map/ppermute | solution.py:45
  44.3 14.6 %collective-permute-start.6 = (bf16[64,2304]{1,0:T(8,128)(2,1)S(1)}, bf16[64,2304]{1,0:T(8,128)(2,1)S(1)}, u32[]{:S(2)}, u32[]{:S(2)}) collective-permute-start(bf16[64,2304]{1,0:T(8,128)(2,1)S(1)} %get-tuple-element.83), channel_id=1, source_target_pairs={{0,12},{4,0},{8,4},{12,8},{1,13},{5,1},{9,5},{13,9},{2,14},{6,2},{... | collective-permute-start | bytes 884744 | tf_op jit(solution)/shard_map/ppermute | solution.py:45
  45.5 14.6 %collective-permute-start.8 = (bf16[32,2688]{1,0:T(8,128)(2,1)S(1)}, bf16[32,2688]{1,0:T(8,128)(2,1)S(1)}, u32[]{:S(2)}, u32[]{:S(2)}) collective-permute-start(bf16[32,2688]{1,0:T(8,128)(2,1)S(1)} %get-tuple-element.87), channel_id=1, source_target_pairs={{0,2},{2,0},{1,3},{3,1},{4,6},{6,4},{5,7},{7,5},{8,10},{10,8},{9,1... | collective-permute-start | bytes 516104 | tf_op jit(solution)/shard_map/ppermute | solution.py:57
  52.6 11.3 %collective-permute-start.10 = (bf16[32,2688]{1,0:T(8,128)(2,1)S(1)}, bf16[32,2688]{1,0:T(8,128)(2,1)S(1)}, u32[]{:S(2)}, u32[]{:S(2)}) collective-permute-start(bf16[32,2688]{1,0:T(8,128)(2,1)S(1)} %get-tuple-element.89), channel_id=1, source_target_pairs={{0,4},{4,8},{8,12},{12,0},{1,5},{5,9},{9,13},{13,1},{2,6},{6,10},{... | collective-permute-start | bytes 516104 | tf_op jit(solution)/shard_map/ppermute | solution.py:45
  52.7 11.2 %collective-permute-start.11 = (bf16[32,2688]{1,0:T(8,128)(2,1)S(1)}, bf16[32,2688]{1,0:T(8,128)(2,1)S(1)}, u32[]{:S(2)}, u32[]{:S(2)}) collective-permute-start(bf16[32,2688]{1,0:T(8,128)(2,1)S(1)} %get-tuple-element.90), channel_id=1, source_target_pairs={{0,8},{4,12},{8,0},{12,4},{1,9},{5,13},{9,1},{13,5},{2,10},{6,14},... | collective-permute-start | bytes 516104 | tf_op jit(solution)/shard_map/ppermute | solution.py:45
  57.8 7.8 %collective-permute-start.12 = (bf16[32,2688]{1,0:T(8,128)(2,1)S(1)}, bf16[32,2688]{1,0:T(8,128)(2,1)S(1)}, u32[]{:S(2)}, u32[]{:S(2)}) collective-permute-start(bf16[32,2688]{1,0:T(8,128)(2,1)S(1)} %get-tuple-element.91), channel_id=1, source_target_pairs={{0,12},{4,0},{8,4},{12,8},{1,13},{5,1},{9,5},{13,9},{2,14},{6,2},{... | collective-permute-start | bytes 516104 | tf_op jit(solution)/shard_map/ppermute | solution.py:45
  59.1 4.4 %collective-permute-start.7 = (bf16[32,2304]{1,0:T(8,128)(2,1)S(1)}, bf16[32,2304]{1,0:T(8,128)(2,1)S(1)}, u32[]{:S(2)}, u32[]{:S(2)}) collective-permute-start(bf16[32,2304]{1,0:T(8,128)(2,1)S(1)} %get-tuple-element.85), channel_id=1, source_target_pairs={{0,2},{2,0},{1,3},{3,1},{4,6},{6,4},{5,7},{7,5},{8,10},{10,8},{9,1... | collective-permute-start | bytes 442376 | tf_op jit(solution)/shard_map/ppermute | solution.py:57
  66.4 9.8 %collective-permute-start.15 = (bf16[32,4992]{1,0:T(8,128)(2,1)S(1)}, bf16[32,4992]{1,0:T(8,128)(2,1)S(1)}, u32[]{:S(2)}, u32[]{:S(2)}) collective-permute-start(bf16[32,4992]{1,0:T(8,128)(2,1)S(1)} %shard_map.117.refs_0_), channel_id=1, source_target_pairs={{0,12},{4,0},{8,4},{12,8},{1,13},{5,1},{9,5},{13,9},{2,14},{6,2},{... | collective-permute-start | bytes 958472 | tf_op jit(solution)/shard_map/ppermute | solution.py:45
  69.9 9.4 %collective-permute-start.14 = (bf16[32,4992]{1,0:T(8,128)(2,1)S(1)}, bf16[32,4992]{1,0:T(8,128)(2,1)S(1)}, u32[]{:S(2)}, u32[]{:S(2)}) collective-permute-start(bf16[32,4992]{1,0:T(8,128)(2,1)S(1)} %shard_map.117.refs_0_), channel_id=1, source_target_pairs={{0,4},{4,8},{8,12},{12,0},{1,5},{5,9},{9,13},{13,1},{2,6},{6,10},{... | collective-permute-start | bytes 958472 | tf_op jit(solution)/shard_map/ppermute | solution.py:45
  69.9 9.4 %collective-permute-start.13 = (bf16[32,4992]{1,0:T(8,128)(2,1)S(1)}, bf16[32,4992]{1,0:T(8,128)(2,1)S(1)}, u32[]{:S(2)}, u32[]{:S(2)}) collective-permute-start(bf16[32,4992]{1,0:T(8,128)(2,1)S(1)} %shard_map.117.refs_0_), channel_id=1, source_target_pairs={{0,2},{2,0},{1,3},{3,1},{4,6},{6,4},{5,7},{7,5},{8,10},{10,8},{9,1... | collective-permute-start | bytes 958472 | tf_op jit(solution)/shard_map/ppermute | solution.py:57
  79.3 8.5 %collective-permute-start.18 = (bf16[32,4992]{1,0:T(8,128)(2,1)S(1)}, bf16[32,4992]{1,0:T(8,128)(2,1)S(1)}, u32[]{:S(2)}, u32[]{:S(2)}) collective-permute-start(bf16[32,4992]{1,0:T(8,128)(2,1)S(1)} %collective-permute-done.13.refs_1_), channel_id=1, source_target_pairs={{0,4},{4,8},{8,12},{12,0},{1,5},{5,9},{9,13},{13,1},{2,6},{6,10},{... | collective-permute-start | bytes 958472 | tf_op jit(solution)/shard_map/ppermute | solution.py:45
  79.3 8.5 %collective-permute-start.17 = (bf16[32,4992]{1,0:T(8,128)(2,1)S(1)}, bf16[32,4992]{1,0:T(8,128)(2,1)S(1)}, u32[]{:S(2)}, u32[]{:S(2)}) collective-permute-start(bf16[32,4992]{1,0:T(8,128)(2,1)S(1)} %collective-permute-done.15.refs_2_), channel_id=1, source_target_pairs={{0,2},{2,0},{1,3},{3,1},{4,6},{6,4},{5,7},{7,5},{8,10},{10,8},{9,1... | collective-permute-start | bytes 958472 | tf_op jit(solution)/shard_map/ppermute | solution.py:57
  80.2 7.5 %collective-permute-start.16 = (bf16[32,4992]{1,0:T(8,128)(2,1)S(1)}, bf16[32,4992]{1,0:T(8,128)(2,1)S(1)}, u32[]{:S(2)}, u32[]{:S(2)}) collective-permute-start(bf16[32,4992]{1,0:T(8,128)(2,1)S(1)} %collective-permute-done.15.refs_2_), channel_id=1, source_target_pairs={{0,12},{4,0},{8,4},{12,8},{1,13},{5,1},{9,5},{13,9},{2,14},{6,2},{... | collective-permute-start | bytes 958472 | tf_op jit(solution)/shard_map/ppermute | solution.py:45
  83.9 16.1 %copy-start.1 = (bf16[128,4992]{1,0:T(8,128)(2,1)}, bf16[128,4992]{1,0:T(8,128)(2,1)S(1)}, u32[]{:S(2)}) copy-start(bf16[128,4992]{1,0:T(8,128)(2,1)S(1)} %shard_map.118.refs_0_.early_in) | copy-start | bytes 3833860
  87.7 5.8 %collective-permute-start.19 = (bf16[32,4992]{1,0:T(8,128)(2,1)S(1)}, bf16[32,4992]{1,0:T(8,128)(2,1)S(1)}, u32[]{:S(2)}, u32[]{:S(2)}) collective-permute-start(bf16[32,4992]{1,0:T(8,128)(2,1)S(1)} %collective-permute-done.16.refs_0_), channel_id=1, source_target_pairs={{0,2},{2,0},{1,3},{3,1},{4,6},{6,4},{5,7},{7,5},{8,10},{10,8},{9,1... | collective-permute-start | bytes 958472 | tf_op jit(solution)/shard_map/ppermute | solution.py:57
  95.8 5.5 %collective-permute-start.20 = (bf16[512,320]{1,0:T(8,128)(2,1)S(1)}, bf16[512,320]{1,0:T(8,128)(2,1)S(1)}, u32[]{:S(2)}, u32[]{:S(2)}) collective-permute-start(bf16[512,320]{1,0:T(8,128)(2,1)S(1)} %shard_map.124), channel_id=1, source_target_pairs={{0,1},{1,0},{2,3},{3,2},{4,5},{5,4},{6,7},{7,6},{8,9},{9,8},{10,11... | collective-permute-start | bytes 983048 | tf_op jit(solution)/shard_map/ppermute | solution.py:61
  100.0 9.1 %collective-permute-start.21 = (bf16[128,4992]{1,0:T(8,128)(2,1)S(1)}, bf16[128,4992]{1,0:T(8,128)(2,1)}, u32[]{:S(2)}, u32[]{:S(2)}) collective-permute-start(bf16[128,4992]{1,0:T(8,128)(2,1)S(1)} %shard_map.118.refs_0_.early_in), channel_id=1, source_target_pairs={{0,1},{1,0},{2,3},{3,2},{4,5},{5,4},{6,7},{7,6},{8,9},{9,8},{10,11... | collective-permute-start | bytes 3833864 | tf_op jit(solution)/shard_map/ppermute | solution.py:61
  100.2 2.3 %copy-start.2 = (bf16[128,4992]{1,0:T(8,128)(2,1)}, bf16[128,4992]{1,0:T(8,128)(2,1)S(1)}, u32[]{:S(2)}) copy-start(bf16[128,4992]{1,0:T(8,128)(2,1)S(1)} %shard_map.125.late_in) | copy-start | bytes 3833860
  101.4 7.8 %collective-permute-start.22 = (bf16[128,4992]{1,0:T(8,128)(2,1)S(1)}, bf16[128,4992]{1,0:T(8,128)(2,1)}, u32[]{:S(2)}, u32[]{:S(2)}) collective-permute-start(bf16[128,4992]{1,0:T(8,128)(2,1)S(1)} %shard_map.125.late_in), channel_id=1, source_target_pairs={{0,1},{1,0},{2,3},{3,2},{4,5},{5,4},{6,7},{7,6},{8,9},{9,8},{10,11... | collective-permute-start | bytes 3833864 | tf_op jit(solution)/shard_map/ppermute | solution.py:61
  102.6 17.8 %all-to-all-start.1 = ((bf16[64,8,320]{2,1,0:T(8,128)(2,1)}), bf16[64,8,320]{2,1,0:T(8,128)(2,1)S(1)}, u32[]{:S(2)}, u32[]{:S(2)}) async-start(bf16[64,8,320]{2,1,0:T(8,128)(2,1)} %bitcast.5), calls=%async_computation.1 | async-start | bytes 786432 | tf_op jit(solution)/shard_map/all_to_all | solution.py:482
  109.1 11.2 %copy-start.4 = (bf16[8,128]{1,0:T(8,128)(2,1)S(1)}, bf16[8,128]{1,0:T(8,128)(2,1)}, u32[]{:S(2)}) copy-start(bf16[8,128]{1,0:T(8,128)(2,1)} %get-tuple-element.63.owner) | copy-start | bytes 6148

commit v5 on v4

--- a/solution.py
+++ b/solution.py
@@ -9,6 +9,7 @@
 SIZES = (4, 2, 4, 2, 2)
 N_DP, N_FSDP, N_DEV = 8, 16, 128
 CAP = 4
+PART = 2560
 GROUP = 32
 LIVE = N_DP * GROUP
 ROWS = 128
@@ -259,7 +260,7 @@
     return hidden, gate_delta, up_delta
 
 
-def value_kernel(index, mine_a, far_a, near, far0, right, two, left, out):
+def value_kernel(index, mine_a, far_a, near, far0, right, two, left, out, piece, rest):
     sums_a = mine_a[...] + far_a[...].astype(F32)
     sums_b = near[0:GROUP] + far0[...].astype(F32) + right[...].astype(F32) + two[...].astype(F32) + left[...].astype(F32)
     of_a = swiglu_backward(*[sums_a[:, k * NA : (k + 1) * NA] for k in range(3)])
@@ -269,15 +270,20 @@
     for k in range(3):
         out[:, k * WIN : k * WIN + NA] = jnp.where(keep, of_a[k], 0.0).astype(BF)
         out[:, k * WIN + NA : (k + 1) * WIN] = of_b[k].astype(BF)
+    piece[...] = out[:, :PART]
+    rest[...] = out[:, PART:]
 
 
 def lay_kernel(*refs):
-    for k, block in enumerate(refs[:-1]):
-        refs[-1][k * GROUP : (k + 1) * GROUP, :] = block[...]
+    row = col = 0
+    for block in refs[:-1]:
+        width = block.shape[1]
+        refs[-1][row * GROUP : (row + 1) * GROUP, col : col + width] = block[...]
+        row, col = (row + 1, 0) if col + width == 3 * WIN else (row, width)
 
 
 def laid(blocks):
-    rows = len(blocks) * GROUP
+    rows = sum(block.shape[1] for block in blocks) // (3 * WIN) * GROUP
     return call(lay_kernel, [((rows, 3 * WIN), BF)], blocks, estimate=cost(0, 4 * 2**20))[0]
 
 
@@ -313,19 +319,27 @@
     out[...] = jnp.transpose(lines)[0:8, :].astype(jnp.int32)
 
 
-def unpack(index, core, lines, parts):
+def unpack(index, core, lines, parts, start=0):
     c = index[3]
     line = jnp.where(core == 0, lines[0:1, :], lines[1:2, :])
     mine = jnp.concatenate([part[...] for part in parts[0::2]])
     other = jnp.concatenate([part[...] for part in parts[1::2]])
-    at = lax.broadcasted_iota(jnp.int32, (CAP * N_DEV, LIVE), 0)
+    rows = mine.shape[0]
+    line = line[:, start : start + rows]
+    at = lax.broadcasted_iota(jnp.int32, (CAP * N_DEV, rows), 0)
     low = jnp.where(at == jnp.where(c == 0, line, line + CAP), 1.0, 0.0).astype(BF)
     high = jnp.where(at == jnp.where(c == 0, line + CAP, line), 1.0, 0.0).astype(BF)
     return dot(low, mine.astype(BF), 1, 0) + dot(high, other.astype(BF), 1, 0)
 
 
-def unpack_send_kernel(index, lines, *refs):
-    refs[-1][...] = unpack(index, 1 - index[3], lines, refs[:-1]).astype(BF)
+def unpack_early_kernel(index, lines, *refs):
+    refs[-1][...] = unpack(index, 1 - index[3], lines, refs[:-1])
+
+
+def unpack_last_kernel(index, lines, sent, value, go, gs, uo, us, mine, other, out):
+    back_kernel(value, go, gs, uo, us, mine, other)
+    last = unpack(index, 1 - index[3], lines, (mine, other), LIVE - GROUP)
+    out[...] = (sent[...] + last).astype(BF)
 
 
 def unpack_keep_kernel(index, lines, *refs):
@@ -450,31 +464,43 @@
     here_a, far_a = call(sum_a_kernel, [(shape_a, F32), (shape_a, BF)], [here_a, right, two, left])
     far_a = across(far_a)
     right_b, left_b, two_b = up(right_b), down(left_b), along(two_b, 2)
-    v00 = call(
+    v00, *p00 = call(
         value_kernel,
-        [((GROUP, 3 * WIN), BF)],
+        [((GROUP, 3 * WIN), BF), ((GROUP, PART), BF), ((GROUP, 3 * WIN - PART), BF)],
         [index, here_a, far_a, near, far0, right_b, two_b, left_b],
         smem=1,
-    )[0]
-
-    v01, v30, v10 = lax.optimization_barrier((across(v00), up(v00), down(v00)))
-    early = laid([v00, v01, v10, v30])
+    )
+
+    v10 = [down(p) for p in p00]
+    v01, v30 = across(v00), up(v00)
+    v10[0], v30 = lax.optimization_barrier((v10[0], v30))
+    v10[1], v01 = lax.optimization_barrier((v10[1], v01))
+    v20 = [down(p) for p in v10]
+    v11 = [across(p) for p in v10]
+    v31 = up(v01)
+    early = laid([v00, v01, *v10, v30])
     backs = back_products(early, weights[:4])
     lines = call(line_kernel, [((8, LIVE), jnp.int32)], [index, own], smem=1)[0]
-    v20, v11, v31, early, lines = lax.optimization_barrier(
-        (down(v10), across(v10), up(v01), early, lines)
-    )
-    v21 = across(v20)
-    backs += back_products(laid([v20, v11, v31]), weights[:4])
-    v21, *backs = lax.optimization_barrier((v21, *backs))
-    backs += back_products(v21, weights[:4])
+    v20[1], v31, early, lines = lax.optimization_barrier((v20[1], v31, early, lines))
+    v21 = [across(p) for p in v20]
+    backs += back_products(laid([*v20, *v11, v31]), weights[:4])
+    shape, price = (CAP * N_DEV, DL), cost(2 * CAP * N_DEV * LIVE * DL, 2**20)
+    sent = call(unpack_early_kernel, [(shape, F32)], [index, lines, *backs], smem=1, estimate=price)[0]
+    v21[0], v21[1], sent, *backs = lax.optimization_barrier((*v21, sent, *backs))
+    last = laid(v21)
+    mine, other, sent = call(
+        unpack_last_kernel,
+        [((GROUP, DL), F32)] * 2 + [(shape, BF)],
+        [index, lines, sent, last, *weights[:4]],
+        smem=1,
+        estimate=price,
+    )
+    backs += [mine, other]
     early_other = sibling(early)
 
     backs = [index, lines, *backs]
-    shape, price = (CAP * N_DEV, DL), cost(2 * CAP * N_DEV * LIVE * DL, 2**20)
-    sent = call(unpack_send_kernel, [(shape, BF)], backs, smem=1, estimate=price)[0]
-    v20, v21, sent = lax.optimization_barrier((v20, v21, sent))
-    late = laid([v20, v11, v31, v21])
+    last, sent = lax.optimization_barrier((last, sent))
+    late = laid([*v20, *v11, v31, last])
     kept = call(unpack_keep_kernel, [(shape, F32)], backs, smem=1, estimate=price)[0]
     sent, late, kept = lax.optimization_barrier((sibling(sent), late, kept))
     late_other = sibling(late)

time: 123 us -> 120 us (0.976)
  waiting for transfers between devices: 42.4 us -> 36.7 us
  starting transfers between devices: 42.8 us -> 45.1 us
    ppermute x10 -> x12, waiting for transfers between devices: 18 us -> 10.2 us  [along(): return lax.ppermute(t, 'x', [(i, (i + step) % 4) for i in range(4)])]
    ppermute x10 -> x12, starting transfers between devices: 12.2 us -> 15.4 us  [along(): return lax.ppermute(t, 'x', [(i, (i + step) % 4) for i in range(4)])]
    all_to_all x1, starting transfers between devices: 6.56 us -> 4.63 us  [shards(): lax.all_to_all(back.reshape(N_DEV // 2, 2 * CAP, DL), AXES[:4], 0, 0, til...]
    ppermute x6 -> x8, waiting for transfers between devices: 10.7 us -> 12.5 us  [across(): return lax.ppermute(t, 'zl', SWAP)]
    ppermute x6 -> x8, starting transfers between devices: 5.97 us -> 7.52 us  [across(): return lax.ppermute(t, 'zl', SWAP)]
    pallas_call x17 -> x18, Pallas kernels: 16.8 us -> 17.9 us  [call(): pl.pallas_call(kernel, out_shape=[jax.ShapeDtypeStruct(s, k) for s, k in...]
  transfers between devices with their start and end apart: 25 -> 29, of which waited for: 13 -> 15; matrix products, arithmetic and copies ran while one was open for 5% -> 5% of each run, Pallas kernels for 14% -> 15%
where the time goes in v5:
time: 120 us
  starting transfers between devices  45.1 us (38%)
  waiting for transfers between devices  36.7 us (31%)
  Pallas kernels  29.1 us (24%)
  other arithmetic  6.06 us (5%)
  local copies, waits for them, and re-layouts  2.03 us (2%)
    pallas_call x18, Pallas kernels, call(): pl.pallas_call(kernel, out_shape=[jax.ShapeDtypeStruct(s, k) for s, k in...  17.9 us
    ppermute x12, starting transfers between devices, along(): return lax.ppermute(t, 'x', [(i, (i + step) % 4) for i in range(4)])  15.4 us
    ppermute x8, waiting for transfers between devices, across(): return lax.ppermute(t, 'zl', SWAP)  12.5 us
    all_to_all x1, starting transfers between devices, shards(): got = lax.all_to_all(message, AXES, 0, 0, tiled=True)  11.5 us
    ppermute x12, waiting for transfers between devices, along(): return lax.ppermute(t, 'x', [(i, (i + step) % 4) for i in range(4)])  10.2 us
    all_to_all x1, waiting for transfers between devices, shards(): got = lax.all_to_all(message, AXES, 0, 0, tiled=True)  9.94 us
    pallas_call x1, Pallas kernels, weight_grads(): pl.pallas_call(grad_kernel, out_shape=[jax.ShapeDtypeStruct((DL, FL), BF)...  7.55 us
    ppermute x8, starting transfers between devices, across(): return lax.ppermute(t, 'zl', SWAP)  7.52 us
  transfers between devices with their start and end apart: 29, of which 15 were waited for; matrix products, arithmetic and copies ran while one was open for 5% of the time, Pallas kernels for 15%

profile of v5, /device:TPU:1, one launch (start us, length us, event | category | flops | bytes accessed | tf_op | source)
XLA Modules:
  0.0 119.9 jit_solution(15287196745211808580)
XLA Ops:
  0.6 3.6 %shard_map.111 = (bf16[128,8,384]{2,1,0:T(8,128)(2,1)}, bf16[8,128]{1,0:T(8,128)(2,1)}) custom-call(s32[1,1,4]{2,1,0:T(1,128)} %chosen_in.1, s32[1,16]{1,0:T(1,128)} %counts_in.1, f32[128]{0:T(128)} %advantage_in.1, bf16[128,5120]{1,0:T(8,128)(2,1)} %tokens.1, bf16[128,5120]{1,0:T(8,128)(2,1)} %cotangent.1), custom_call_target="tpu_custom_call" | custom-call | tf_op jit(solution)/shard_map/pallas_call | solution.py:143
  4.2 11.5 %all-to-all-start = ((bf16[128,8,384]{2,1,0:T(8,128)(2,1)}), bf16[128,8,384]{2,1,0:T(8,128)(2,1)S(1)}, u32[]{:S(2)}, u32[]{:S(2)}) async-start(bf16[128,8,384]{2,1,0:T(8,128)(2,1)} %get-tuple-element.70), calls=%async_computation | async-start | bytes 1572864 | tf_op jit(solution)/shard_map/all_to_all | solution.py:446
  15.8 1.1 slice_select_fusion.5
  16.9 0.8 copy-done.6
  17.7 1.1 slice_select_fusion.4
  18.8 0.9 copy-done.5
  19.7 1.1 slice_select_fusion.3
  20.8 1.1 collective-permute-start.3
  21.9 0.5 collective-permute-start.1
  22.5 9.9 %all-to-all-done = bf16[128,8,384]{2,1,0:T(8,128)(2,1)S(1)} async-done(((bf16[128,8,384]{2,1,0:T(8,128)(2,1)}), bf16[128,8,384]{2,1,0:T(8,128)(2,1)S(1)}, u32[]{:S(2)}, u32[]{:S(2)}) %all-to-all-start) | async-done | bytes 786464 | tf_op jit(solution)/shard_map/all_to_all | solution.py:446
  32.4 0.8 shard_map.112.own
  33.2 0.4 collective-permute-start
  33.6 2.6 %slice_select_fusion = (bf16[320,1664]{1,0:T(8,128)(2,1)S(1)}, bf16[320,1664]{1,0:T(8,128)(2,1)S(1)}) fusion(bf16[320,3200]{1,0:T(8,128)(2,1)} %bitcast.8, pred[]{:T(512)S(6)} %eq.3, bf16[320,3200]{1,0:T(8,128)(2,1)} %param.14), kind=kLoop, calls=%fused_computation | loop fusion | flops 1064960 | bytes 6389761 | tf_op jit(solution)/shard_map/jit(_where)/select_n | solution.py:438
  36.1 0.3 copy-done.8
  36.4 0.1 slice_select_fusion.2.w0.refs_1_.go
  36.6 2.7 %shard_map.113 = (bf16[32,2688]{1,0:T(8,128)(2,1)S(1)}, bf16[96,2688]{1,0:T(8,128)(2,1)S(1)}, f32[128,2688]{1,0:T(8,128)S(1)}) custom-call(s32[4]{0:T(128)S(1)} %pad_add_fusion.index, bf16[8,64,384]{2,1,0:T(8,128)(2,1)S(1)} %shard_map.112.own, bf16[8,64,384]{2,1,0:T(8,128)(2,1)S(1)} %collective-permute-done.sib, ...), custom_call_target="tpu_custom_call" | custom-call | flops 880803840 | bytes 10485760 | tf_op jit(solution)/shard_map/pallas_call | solution.py:66
  39.3 0.6 collective-permute-start.9
  39.9 2.4 %shard_map.114 = (f32[64,2304]{1,0:T(8,128)S(1)}, bf16[64,2304]{1,0:T(8,128)(2,1)S(1)}, bf16[64,2304]{1,0:T(8,128)(2,1)S(1)}, bf16[64,2304]{1,0:T(8,128)(2,1)S(1)}) custom-call(s32[4]{0:T(128)S(1)} %pad_add_fusion.index, bf16[8,64,384]{2,1,0:T(8,128)(2,1)S(1)} %shard_map.112.own, bf16[8,64,384]{2,1,0:T(8,128)(2,1)S(1)} %collective-permute-done.sib, ...), custom_call_target="tpu_custom_call" | custom-call | flops 754974720 | bytes 10485760 | tf_op jit(solution)/shard_map/pallas_call | solution.py:66
  42.3 0.3 collective-permute-start.4
  42.6 1.8 %collective-permute-start.5 = (bf16[64,2304]{1,0:T(8,128)(2,1)S(1)}, bf16[64,2304]{1,0:T(8,128)(2,1)S(1)}, u32[]{:S(2)}, u32[]{:S(2)}) collective-permute-start(bf16[64,2304]{1,0:T(8,128)(2,1)S(1)} %get-tuple-element.87), channel_id=1, source_target_pairs={{0,8},{4,12},{8,0},{12,4},{1,9},{5,13},{9,1},{13,5},{2,10},{6,14},... | collective-permute-start | bytes 884744 | tf_op jit(solution)/shard_map/ppermute | solution.py:46
  44.3 1.2 collective-permute-start.6
  45.5 1.4 %collective-permute-start.8 = (bf16[32,2688]{1,0:T(8,128)(2,1)S(1)}, bf16[32,2688]{1,0:T(8,128)(2,1)S(1)}, u32[]{:S(2)}, u32[]{:S(2)}) collective-permute-start(bf16[32,2688]{1,0:T(8,128)(2,1)S(1)} %get-tuple-element.92), channel_id=1, source_target_pairs={{0,2},{2,0},{1,3},{3,1},{4,6},{6,4},{5,7},{7,5},{8,10},{10,8},{9,1... | collective-permute-start | bytes 516104 | tf_op jit(solution)/shard_map/ppermute | solution.py:58
  47.0 5.5 %collective-permute-done.9.far = bf16[96,2688]{1,0:T(8,128)(2,1)S(1)} collective-permute-done((bf16[96,2688]{1,0:T(8,128)(2,1)S(1)}, bf16[96,2688]{1,0:T(8,128)(2,1)S(1)}, u32[]{:S(2)}, u32[]{:S(2)}) %collective-permute-start.9) | collective-permute-done | bytes 516128 | tf_op jit(solution)/shard_map/ppermute | solution.py:58
  52.5 0.1 shard_map.116
  52.7 2.7 %collective-permute-start.11 = (bf16[32,2688]{1,0:T(8,128)(2,1)S(1)}, bf16[32,2688]{1,0:T(8,128)(2,1)S(1)}, u32[]{:S(2)}, u32[]{:S(2)}) collective-permute-start(bf16[32,2688]{1,0:T(8,128)(2,1)S(1)} %get-tuple-element.95), channel_id=1, source_target_pairs={{0,8},{4,12},{8,0},{12,4},{1,9},{5,13},{9,1},{13,5},{2,10},{6,14},... | collective-permute-start | bytes 516104 | tf_op jit(solution)/shard_map/ppermute | solution.py:46
  55.4 2.4 %collective-permute-done.5.b = bf16[64,2304]{1,0:T(8,128)(2,1)S(1)} collective-permute-done((bf16[64,2304]{1,0:T(8,128)(2,1)S(1)}, bf16[64,2304]{1,0:T(8,128)(2,1)S(1)}, u32[]{:S(2)}, u32[]{:S(2)}) %collective-permute-start.5) | collective-permute-done | bytes 294944 | tf_op jit(solution)/shard_map/ppermute | solution.py:46
  57.8 1.1 collective-permute-done.6.c
  59.0 0.1 shard_map.115
  59.1 1.1 collective-permute-start.7
  60.2 3.3 %collective-permute-done.7.far_a = bf16[32,2304]{1,0:T(8,128)(2,1)S(1)} collective-permute-done((bf16[32,2304]{1,0:T(8,128)(2,1)S(1)}, bf16[32,2304]{1,0:T(8,128)(2,1)S(1)}, u32[]{:S(2)}, u32[]{:S(2)}) %collective-permute-start.7) | collective-permute-done | bytes 147488 | tf_op jit(solution)/shard_map/ppermute | solution.py:58
  63.5 0.4 collective-permute-done.10.right
  63.9 1.7 %collective-permute-done.12.left = bf16[32,2688]{1,0:T(8,128)(2,1)S(1)} collective-permute-done((bf16[32,2688]{1,0:T(8,128)(2,1)S(1)}, bf16[32,2688]{1,0:T(8,128)(2,1)S(1)}, u32[]{:S(2)}, u32[]{:S(2)}) %collective-permute-start.12) | collective-permute-done | bytes 172064 | tf_op jit(solution)/shard_map/ppermute | solution.py:46
  65.6 0.9 shard_map.117
  66.5 1.7 %collective-permute-start.18 = (bf16[32,4992]{1,0:T(8,128)(2,1)S(1)}, bf16[32,4992]{1,0:T(8,128)(2,1)S(1)}, u32[]{:S(2)}, u32[]{:S(2)}) collective-permute-start(bf16[32,4992]{1,0:T(8,128)(2,1)S(1)} %get-tuple-element.98.refs_0_), channel_id=1, source_target_pairs={{0,2},{2,0},{1,3},{3,1},{4,6},{6,4},{5,7},{7,5},{8,10},{10,8},{9,1... | collective-permute-start | bytes 958472 | tf_op jit(solution)/shard_map/ppermute | solution.py:58
  68.2 1.4 %collective-permute-start.14 = (bf16[32,4992]{1,0:T(8,128)(2,1)S(1)}, bf16[32,4992]{1,0:T(8,128)(2,1)S(1)}, u32[]{:S(2)}, u32[]{:S(2)}) collective-permute-start(bf16[32,4992]{1,0:T(8,128)(2,1)S(1)} %get-tuple-element.98.refs_0_), channel_id=1, source_target_pairs={{0,4},{4,8},{8,12},{12,0},{1,5},{5,9},{9,13},{13,1},{2,6},{6,10},{... | collective-permute-start | bytes 958472 | tf_op jit(solution)/shard_map/ppermute | solution.py:46
  69.6 1.4 %collective-permute-start.17 = (bf16[32,2432]{1,0:T(8,128)(2,1)S(1)}, bf16[32,2432]{1,0:T(8,128)(2,1)S(1)}, u32[]{:S(2)}, u32[]{:S(2)}) collective-permute-start(bf16[32,2432]{1,0:T(8,128)(2,1)S(1)} %get-tuple-element.100), channel_id=1, source_target_pairs={{0,12},{4,0},{8,4},{12,8},{1,13},{5,1},{9,5},{13,9},{2,14},{6,2},{... | collective-permute-start | bytes 466952 | tf_op jit(solution)/shard_map/ppermute | solution.py:46
  70.9 1.5 %collective-permute-start.13 = (bf16[32,2560]{1,0:T(8,128)(2,1)S(1)}, bf16[32,2560]{1,0:T(8,128)(2,1)S(1)}, u32[]{:S(2)}, u32[]{:S(2)}) collective-permute-start(bf16[32,2560]{1,0:T(8,128)(2,1)S(1)} %get-tuple-element.97), channel_id=1, source_target_pairs={{0,12},{4,0},{8,4},{12,8},{1,13},{5,1},{9,5},{13,9},{2,14},{6,2},{... | collective-permute-start | bytes 491528 | tf_op jit(solution)/shard_map/ppermute | solution.py:46
  72.4 1.5 %collective-permute-done.17.refs_3_ = bf16[32,2432]{1,0:T(8,128)(2,1)S(1)} collective-permute-done((bf16[32,2432]{1,0:T(8,128)(2,1)S(1)}, bf16[32,2432]{1,0:T(8,128)(2,1)S(1)}, u32[]{:S(2)}, u32[]{:S(2)}) %collective-permute-start.17) | collective-permute-done | bytes 155680 | tf_op jit(solution)/shard_map/ppermute | solution.py:46
  73.9 0.3 collective-permute-done.18.refs_1_
  74.2 2.4 %collective-permute-start.20 = (bf16[32,4992]{1,0:T(8,128)(2,1)S(1)}, bf16[32,4992]{1,0:T(8,128)(2,1)S(1)}, u32[]{:S(2)}, u32[]{:S(2)}) collective-permute-start(bf16[32,4992]{1,0:T(8,128)(2,1)S(1)} %collective-permute-done.18.refs_1_), channel_id=1, source_target_pairs={{0,4},{4,8},{8,12},{12,0},{1,5},{5,9},{9,13},{13,1},{2,6},{6,10},{... | collective-permute-start | bytes 958472 | tf_op jit(solution)/shard_map/ppermute | solution.py:46
  76.6 0.9 collective-permute-done.13.refs_2_
  77.4 2.2 %collective-permute-start.15 = (bf16[32,2560]{1,0:T(8,128)(2,1)S(1)}, bf16[32,2560]{1,0:T(8,128)(2,1)S(1)}, u32[]{:S(2)}, u32[]{:S(2)}) collective-permute-start(bf16[32,2560]{1,0:T(8,128)(2,1)S(1)} %collective-permute-done.13.refs_2_), channel_id=1, source_target_pairs={{0,12},{4,0},{8,4},{12,8},{1,13},{5,1},{9,5},{13,9},{2,14},{6,2},{... | collective-permute-start | bytes 491528 | tf_op jit(solution)/shard_map/ppermute | solution.py:46
  79.7 0.6 collective-permute-start.19
  80.3 0.6 collective-permute-start.22
  80.9 0.8 collective-permute-start.23
  81.7 0.2 collective-permute-done.15.refs_0_
  81.9 0.6 collective-permute-start.16
  82.5 0.9 shard_map.119.lines
  83.5 1.9 %collective-permute-done.19.refs_1_ = bf16[32,2432]{1,0:T(8,128)(2,1)S(1)} collective-permute-done((bf16[32,2432]{1,0:T(8,128)(2,1)S(1)}, bf16[32,2432]{1,0:T(8,128)(2,1)S(1)}, u32[]{:S(2)}, u32[]{:S(2)}) %collective-permute-start.19) | collective-permute-done | bytes 155680 | tf_op jit(solution)/shard_map/ppermute | solution.py:46
  85.4 0.7 collective-permute-start.21
  86.1 1.5 %shard_map.120 = (f32[128,320]{1,0:T(8,128)S(1)}, f32[128,320]{1,0:T(8,128)S(1)}) custom-call(bf16[128,4992]{1,0:T(8,128)(2,1)S(1)} %shard_map.118.refs_0_.early_in, bf16[320,1664]{1,0:T(8,128)(2,1)S(1)} %slice_select_fusion.2.w0.refs_1_.go, bf16[320,1664]{1,0:T(8,128)(2,1)S(1)} %collective-permute-done.1.w1.refs_2_.gs, ...), custom_call_target="tpu_custom_call" | custom-call | flops 545259520 | bytes 6291456 | tf_op jit(solution)/shard_map/pallas_call | solution.py:66
  87.7 1.5 %shard_map.122 = (f32[96,320]{1,0:T(8,128)S(1)}, f32[96,320]{1,0:T(8,128)S(1)}) custom-call(bf16[96,4992]{1,0:T(8,128)(2,1)S(1)} %shard_map.121.refs_0_, bf16[320,1664]{1,0:T(8,128)(2,1)S(1)} %slice_select_fusion.2.w0.refs_1_.go, bf16[320,1664]{1,0:T(8,128)(2,1)S(1)} %collective-permute-done.1.w1.refs_2_.gs, ...), custom_call_target="tpu_custom_call" | custom-call | flops 408944640 | bytes 6291456 | tf_op jit(solution)/shard_map/pallas_call | solution.py:66
  89.2 1.0 shard_map.123.sent
  90.2 3.3 %collective-permute-done.21.refs_1_ = bf16[32,2432]{1,0:T(8,128)(2,1)S(1)} collective-permute-done((bf16[32,2432]{1,0:T(8,128)(2,1)S(1)}, bf16[32,2432]{1,0:T(8,128)(2,1)S(1)}, u32[]{:S(2)}, u32[]{:S(2)}) %collective-permute-start.21) | collective-permute-done | bytes 155680 | tf_op jit(solution)/shard_map/ppermute | solution.py:58
  93.5 2.3 %shard_map.125 = (f32[32,320]{1,0:T(8,128)S(1)}, f32[32,320]{1,0:T(8,128)S(1)}, bf16[512,320]{1,0:T(8,128)(2,1)S(1)}) custom-call(s32[4]{0:T(128)S(1)} %pad_add_fusion.index, s32[8,256]{1,0:T(8,128)S(1)} %shard_map.119.lines, f32[512,320]{1,0:T(8,128)S(1)} %shard_map.123.sent, bf16[32,4992]{1,0:T(8,128)(2,1)S(1)} %shard_map.124.value.refs_5_, ...), custom_call_target="tpu_custom_call" | custom-call | flops 83886080 | bytes 1048576 | tf_op jit(solution)/shard_map/pallas_call | solution.py:66
  95.8 3.6 %collective-permute-start.24 = (bf16[512,320]{1,0:T(8,128)(2,1)S(1)}, bf16[512,320]{1,0:T(8,128)(2,1)S(1)}, u32[]{:S(2)}, u32[]{:S(2)}) collective-permute-start(bf16[512,320]{1,0:T(8,128)(2,1)S(1)} %get-tuple-element.115), channel_id=1, source_target_pairs={{0,1},{1,0},{2,3},{3,2},{4,5},{5,4},{6,7},{7,6},{8,9},{9,8},{10,11... | collective-permute-start | bytes 983048 | tf_op jit(solution)/shard_map/ppermute | solution.py:62
  99.7 1.0 shard_map.127.kept
  100.7 0.2 collective-permute-done.24.sent
  100.8 0.4 collective-permute-start.26
  101.2 0.8 shard_map.128
  102.0 4.6 %all-to-all-start.1 = ((bf16[64,8,320]{2,1,0:T(8,128)(2,1)}), bf16[64,8,320]{2,1,0:T(8,128)(2,1)S(1)}, u32[]{:S(2)}, u32[]{:S(2)}) async-start(bf16[64,8,320]{2,1,0:T(8,128)(2,1)} %bitcast.5), calls=%async_computation.1 | async-start | bytes 786432 | tf_op jit(solution)/shard_map/all_to_all | solution.py:508
  106.7 7.6 %shard_map.129 = (bf16[320,3200]{1,0:T(8,128)(2,1)}, bf16[320,3200]{1,0:T(8,128)(2,1)}, bf16[320,3200]{1,0:T(8,128)(2,1)}) custom-call(s32[4]{0:T(128)} %copy-done.3, bf16[8,64,384]{2,1,0:T(8,128)(2,1)} %copy-done, bf16[128,4992]{1,0:T(8,128)(2,1)} %copy-done.1, bf16[128,4992]{1,0:T(8,128)(2,1)} %copy-done.2, ...), custom_call_target="tpu_custom_call" | custom-call | flops 1572864000 | bytes 12582912 | tf_op jit(solution)/shard_map/pallas_call | solution.py:413
  114.2 3.9 %all-to-all-done.1.back = bf16[64,8,320]{2,1,0:T(8,128)(2,1)S(1)} async-done(((bf16[64,8,320]{2,1,0:T(8,128)(2,1)}), bf16[64,8,320]{2,1,0:T(8,128)(2,1)S(1)}, u32[]{:S(2)}, u32[]{:S(2)}) %all-to-all-start.1) | async-done | bytes 327712 | tf_op jit(solution)/shard_map/all_to_all | solution.py:508
  118.2 1.7 %shard_map.130 = bf16[128,5120]{1,0:T(8,128)(2,1)} custom-call(bf16[8,128]{1,0:T(8,128)(2,1)S(1)} %copy-done.4, bf16[64,8,320]{2,1,0:T(8,128)(2,1)S(1)} %all-to-all-done.1.back), custom_call_target="tpu_custom_call" | custom-call | tf_op jit(solution)/shard_map/pallas_call | solution.py:66
  (38 shorter events, 0.6 us)
Async XLA Ops:
  0.6 15.1 %copy-start.7 = (bf16[320,3200]{1,0:T(8,128)(2,1)S(1)}, bf16[320,3200]{1,0:T(8,128)(2,1)}, u32[]{:S(2)}) copy-start(bf16[320,3200]{1,0:T(8,128)(2,1)} %param.13) | copy-start | bytes 6144004
  4.2 28.1 %all-to-all-start = ((bf16[128,8,384]{2,1,0:T(8,128)(2,1)}), bf16[128,8,384]{2,1,0:T(8,128)(2,1)S(1)}, u32[]{:S(2)}, u32[]{:S(2)}) async-start(bf16[128,8,384]{2,1,0:T(8,128)(2,1)} %get-tuple-element.70), calls=%async_computation | async-start | bytes 1572864 | tf_op jit(solution)/shard_map/all_to_all | solution.py:446
  15.8 2.0 %copy-start.6 = (bf16[320,3200]{1,0:T(8,128)(2,1)S(1)}, bf16[320,3200]{1,0:T(8,128)(2,1)}, u32[]{:S(2)}) copy-start(bf16[320,3200]{1,0:T(8,128)(2,1)} %param.14) | copy-start | bytes 6144004
  17.7 2.0 %copy-start.5 = (bf16[3200,320]{0,1:T(8,128)(2,1)S(1)}, bf16[3200,320]{0,1:T(8,128)(2,1)}, u32[]{:S(2)}) copy-start(bf16[3200,320]{0,1:T(8,128)(2,1)} %param.15) | copy-start | bytes 6144004
  20.8 15.8 %collective-permute-start.3 = (bf16[320,1664]{1,0:T(8,128)(2,1)}, bf16[320,1664]{1,0:T(8,128)(2,1)}, u32[]{:S(2)}, u32[]{:S(2)}) collective-permute-start(bf16[320,1664]{1,0:T(8,128)(2,1)} %slice_select_fusion.3), channel_id=1, source_target_pairs={{0,1},{1,0},{2,3},{3,2},{4,5},{5,4},{6,7},{7,6},{8,9},{9,8},{10,11... | collective-permute-start | bytes 3194888 | tf_op jit(solution)/shard_map/ppermute | solution.py:62
  21.9 14.7 %collective-permute-start.2 = (bf16[320,1664]{1,0:T(8,128)(2,1)}, bf16[320,1664]{1,0:T(8,128)(2,1)S(1)}, u32[]{:S(2)}, u32[]{:S(2)}) collective-permute-start(bf16[320,1664]{1,0:T(8,128)(2,1)} %slice_select_fusion.4), channel_id=1, source_target_pairs={{0,1},{1,0},{2,3},{3,2},{4,5},{5,4},{6,7},{7,6},{8,9},{9,8},{10,11... | collective-permute-start | bytes 3194888 | tf_op jit(solution)/shard_map/ppermute | solution.py:62
  21.9 14.7 %collective-permute-start.1 = (bf16[320,1664]{1,0:T(8,128)(2,1)}, bf16[320,1664]{1,0:T(8,128)(2,1)S(1)}, u32[]{:S(2)}, u32[]{:S(2)}) collective-permute-start(bf16[320,1664]{1,0:T(8,128)(2,1)} %slice_select_fusion.5), channel_id=1, source_target_pairs={{0,1},{1,0},{2,3},{3,2},{4,5},{5,4},{6,7},{7,6},{8,9},{9,8},{10,11... | collective-permute-start | bytes 3194888 | tf_op jit(solution)/shard_map/ppermute | solution.py:62
  22.5 77.2 %copy-start.3 = (s32[4]{0:T(128)}, s32[4]{0:T(128)S(1)}, u32[]{:S(2)}) copy-start(s32[4]{0:T(128)S(1)} %pad_add_fusion.index) | copy-start | bytes 52
  33.2 49.3 %copy-start = (bf16[8,64,384]{2,1,0:T(8,128)(2,1)}, bf16[8,64,384]{2,1,0:T(8,128)(2,1)S(1)}, u32[]{:S(2)}) copy-start(bf16[8,64,384]{2,1,0:T(8,128)(2,1)S(1)} %shard_map.112.own) | copy-start | bytes 1179652
  33.2 3.4 %collective-permute-start = (bf16[8,64,384]{2,1,0:T(8,128)(2,1)S(1)}, bf16[8,64,384]{2,1,0:T(8,128)(2,1)S(1)}, u32[]{:S(2)}, u32[]{:S(2)}) collective-permute-start(bf16[8,64,384]{2,1,0:T(8,128)(2,1)S(1)} %shard_map.112.own), channel_id=1, source_target_pairs={{0,1},{1,0},{2,3},{3,2},{4,5},{5,4},{6,7},{7,6},{8,9},{9,8},{10,11... | collective-permute-start | bytes 1179656 | tf_op jit(solution)/shard_map/ppermute | solution.py:62
  33.6 2.9 %copy-start.8 = (bf16[320,3200]{1,0:T(8,128)(2,1)S(1)}, bf16[320,3200]{1,0:T(8,128)(2,1)}, u32[]{:S(2)}) copy-start(bf16[320,3200]{1,0:T(8,128)(2,1)} %param.13) | copy-start | bytes 6144004
  39.3 13.2 %collective-permute-start.9 = (bf16[96,2688]{1,0:T(8,128)(2,1)S(1)}, bf16[96,2688]{1,0:T(8,128)(2,1)S(1)}, u32[]{:S(2)}, u32[]{:S(2)}) collective-permute-start(bf16[96,2688]{1,0:T(8,128)(2,1)S(1)} %get-tuple-element.93), channel_id=1, source_target_pairs={{0,2},{2,0},{1,3},{3,1},{4,6},{6,4},{5,7},{7,5},{8,10},{10,8},{9,1... | collective-permute-start | bytes 1548296 | tf_op jit(solution)/shard_map/ppermute | solution.py:58
  42.3 10.4 %collective-permute-start.4 = (bf16[64,2304]{1,0:T(8,128)(2,1)S(1)}, bf16[64,2304]{1,0:T(8,128)(2,1)S(1)}, u32[]{:S(2)}, u32[]{:S(2)}) collective-permute-start(bf16[64,2304]{1,0:T(8,128)(2,1)S(1)} %get-tuple-element.86), channel_id=1, source_target_pairs={{0,4},{4,8},{8,12},{12,0},{1,5},{5,9},{9,13},{13,1},{2,6},{6,10},{... | collective-permute-start | bytes 884744 | tf_op jit(solution)/shard_map/ppermute | solution.py:46
  42.6 15.2 %collective-permute-start.5 = (bf16[64,2304]{1,0:T(8,128)(2,1)S(1)}, bf16[64,2304]{1,0:T(8,128)(2,1)S(1)}, u32[]{:S(2)}, u32[]{:S(2)}) collective-permute-start(bf16[64,2304]{1,0:T(8,128)(2,1)S(1)} %get-tuple-element.87), channel_id=1, source_target_pairs={{0,8},{4,12},{8,0},{12,4},{1,9},{5,13},{9,1},{13,5},{2,10},{6,14},... | collective-permute-start | bytes 884744 | tf_op jit(solution)/shard_map/ppermute | solution.py:46
  44.3 14.6 %collective-permute-start.6 = (bf16[64,2304]{1,0:T(8,128)(2,1)S(1)}, bf16[64,2304]{1,0:T(8,128)(2,1)S(1)}, u32[]{:S(2)}, u32[]{:S(2)}) collective-permute-start(bf16[64,2304]{1,0:T(8,128)(2,1)S(1)} %get-tuple-element.88), channel_id=1, source_target_pairs={{0,12},{4,0},{8,4},{12,8},{1,13},{5,1},{9,5},{13,9},{2,14},{6,2},{... | collective-permute-start | bytes 884744 | tf_op jit(solution)/shard_map/ppermute | solution.py:46
  45.5 14.7 %collective-permute-start.8 = (bf16[32,2688]{1,0:T(8,128)(2,1)S(1)}, bf16[32,2688]{1,0:T(8,128)(2,1)S(1)}, u32[]{:S(2)}, u32[]{:S(2)}) collective-permute-start(bf16[32,2688]{1,0:T(8,128)(2,1)S(1)} %get-tuple-element.92), channel_id=1, source_target_pairs={{0,2},{2,0},{1,3},{3,1},{4,6},{6,4},{5,7},{7,5},{8,10},{10,8},{9,1... | collective-permute-start | bytes 516104 | tf_op jit(solution)/shard_map/ppermute | solution.py:58
  52.6 11.3 %collective-permute-start.10 = (bf16[32,2688]{1,0:T(8,128)(2,1)S(1)}, bf16[32,2688]{1,0:T(8,128)(2,1)S(1)}, u32[]{:S(2)}, u32[]{:S(2)}) collective-permute-start(bf16[32,2688]{1,0:T(8,128)(2,1)S(1)} %get-tuple-element.94), channel_id=1, source_target_pairs={{0,4},{4,8},{8,12},{12,0},{1,5},{5,9},{9,13},{13,1},{2,6},{6,10},{... | collective-permute-start | bytes 516104 | tf_op jit(solution)/shard_map/ppermute | solution.py:46
  52.7 11.2 %collective-permute-start.11 = (bf16[32,2688]{1,0:T(8,128)(2,1)S(1)}, bf16[32,2688]{1,0:T(8,128)(2,1)S(1)}, u32[]{:S(2)}, u32[]{:S(2)}) collective-permute-start(bf16[32,2688]{1,0:T(8,128)(2,1)S(1)} %get-tuple-element.95), channel_id=1, source_target_pairs={{0,8},{4,12},{8,0},{12,4},{1,9},{5,13},{9,1},{13,5},{2,10},{6,14},... | collective-permute-start | bytes 516104 | tf_op jit(solution)/shard_map/ppermute | solution.py:46
  57.8 7.8 %collective-permute-start.12 = (bf16[32,2688]{1,0:T(8,128)(2,1)S(1)}, bf16[32,2688]{1,0:T(8,128)(2,1)S(1)}, u32[]{:S(2)}, u32[]{:S(2)}) collective-permute-start(bf16[32,2688]{1,0:T(8,128)(2,1)S(1)} %get-tuple-element.96), channel_id=1, source_target_pairs={{0,12},{4,0},{8,4},{12,8},{1,13},{5,1},{9,5},{13,9},{2,14},{6,2},{... | collective-permute-start | bytes 516104 | tf_op jit(solution)/shard_map/ppermute | solution.py:46
  59.1 4.4 %collective-permute-start.7 = (bf16[32,2304]{1,0:T(8,128)(2,1)S(1)}, bf16[32,2304]{1,0:T(8,128)(2,1)S(1)}, u32[]{:S(2)}, u32[]{:S(2)}) collective-permute-start(bf16[32,2304]{1,0:T(8,128)(2,1)S(1)} %get-tuple-element.90), channel_id=1, source_target_pairs={{0,2},{2,0},{1,3},{3,1},{4,6},{6,4},{5,7},{7,5},{8,10},{10,8},{9,1... | collective-permute-start | bytes 442376 | tf_op jit(solution)/shard_map/ppermute | solution.py:58
  66.5 7.7 %collective-permute-start.18 = (bf16[32,4992]{1,0:T(8,128)(2,1)S(1)}, bf16[32,4992]{1,0:T(8,128)(2,1)S(1)}, u32[]{:S(2)}, u32[]{:S(2)}) collective-permute-start(bf16[32,4992]{1,0:T(8,128)(2,1)S(1)} %get-tuple-element.98.refs_0_), channel_id=1, source_target_pairs={{0,2},{2,0},{1,3},{3,1},{4,6},{6,4},{5,7},{7,5},{8,10},{10,8},{9,1... | collective-permute-start | bytes 958472 | tf_op jit(solution)/shard_map/ppermute | solution.py:58
  68.2 9.3 %collective-permute-start.14 = (bf16[32,4992]{1,0:T(8,128)(2,1)S(1)}, bf16[32,4992]{1,0:T(8,128)(2,1)S(1)}, u32[]{:S(2)}, u32[]{:S(2)}) collective-permute-start(bf16[32,4992]{1,0:T(8,128)(2,1)S(1)} %get-tuple-element.98.refs_0_), channel_id=1, source_target_pairs={{0,4},{4,8},{8,12},{12,0},{1,5},{5,9},{9,13},{13,1},{2,6},{6,10},{... | collective-permute-start | bytes 958472 | tf_op jit(solution)/shard_map/ppermute | solution.py:46
  69.6 4.4 %collective-permute-start.17 = (bf16[32,2432]{1,0:T(8,128)(2,1)S(1)}, bf16[32,2432]{1,0:T(8,128)(2,1)S(1)}, u32[]{:S(2)}, u32[]{:S(2)}) collective-permute-start(bf16[32,2432]{1,0:T(8,128)(2,1)S(1)} %get-tuple-element.100), channel_id=1, source_target_pairs={{0,12},{4,0},{8,4},{12,8},{1,13},{5,1},{9,5},{13,9},{2,14},{6,2},{... | collective-permute-start | bytes 466952 | tf_op jit(solution)/shard_map/ppermute | solution.py:46
  70.9 6.5 %collective-permute-start.13 = (bf16[32,2560]{1,0:T(8,128)(2,1)S(1)}, bf16[32,2560]{1,0:T(8,128)(2,1)S(1)}, u32[]{:S(2)}, u32[]{:S(2)}) collective-permute-start(bf16[32,2560]{1,0:T(8,128)(2,1)S(1)} %get-tuple-element.97), channel_id=1, source_target_pairs={{0,12},{4,0},{8,4},{12,8},{1,13},{5,1},{9,5},{13,9},{2,14},{6,2},{... | collective-permute-start | bytes 491528 | tf_op jit(solution)/shard_map/ppermute | solution.py:46
  74.2 11.2 %collective-permute-start.20 = (bf16[32,4992]{1,0:T(8,128)(2,1)S(1)}, bf16[32,4992]{1,0:T(8,128)(2,1)S(1)}, u32[]{:S(2)}, u32[]{:S(2)}) collective-permute-start(bf16[32,4992]{1,0:T(8,128)(2,1)S(1)} %collective-permute-done.18.refs_1_), channel_id=1, source_target_pairs={{0,4},{4,8},{8,12},{12,0},{1,5},{5,9},{9,13},{13,1},{2,6},{6,10},{... | collective-permute-start | bytes 958472 | tf_op jit(solution)/shard_map/ppermute | solution.py:46
  77.4 4.5 %collective-permute-start.15 = (bf16[32,2560]{1,0:T(8,128)(2,1)S(1)}, bf16[32,2560]{1,0:T(8,128)(2,1)S(1)}, u32[]{:S(2)}, u32[]{:S(2)}) collective-permute-start(bf16[32,2560]{1,0:T(8,128)(2,1)S(1)} %collective-permute-done.13.refs_2_), channel_id=1, source_target_pairs={{0,12},{4,0},{8,4},{12,8},{1,13},{5,1},{9,5},{13,9},{2,14},{6,2},{... | collective-permute-start | bytes 491528 | tf_op jit(solution)/shard_map/ppermute | solution.py:46
  79.7 5.7 %collective-permute-start.19 = (bf16[32,2432]{1,0:T(8,128)(2,1)S(1)}, bf16[32,2432]{1,0:T(8,128)(2,1)S(1)}, u32[]{:S(2)}, u32[]{:S(2)}) collective-permute-start(bf16[32,2432]{1,0:T(8,128)(2,1)S(1)} %collective-permute-done.17.refs_3_), channel_id=1, source_target_pairs={{0,12},{4,0},{8,4},{12,8},{1,13},{5,1},{9,5},{13,9},{2,14},{6,2},{... | collective-permute-start | bytes 466952 | tf_op jit(solution)/shard_map/ppermute | solution.py:46
  80.3 7.3 %collective-permute-start.22 = (bf16[32,2560]{1,0:T(8,128)(2,1)S(1)}, bf16[32,2560]{1,0:T(8,128)(2,1)S(1)}, u32[]{:S(2)}, u32[]{:S(2)}) collective-permute-start(bf16[32,2560]{1,0:T(8,128)(2,1)S(1)} %collective-permute-done.13.refs_2_), channel_id=1, source_target_pairs={{0,2},{2,0},{1,3},{3,1},{4,6},{6,4},{5,7},{7,5},{8,10},{10,8},{9,1... | collective-permute-start | bytes 491528 | tf_op jit(solution)/shard_map/ppermute | solution.py:58
  80.9 6.7 %collective-permute-start.23 = (bf16[32,2432]{1,0:T(8,128)(2,1)S(1)}, bf16[32,2432]{1,0:T(8,128)(2,1)S(1)}, u32[]{:S(2)}, u32[]{:S(2)}) collective-permute-start(bf16[32,2432]{1,0:T(8,128)(2,1)S(1)} %collective-permute-done.17.refs_3_), channel_id=1, source_target_pairs={{0,2},{2,0},{1,3},{3,1},{4,6},{6,4},{5,7},{7,5},{8,10},{10,8},{9,1... | collective-permute-start | bytes 466952 | tf_op jit(solution)/shard_map/ppermute | solution.py:58
  81.9 8.3 %collective-permute-start.16 = (bf16[32,2560]{1,0:T(8,128)(2,1)S(1)}, bf16[32,2560]{1,0:T(8,128)(2,1)S(1)}, u32[]{:S(2)}, u32[]{:S(2)}) collective-permute-start(bf16[32,2560]{1,0:T(8,128)(2,1)S(1)} %collective-permute-done.15.refs_0_), channel_id=1, source_target_pairs={{0,2},{2,0},{1,3},{3,1},{4,6},{6,4},{5,7},{7,5},{8,10},{10,8},{9,1... | collective-permute-start | bytes 491528 | tf_op jit(solution)/shard_map/ppermute | solution.py:58
  83.5 16.0 %copy-start.1 = (bf16[128,4992]{1,0:T(8,128)(2,1)}, bf16[128,4992]{1,0:T(8,128)(2,1)S(1)}, u32[]{:S(2)}) copy-start(bf16[128,4992]{1,0:T(8,128)(2,1)S(1)} %shard_map.118.refs_0_.early_in) | copy-start | bytes 3833860
  85.4 8.1 %collective-permute-start.21 = (bf16[32,2432]{1,0:T(8,128)(2,1)S(1)}, bf16[32,2432]{1,0:T(8,128)(2,1)S(1)}, u32[]{:S(2)}, u32[]{:S(2)}) collective-permute-start(bf16[32,2432]{1,0:T(8,128)(2,1)S(1)} %collective-permute-done.19.refs_1_), channel_id=1, source_target_pairs={{0,2},{2,0},{1,3},{3,1},{4,6},{6,4},{5,7},{7,5},{8,10},{10,8},{9,1... | collective-permute-start | bytes 466952 | tf_op jit(solution)/shard_map/ppermute | solution.py:58
  95.8 5.0 %collective-permute-start.24 = (bf16[512,320]{1,0:T(8,128)(2,1)S(1)}, bf16[512,320]{1,0:T(8,128)(2,1)S(1)}, u32[]{:S(2)}, u32[]{:S(2)}) collective-permute-start(bf16[512,320]{1,0:T(8,128)(2,1)S(1)} %get-tuple-element.115), channel_id=1, source_target_pairs={{0,1},{1,0},{2,3},{3,2},{4,5},{5,4},{6,7},{7,6},{8,9},{9,8},{10,11... | collective-permute-start | bytes 983048 | tf_op jit(solution)/shard_map/ppermute | solution.py:62
  99.5 7.2 %collective-permute-start.25 = (bf16[128,4992]{1,0:T(8,128)(2,1)S(1)}, bf16[128,4992]{1,0:T(8,128)(2,1)}, u32[]{:S(2)}, u32[]{:S(2)}) collective-permute-start(bf16[128,4992]{1,0:T(8,128)(2,1)S(1)} %shard_map.118.refs_0_.early_in), channel_id=1, source_target_pairs={{0,1},{1,0},{2,3},{3,2},{4,5},{5,4},{6,7},{7,6},{8,9},{9,8},{10,11... | collective-permute-start | bytes 3833864 | tf_op jit(solution)/shard_map/ppermute | solution.py:62
  99.7 2.4 %copy-start.2 = (bf16[128,4992]{1,0:T(8,128)(2,1)}, bf16[128,4992]{1,0:T(8,128)(2,1)S(1)}, u32[]{:S(2)}) copy-start(bf16[128,4992]{1,0:T(8,128)(2,1)S(1)} %shard_map.126.late_in) | copy-start | bytes 3833860
  100.8 5.9 %collective-permute-start.26 = (bf16[128,4992]{1,0:T(8,128)(2,1)S(1)}, bf16[128,4992]{1,0:T(8,128)(2,1)}, u32[]{:S(2)}, u32[]{:S(2)}) collective-permute-start(bf16[128,4992]{1,0:T(8,128)(2,1)S(1)} %shard_map.126.late_in), channel_id=1, source_target_pairs={{0,1},{1,0},{2,3},{3,2},{4,5},{5,4},{6,7},{7,6},{8,9},{9,8},{10,11... | collective-permute-start | bytes 3833864 | tf_op jit(solution)/shard_map/ppermute | solution.py:62
  102.0 16.2 %all-to-all-start.1 = ((bf16[64,8,320]{2,1,0:T(8,128)(2,1)}), bf16[64,8,320]{2,1,0:T(8,128)(2,1)S(1)}, u32[]{:S(2)}, u32[]{:S(2)}) async-start(bf16[64,8,320]{2,1,0:T(8,128)(2,1)} %bitcast.5), calls=%async_computation.1 | async-start | bytes 786432 | tf_op jit(solution)/shard_map/all_to_all | solution.py:508
  106.6 11.5 %copy-start.4 = (bf16[8,128]{1,0:T(8,128)(2,1)S(1)}, bf16[8,128]{1,0:T(8,128)(2,1)}, u32[]{:S(2)}) copy-start(bf16[8,128]{1,0:T(8,128)(2,1)} %get-tuple-element.68.owner) | copy-start | bytes 6148

commit v6 on v5

--- a/solution.py
+++ b/solution.py
@@ -463,7 +463,7 @@
     right_b, two_b, left_b = call(sum_b_kernel, [(shape_b, BF)] * 3, [near, far])
     here_a, far_a = call(sum_a_kernel, [(shape_a, F32), (shape_a, BF)], [here_a, right, two, left])
     far_a = across(far_a)
-    right_b, left_b, two_b = up(right_b), down(left_b), along(two_b, 2)
+    two_b, right_b, left_b = along(two_b, 2), up(right_b), down(left_b)
     v00, *p00 = call(
         value_kernel,
         [((GROUP, 3 * WIN), BF), ((GROUP, PART), BF), ((GROUP, 3 * WIN - PART), BF)],

time: 120 us -> 120 us (level)
  no operation moved by 1% of the time
where the time goes in v6:
time: 120 us
  starting transfers between devices  45.1 us (38%)
  waiting for transfers between devices  36.7 us (31%)
  Pallas kernels  29.1 us (24%)
  other arithmetic  6.06 us (5%)
  local copies, waits for them, and re-layouts  2.03 us (2%)
    pallas_call x18, Pallas kernels, call(): pl.pallas_call(kernel, out_shape=[jax.ShapeDtypeStruct(s, k) for s, k in...  17.9 us
    ppermute x12, starting transfers between devices, along(): return lax.ppermute(t, 'x', [(i, (i + step) % 4) for i in range(4)])  15.4 us
    ppermute x8, waiting for transfers between devices, across(): return lax.ppermute(t, 'zl', SWAP)  12.5 us
    all_to_all x1, starting transfers between devices, shards(): got = lax.all_to_all(message, AXES, 0, 0, tiled=True)  11.5 us
    ppermute x12, waiting for transfers between devices, along(): return lax.ppermute(t, 'x', [(i, (i + step) % 4) for i in range(4)])  10.2 us
    all_to_all x1, waiting for transfers between devices, shards(): got = lax.all_to_all(message, AXES, 0, 0, tiled=True)  9.94 us
    pallas_call x1, Pallas kernels, weight_grads(): pl.pallas_call(grad_kernel, out_shape=[jax.ShapeDtypeStruct((DL, FL), BF)...  7.55 us
    ppermute x8, starting transfers between devices, across(): return lax.ppermute(t, 'zl', SWAP)  7.52 us
  transfers between devices with their start and end apart: 29, of which 15 were waited for; matrix products, arithmetic and copies ran while one was open for 5% of the time, Pallas kernels for 15%

profile of v6, /device:TPU:1, one launch (start us, length us, event | category | flops | bytes accessed | tf_op | source)
XLA Modules:
  0.0 119.9 jit_solution(15287196745211808580)
XLA Ops:
  0.6 3.6 %shard_map.111 = (bf16[128,8,384]{2,1,0:T(8,128)(2,1)}, bf16[8,128]{1,0:T(8,128)(2,1)}) custom-call(s32[1,1,4]{2,1,0:T(1,128)} %chosen_in.1, s32[1,16]{1,0:T(1,128)} %counts_in.1, f32[128]{0:T(128)} %advantage_in.1, bf16[128,5120]{1,0:T(8,128)(2,1)} %tokens.1, bf16[128,5120]{1,0:T(8,128)(2,1)} %cotangent.1), custom_call_target="tpu_custom_call" | custom-call | tf_op jit(solution)/shard_map/pallas_call | solution.py:143
  4.2 11.5 %all-to-all-start = ((bf16[128,8,384]{2,1,0:T(8,128)(2,1)}), bf16[128,8,384]{2,1,0:T(8,128)(2,1)S(1)}, u32[]{:S(2)}, u32[]{:S(2)}) async-start(bf16[128,8,384]{2,1,0:T(8,128)(2,1)} %get-tuple-element.70), calls=%async_computation | async-start | bytes 1572864 | tf_op jit(solution)/shard_map/all_to_all | solution.py:446
  15.8 1.1 slice_select_fusion.5
  16.9 0.8 copy-done.6
  17.7 1.1 slice_select_fusion.4
  18.8 0.9 copy-done.5
  19.7 1.1 slice_select_fusion.3
  20.8 1.1 collective-permute-start.3
  21.9 0.5 collective-permute-start.1
  22.5 9.9 %all-to-all-done = bf16[128,8,384]{2,1,0:T(8,128)(2,1)S(1)} async-done(((bf16[128,8,384]{2,1,0:T(8,128)(2,1)}), bf16[128,8,384]{2,1,0:T(8,128)(2,1)S(1)}, u32[]{:S(2)}, u32[]{:S(2)}) %all-to-all-start) | async-done | bytes 786464 | tf_op jit(solution)/shard_map/all_to_all | solution.py:446
  32.4 0.8 shard_map.112.own
  33.2 0.4 collective-permute-start
  33.6 2.6 %slice_select_fusion = (bf16[320,1664]{1,0:T(8,128)(2,1)S(1)}, bf16[320,1664]{1,0:T(8,128)(2,1)S(1)}) fusion(bf16[320,3200]{1,0:T(8,128)(2,1)} %bitcast.8, pred[]{:T(512)S(6)} %eq.3, bf16[320,3200]{1,0:T(8,128)(2,1)} %param.14), kind=kLoop, calls=%fused_computation | loop fusion | flops 1064960 | bytes 6389761 | tf_op jit(solution)/shard_map/jit(_where)/select_n | solution.py:438
  36.1 0.3 copy-done.8
  36.4 0.1 slice_select_fusion.2.w0.refs_1_.go
  36.6 2.7 %shard_map.113 = (bf16[32,2688]{1,0:T(8,128)(2,1)S(1)}, bf16[96,2688]{1,0:T(8,128)(2,1)S(1)}, f32[128,2688]{1,0:T(8,128)S(1)}) custom-call(s32[4]{0:T(128)S(1)} %pad_add_fusion.index, bf16[8,64,384]{2,1,0:T(8,128)(2,1)S(1)} %shard_map.112.own, bf16[8,64,384]{2,1,0:T(8,128)(2,1)S(1)} %collective-permute-done.sib, ...), custom_call_target="tpu_custom_call" | custom-call | flops 880803840 | bytes 10485760 | tf_op jit(solution)/shard_map/pallas_call | solution.py:66
  39.3 0.6 collective-permute-start.9
  39.9 2.4 %shard_map.114 = (f32[64,2304]{1,0:T(8,128)S(1)}, bf16[64,2304]{1,0:T(8,128)(2,1)S(1)}, bf16[64,2304]{1,0:T(8,128)(2,1)S(1)}, bf16[64,2304]{1,0:T(8,128)(2,1)S(1)}) custom-call(s32[4]{0:T(128)S(1)} %pad_add_fusion.index, bf16[8,64,384]{2,1,0:T(8,128)(2,1)S(1)} %shard_map.112.own, bf16[8,64,384]{2,1,0:T(8,128)(2,1)S(1)} %collective-permute-done.sib, ...), custom_call_target="tpu_custom_call" | custom-call | flops 754974720 | bytes 10485760 | tf_op jit(solution)/shard_map/pallas_call | solution.py:66
  42.3 0.3 collective-permute-start.4
  42.6 1.8 %collective-permute-start.5 = (bf16[64,2304]{1,0:T(8,128)(2,1)S(1)}, bf16[64,2304]{1,0:T(8,128)(2,1)S(1)}, u32[]{:S(2)}, u32[]{:S(2)}) collective-permute-start(bf16[64,2304]{1,0:T(8,128)(2,1)S(1)} %get-tuple-element.87), channel_id=1, source_target_pairs={{0,8},{4,12},{8,0},{12,4},{1,9},{5,13},{9,1},{13,5},{2,10},{6,14},... | collective-permute-start | bytes 884744 | tf_op jit(solution)/shard_map/ppermute | solution.py:46
  44.3 1.2 collective-permute-start.6
  45.5 1.4 %collective-permute-start.8 = (bf16[32,2688]{1,0:T(8,128)(2,1)S(1)}, bf16[32,2688]{1,0:T(8,128)(2,1)S(1)}, u32[]{:S(2)}, u32[]{:S(2)}) collective-permute-start(bf16[32,2688]{1,0:T(8,128)(2,1)S(1)} %get-tuple-element.92), channel_id=1, source_target_pairs={{0,2},{2,0},{1,3},{3,1},{4,6},{6,4},{5,7},{7,5},{8,10},{10,8},{9,1... | collective-permute-start | bytes 516104 | tf_op jit(solution)/shard_map/ppermute | solution.py:58
  47.0 5.5 %collective-permute-done.9.far = bf16[96,2688]{1,0:T(8,128)(2,1)S(1)} collective-permute-done((bf16[96,2688]{1,0:T(8,128)(2,1)S(1)}, bf16[96,2688]{1,0:T(8,128)(2,1)S(1)}, u32[]{:S(2)}, u32[]{:S(2)}) %collective-permute-start.9) | collective-permute-done | bytes 516128 | tf_op jit(solution)/shard_map/ppermute | solution.py:58
  52.5 0.1 shard_map.116
  52.7 2.7 %collective-permute-start.11 = (bf16[32,2688]{1,0:T(8,128)(2,1)S(1)}, bf16[32,2688]{1,0:T(8,128)(2,1)S(1)}, u32[]{:S(2)}, u32[]{:S(2)}) collective-permute-start(bf16[32,2688]{1,0:T(8,128)(2,1)S(1)} %get-tuple-element.95), channel_id=1, source_target_pairs={{0,8},{4,12},{8,0},{12,4},{1,9},{5,13},{9,1},{13,5},{2,10},{6,14},... | collective-permute-start | bytes 516104 | tf_op jit(solution)/shard_map/ppermute | solution.py:46
  55.4 2.4 %collective-permute-done.5.b = bf16[64,2304]{1,0:T(8,128)(2,1)S(1)} collective-permute-done((bf16[64,2304]{1,0:T(8,128)(2,1)S(1)}, bf16[64,2304]{1,0:T(8,128)(2,1)S(1)}, u32[]{:S(2)}, u32[]{:S(2)}) %collective-permute-start.5) | collective-permute-done | bytes 294944 | tf_op jit(solution)/shard_map/ppermute | solution.py:46
  57.8 1.1 collective-permute-done.6.c
  59.0 0.1 shard_map.115
  59.1 1.1 collective-permute-start.7
  60.2 3.3 %collective-permute-done.7.far_a = bf16[32,2304]{1,0:T(8,128)(2,1)S(1)} collective-permute-done((bf16[32,2304]{1,0:T(8,128)(2,1)S(1)}, bf16[32,2304]{1,0:T(8,128)(2,1)S(1)}, u32[]{:S(2)}, u32[]{:S(2)}) %collective-permute-start.7) | collective-permute-done | bytes 147488 | tf_op jit(solution)/shard_map/ppermute | solution.py:58
  63.5 0.4 collective-permute-done.10.right
  63.9 1.7 %collective-permute-done.12.left = bf16[32,2688]{1,0:T(8,128)(2,1)S(1)} collective-permute-done((bf16[32,2688]{1,0:T(8,128)(2,1)S(1)}, bf16[32,2688]{1,0:T(8,128)(2,1)S(1)}, u32[]{:S(2)}, u32[]{:S(2)}) %collective-permute-start.12) | collective-permute-done | bytes 172064 | tf_op jit(solution)/shard_map/ppermute | solution.py:46
  65.6 0.9 shard_map.117
  66.5 1.7 %collective-permute-start.18 = (bf16[32,4992]{1,0:T(8,128)(2,1)S(1)}, bf16[32,4992]{1,0:T(8,128)(2,1)S(1)}, u32[]{:S(2)}, u32[]{:S(2)}) collective-permute-start(bf16[32,4992]{1,0:T(8,128)(2,1)S(1)} %get-tuple-element.98.refs_0_), channel_id=1, source_target_pairs={{0,2},{2,0},{1,3},{3,1},{4,6},{6,4},{5,7},{7,5},{8,10},{10,8},{9,1... | collective-permute-start | bytes 958472 | tf_op jit(solution)/shard_map/ppermute | solution.py:58
  68.2 1.4 %collective-permute-start.14 = (bf16[32,4992]{1,0:T(8,128)(2,1)S(1)}, bf16[32,4992]{1,0:T(8,128)(2,1)S(1)}, u32[]{:S(2)}, u32[]{:S(2)}) collective-permute-start(bf16[32,4992]{1,0:T(8,128)(2,1)S(1)} %get-tuple-element.98.refs_0_), channel_id=1, source_target_pairs={{0,4},{4,8},{8,12},{12,0},{1,5},{5,9},{9,13},{13,1},{2,6},{6,10},{... | collective-permute-start | bytes 958472 | tf_op jit(solution)/shard_map/ppermute | solution.py:46
  69.6 1.4 %collective-permute-start.17 = (bf16[32,2432]{1,0:T(8,128)(2,1)S(1)}, bf16[32,2432]{1,0:T(8,128)(2,1)S(1)}, u32[]{:S(2)}, u32[]{:S(2)}) collective-permute-start(bf16[32,2432]{1,0:T(8,128)(2,1)S(1)} %get-tuple-element.100), channel_id=1, source_target_pairs={{0,12},{4,0},{8,4},{12,8},{1,13},{5,1},{9,5},{13,9},{2,14},{6,2},{... | collective-permute-start | bytes 466952 | tf_op jit(solution)/shard_map/ppermute | solution.py:46
  70.9 1.5 %collective-permute-start.13 = (bf16[32,2560]{1,0:T(8,128)(2,1)S(1)}, bf16[32,2560]{1,0:T(8,128)(2,1)S(1)}, u32[]{:S(2)}, u32[]{:S(2)}) collective-permute-start(bf16[32,2560]{1,0:T(8,128)(2,1)S(1)} %get-tuple-element.97), channel_id=1, source_target_pairs={{0,12},{4,0},{8,4},{12,8},{1,13},{5,1},{9,5},{13,9},{2,14},{6,2},{... | collective-permute-start | bytes 491528 | tf_op jit(solution)/shard_map/ppermute | solution.py:46
  72.4 1.5 %collective-permute-done.17.refs_3_ = bf16[32,2432]{1,0:T(8,128)(2,1)S(1)} collective-permute-done((bf16[32,2432]{1,0:T(8,128)(2,1)S(1)}, bf16[32,2432]{1,0:T(8,128)(2,1)S(1)}, u32[]{:S(2)}, u32[]{:S(2)}) %collective-permute-start.17) | collective-permute-done | bytes 155680 | tf_op jit(solution)/shard_map/ppermute | solution.py:46
  73.9 0.3 collective-permute-done.18.refs_1_
  74.2 2.4 %collective-permute-start.20 = (bf16[32,4992]{1,0:T(8,128)(2,1)S(1)}, bf16[32,4992]{1,0:T(8,128)(2,1)S(1)}, u32[]{:S(2)}, u32[]{:S(2)}) collective-permute-start(bf16[32,4992]{1,0:T(8,128)(2,1)S(1)} %collective-permute-done.18.refs_1_), channel_id=1, source_target_pairs={{0,4},{4,8},{8,12},{12,0},{1,5},{5,9},{9,13},{13,1},{2,6},{6,10},{... | collective-permute-start | bytes 958472 | tf_op jit(solution)/shard_map/ppermute | solution.py:46
  76.6 0.9 collective-permute-done.13.refs_2_
  77.4 2.2 %collective-permute-start.15 = (bf16[32,2560]{1,0:T(8,128)(2,1)S(1)}, bf16[32,2560]{1,0:T(8,128)(2,1)S(1)}, u32[]{:S(2)}, u32[]{:S(2)}) collective-permute-start(bf16[32,2560]{1,0:T(8,128)(2,1)S(1)} %collective-permute-done.13.refs_2_), channel_id=1, source_target_pairs={{0,12},{4,0},{8,4},{12,8},{1,13},{5,1},{9,5},{13,9},{2,14},{6,2},{... | collective-permute-start | bytes 491528 | tf_op jit(solution)/shard_map/ppermute | solution.py:46
  79.7 0.6 collective-permute-start.19
  80.3 0.6 collective-permute-start.22
  80.9 0.8 collective-permute-start.23
  81.7 0.2 collective-permute-done.15.refs_0_
  81.9 0.6 collective-permute-start.16
  82.5 0.9 shard_map.119.lines
  83.5 1.9 %collective-permute-done.19.refs_1_ = bf16[32,2432]{1,0:T(8,128)(2,1)S(1)} collective-permute-done((bf16[32,2432]{1,0:T(8,128)(2,1)S(1)}, bf16[32,2432]{1,0:T(8,128)(2,1)S(1)}, u32[]{:S(2)}, u32[]{:S(2)}) %collective-permute-start.19) | collective-permute-done | bytes 155680 | tf_op jit(solution)/shard_map/ppermute | solution.py:46
  85.4 0.7 collective-permute-start.21
  86.1 1.5 %shard_map.120 = (f32[128,320]{1,0:T(8,128)S(1)}, f32[128,320]{1,0:T(8,128)S(1)}) custom-call(bf16[128,4992]{1,0:T(8,128)(2,1)S(1)} %shard_map.118.refs_0_.early_in, bf16[320,1664]{1,0:T(8,128)(2,1)S(1)} %slice_select_fusion.2.w0.refs_1_.go, bf16[320,1664]{1,0:T(8,128)(2,1)S(1)} %collective-permute-done.1.w1.refs_2_.gs, ...), custom_call_target="tpu_custom_call" | custom-call | flops 545259520 | bytes 6291456 | tf_op jit(solution)/shard_map/pallas_call | solution.py:66
  87.7 1.5 %shard_map.122 = (f32[96,320]{1,0:T(8,128)S(1)}, f32[96,320]{1,0:T(8,128)S(1)}) custom-call(bf16[96,4992]{1,0:T(8,128)(2,1)S(1)} %shard_map.121.refs_0_, bf16[320,1664]{1,0:T(8,128)(2,1)S(1)} %slice_select_fusion.2.w0.refs_1_.go, bf16[320,1664]{1,0:T(8,128)(2,1)S(1)} %collective-permute-done.1.w1.refs_2_.gs, ...), custom_call_target="tpu_custom_call" | custom-call | flops 408944640 | bytes 6291456 | tf_op jit(solution)/shard_map/pallas_call | solution.py:66
  89.2 1.0 shard_map.123.sent
  90.2 3.3 %collective-permute-done.21.refs_1_ = bf16[32,2432]{1,0:T(8,128)(2,1)S(1)} collective-permute-done((bf16[32,2432]{1,0:T(8,128)(2,1)S(1)}, bf16[32,2432]{1,0:T(8,128)(2,1)S(1)}, u32[]{:S(2)}, u32[]{:S(2)}) %collective-permute-start.21) | collective-permute-done | bytes 155680 | tf_op jit(solution)/shard_map/ppermute | solution.py:58
  93.5 2.3 %shard_map.125 = (f32[32,320]{1,0:T(8,128)S(1)}, f32[32,320]{1,0:T(8,128)S(1)}, bf16[512,320]{1,0:T(8,128)(2,1)S(1)}) custom-call(s32[4]{0:T(128)S(1)} %pad_add_fusion.index, s32[8,256]{1,0:T(8,128)S(1)} %shard_map.119.lines, f32[512,320]{1,0:T(8,128)S(1)} %shard_map.123.sent, bf16[32,4992]{1,0:T(8,128)(2,1)S(1)} %shard_map.124.value.refs_5_, ...), custom_call_target="tpu_custom_call" | custom-call | flops 83886080 | bytes 1048576 | tf_op jit(solution)/shard_map/pallas_call | solution.py:66
  95.8 3.6 %collective-permute-start.24 = (bf16[512,320]{1,0:T(8,128)(2,1)S(1)}, bf16[512,320]{1,0:T(8,128)(2,1)S(1)}, u32[]{:S(2)}, u32[]{:S(2)}) collective-permute-start(bf16[512,320]{1,0:T(8,128)(2,1)S(1)} %get-tuple-element.115), channel_id=1, source_target_pairs={{0,1},{1,0},{2,3},{3,2},{4,5},{5,4},{6,7},{7,6},{8,9},{9,8},{10,11... | collective-permute-start | bytes 983048 | tf_op jit(solution)/shard_map/ppermute | solution.py:62
  99.7 1.0 shard_map.127.kept
  100.7 0.2 collective-permute-done.24.sent
  100.8 0.4 collective-permute-start.26
  101.2 0.8 shard_map.128
  102.0 4.6 %all-to-all-start.1 = ((bf16[64,8,320]{2,1,0:T(8,128)(2,1)}), bf16[64,8,320]{2,1,0:T(8,128)(2,1)S(1)}, u32[]{:S(2)}, u32[]{:S(2)}) async-start(bf16[64,8,320]{2,1,0:T(8,128)(2,1)} %bitcast.5), calls=%async_computation.1 | async-start | bytes 786432 | tf_op jit(solution)/shard_map/all_to_all | solution.py:508
  106.7 7.6 %shard_map.129 = (bf16[320,3200]{1,0:T(8,128)(2,1)}, bf16[320,3200]{1,0:T(8,128)(2,1)}, bf16[320,3200]{1,0:T(8,128)(2,1)}) custom-call(s32[4]{0:T(128)} %copy-done.3, bf16[8,64,384]{2,1,0:T(8,128)(2,1)} %copy-done, bf16[128,4992]{1,0:T(8,128)(2,1)} %copy-done.1, bf16[128,4992]{1,0:T(8,128)(2,1)} %copy-done.2, ...), custom_call_target="tpu_custom_call" | custom-call | flops 1572864000 | bytes 12582912 | tf_op jit(solution)/shard_map/pallas_call | solution.py:413
  114.2 3.9 %all-to-all-done.1.back = bf16[64,8,320]{2,1,0:T(8,128)(2,1)S(1)} async-done(((bf16[64,8,320]{2,1,0:T(8,128)(2,1)}), bf16[64,8,320]{2,1,0:T(8,128)(2,1)S(1)}, u32[]{:S(2)}, u32[]{:S(2)}) %all-to-all-start.1) | async-done | bytes 327712 | tf_op jit(solution)/shard_map/all_to_all | solution.py:508
  118.2 1.7 %shard_map.130 = bf16[128,5120]{1,0:T(8,128)(2,1)} custom-call(bf16[8,128]{1,0:T(8,128)(2,1)S(1)} %copy-done.4, bf16[64,8,320]{2,1,0:T(8,128)(2,1)S(1)} %all-to-all-done.1.back), custom_call_target="tpu_custom_call" | custom-call | tf_op jit(solution)/shard_map/pallas_call | solution.py:66
  (38 shorter events, 0.6 us)
Async XLA Ops:
  0.6 15.1 %copy-start.7 = (bf16[320,3200]{1,0:T(8,128)(2,1)S(1)}, bf16[320,3200]{1,0:T(8,128)(2,1)}, u32[]{:S(2)}) copy-start(bf16[320,3200]{1,0:T(8,128)(2,1)} %param.13) | copy-start | bytes 6144004
  4.2 28.1 %all-to-all-start = ((bf16[128,8,384]{2,1,0:T(8,128)(2,1)}), bf16[128,8,384]{2,1,0:T(8,128)(2,1)S(1)}, u32[]{:S(2)}, u32[]{:S(2)}) async-start(bf16[128,8,384]{2,1,0:T(8,128)(2,1)} %get-tuple-element.70), calls=%async_computation | async-start | bytes 1572864 | tf_op jit(solution)/shard_map/all_to_all | solution.py:446
  15.8 2.0 %copy-start.6 = (bf16[320,3200]{1,0:T(8,128)(2,1)S(1)}, bf16[320,3200]{1,0:T(8,128)(2,1)}, u32[]{:S(2)}) copy-start(bf16[320,3200]{1,0:T(8,128)(2,1)} %param.14) | copy-start | bytes 6144004
  17.7 2.0 %copy-start.5 = (bf16[3200,320]{0,1:T(8,128)(2,1)S(1)}, bf16[3200,320]{0,1:T(8,128)(2,1)}, u32[]{:S(2)}) copy-start(bf16[3200,320]{0,1:T(8,128)(2,1)} %param.15) | copy-start | bytes 6144004
  20.8 15.8 %collective-permute-start.3 = (bf16[320,1664]{1,0:T(8,128)(2,1)}, bf16[320,1664]{1,0:T(8,128)(2,1)}, u32[]{:S(2)}, u32[]{:S(2)}) collective-permute-start(bf16[320,1664]{1,0:T(8,128)(2,1)} %slice_select_fusion.3), channel_id=1, source_target_pairs={{0,1},{1,0},{2,3},{3,2},{4,5},{5,4},{6,7},{7,6},{8,9},{9,8},{10,11... | collective-permute-start | bytes 3194888 | tf_op jit(solution)/shard_map/ppermute | solution.py:62
  21.9 14.7 %collective-permute-start.2 = (bf16[320,1664]{1,0:T(8,128)(2,1)}, bf16[320,1664]{1,0:T(8,128)(2,1)S(1)}, u32[]{:S(2)}, u32[]{:S(2)}) collective-permute-start(bf16[320,1664]{1,0:T(8,128)(2,1)} %slice_select_fusion.4), channel_id=1, source_target_pairs={{0,1},{1,0},{2,3},{3,2},{4,5},{5,4},{6,7},{7,6},{8,9},{9,8},{10,11... | collective-permute-start | bytes 3194888 | tf_op jit(solution)/shard_map/ppermute | solution.py:62
  21.9 14.7 %collective-permute-start.1 = (bf16[320,1664]{1,0:T(8,128)(2,1)}, bf16[320,1664]{1,0:T(8,128)(2,1)S(1)}, u32[]{:S(2)}, u32[]{:S(2)}) collective-permute-start(bf16[320,1664]{1,0:T(8,128)(2,1)} %slice_select_fusion.5), channel_id=1, source_target_pairs={{0,1},{1,0},{2,3},{3,2},{4,5},{5,4},{6,7},{7,6},{8,9},{9,8},{10,11... | collective-permute-start | bytes 3194888 | tf_op jit(solution)/shard_map/ppermute | solution.py:62
  22.5 77.2 %copy-start.3 = (s32[4]{0:T(128)}, s32[4]{0:T(128)S(1)}, u32[]{:S(2)}) copy-start(s32[4]{0:T(128)S(1)} %pad_add_fusion.index) | copy-start | bytes 52
  33.2 49.3 %copy-start = (bf16[8,64,384]{2,1,0:T(8,128)(2,1)}, bf16[8,64,384]{2,1,0:T(8,128)(2,1)S(1)}, u32[]{:S(2)}) copy-start(bf16[8,64,384]{2,1,0:T(8,128)(2,1)S(1)} %shard_map.112.own) | copy-start | bytes 1179652
  33.2 3.4 %collective-permute-start = (bf16[8,64,384]{2,1,0:T(8,128)(2,1)S(1)}, bf16[8,64,384]{2,1,0:T(8,128)(2,1)S(1)}, u32[]{:S(2)}, u32[]{:S(2)}) collective-permute-start(bf16[8,64,384]{2,1,0:T(8,128)(2,1)S(1)} %shard_map.112.own), channel_id=1, source_target_pairs={{0,1},{1,0},{2,3},{3,2},{4,5},{5,4},{6,7},{7,6},{8,9},{9,8},{10,11... | collective-permute-start | bytes 1179656 | tf_op jit(solution)/shard_map/ppermute | solution.py:62
  33.6 2.9 %copy-start.8 = (bf16[320,3200]{1,0:T(8,128)(2,1)S(1)}, bf16[320,3200]{1,0:T(8,128)(2,1)}, u32[]{:S(2)}) copy-start(bf16[320,3200]{1,0:T(8,128)(2,1)} %param.13) | copy-start | bytes 6144004
  39.3 13.2 %collective-permute-start.9 = (bf16[96,2688]{1,0:T(8,128)(2,1)S(1)}, bf16[96,2688]{1,0:T(8,128)(2,1)S(1)}, u32[]{:S(2)}, u32[]{:S(2)}) collective-permute-start(bf16[96,2688]{1,0:T(8,128)(2,1)S(1)} %get-tuple-element.93), channel_id=1, source_target_pairs={{0,2},{2,0},{1,3},{3,1},{4,6},{6,4},{5,7},{7,5},{8,10},{10,8},{9,1... | collective-permute-start | bytes 1548296 | tf_op jit(solution)/shard_map/ppermute | solution.py:58
  42.3 10.4 %collective-permute-start.4 = (bf16[64,2304]{1,0:T(8,128)(2,1)S(1)}, bf16[64,2304]{1,0:T(8,128)(2,1)S(1)}, u32[]{:S(2)}, u32[]{:S(2)}) collective-permute-start(bf16[64,2304]{1,0:T(8,128)(2,1)S(1)} %get-tuple-element.86), channel_id=1, source_target_pairs={{0,4},{4,8},{8,12},{12,0},{1,5},{5,9},{9,13},{13,1},{2,6},{6,10},{... | collective-permute-start | bytes 884744 | tf_op jit(solution)/shard_map/ppermute | solution.py:46
  42.6 15.2 %collective-permute-start.5 = (bf16[64,2304]{1,0:T(8,128)(2,1)S(1)}, bf16[64,2304]{1,0:T(8,128)(2,1)S(1)}, u32[]{:S(2)}, u32[]{:S(2)}) collective-permute-start(bf16[64,2304]{1,0:T(8,128)(2,1)S(1)} %get-tuple-element.87), channel_id=1, source_target_pairs={{0,8},{4,12},{8,0},{12,4},{1,9},{5,13},{9,1},{13,5},{2,10},{6,14},... | collective-permute-start | bytes 884744 | tf_op jit(solution)/shard_map/ppermute | solution.py:46
  44.3 14.6 %collective-permute-start.6 = (bf16[64,2304]{1,0:T(8,128)(2,1)S(1)}, bf16[64,2304]{1,0:T(8,128)(2,1)S(1)}, u32[]{:S(2)}, u32[]{:S(2)}) collective-permute-start(bf16[64,2304]{1,0:T(8,128)(2,1)S(1)} %get-tuple-element.88), channel_id=1, source_target_pairs={{0,12},{4,0},{8,4},{12,8},{1,13},{5,1},{9,5},{13,9},{2,14},{6,2},{... | collective-permute-start | bytes 884744 | tf_op jit(solution)/shard_map/ppermute | solution.py:46
  45.5 14.7 %collective-permute-start.8 = (bf16[32,2688]{1,0:T(8,128)(2,1)S(1)}, bf16[32,2688]{1,0:T(8,128)(2,1)S(1)}, u32[]{:S(2)}, u32[]{:S(2)}) collective-permute-start(bf16[32,2688]{1,0:T(8,128)(2,1)S(1)} %get-tuple-element.92), channel_id=1, source_target_pairs={{0,2},{2,0},{1,3},{3,1},{4,6},{6,4},{5,7},{7,5},{8,10},{10,8},{9,1... | collective-permute-start | bytes 516104 | tf_op jit(solution)/shard_map/ppermute | solution.py:58
  52.6 11.3 %collective-permute-start.10 = (bf16[32,2688]{1,0:T(8,128)(2,1)S(1)}, bf16[32,2688]{1,0:T(8,128)(2,1)S(1)}, u32[]{:S(2)}, u32[]{:S(2)}) collective-permute-start(bf16[32,2688]{1,0:T(8,128)(2,1)S(1)} %get-tuple-element.94), channel_id=1, source_target_pairs={{0,4},{4,8},{8,12},{12,0},{1,5},{5,9},{9,13},{13,1},{2,6},{6,10},{... | collective-permute-start | bytes 516104 | tf_op jit(solution)/shard_map/ppermute | solution.py:46
  52.7 11.2 %collective-permute-start.11 = (bf16[32,2688]{1,0:T(8,128)(2,1)S(1)}, bf16[32,2688]{1,0:T(8,128)(2,1)S(1)}, u32[]{:S(2)}, u32[]{:S(2)}) collective-permute-start(bf16[32,2688]{1,0:T(8,128)(2,1)S(1)} %get-tuple-element.95), channel_id=1, source_target_pairs={{0,8},{4,12},{8,0},{12,4},{1,9},{5,13},{9,1},{13,5},{2,10},{6,14},... | collective-permute-start | bytes 516104 | tf_op jit(solution)/shard_map/ppermute | solution.py:46
  57.8 7.8 %collective-permute-start.12 = (bf16[32,2688]{1,0:T(8,128)(2,1)S(1)}, bf16[32,2688]{1,0:T(8,128)(2,1)S(1)}, u32[]{:S(2)}, u32[]{:S(2)}) collective-permute-start(bf16[32,2688]{1,0:T(8,128)(2,1)S(1)} %get-tuple-element.96), channel_id=1, source_target_pairs={{0,12},{4,0},{8,4},{12,8},{1,13},{5,1},{9,5},{13,9},{2,14},{6,2},{... | collective-permute-start | bytes 516104 | tf_op jit(solution)/shard_map/ppermute | solution.py:46
  59.1 4.4 %collective-permute-start.7 = (bf16[32,2304]{1,0:T(8,128)(2,1)S(1)}, bf16[32,2304]{1,0:T(8,128)(2,1)S(1)}, u32[]{:S(2)}, u32[]{:S(2)}) collective-permute-start(bf16[32,2304]{1,0:T(8,128)(2,1)S(1)} %get-tuple-element.90), channel_id=1, source_target_pairs={{0,2},{2,0},{1,3},{3,1},{4,6},{6,4},{5,7},{7,5},{8,10},{10,8},{9,1... | collective-permute-start | bytes 442376 | tf_op jit(solution)/shard_map/ppermute | solution.py:58
  66.5 7.7 %collective-permute-start.18 = (bf16[32,4992]{1,0:T(8,128)(2,1)S(1)}, bf16[32,4992]{1,0:T(8,128)(2,1)S(1)}, u32[]{:S(2)}, u32[]{:S(2)}) collective-permute-start(bf16[32,4992]{1,0:T(8,128)(2,1)S(1)} %get-tuple-element.98.refs_0_), channel_id=1, source_target_pairs={{0,2},{2,0},{1,3},{3,1},{4,6},{6,4},{5,7},{7,5},{8,10},{10,8},{9,1... | collective-permute-start | bytes 958472 | tf_op jit(solution)/shard_map/ppermute | solution.py:58
  68.2 9.3 %collective-permute-start.14 = (bf16[32,4992]{1,0:T(8,128)(2,1)S(1)}, bf16[32,4992]{1,0:T(8,128)(2,1)S(1)}, u32[]{:S(2)}, u32[]{:S(2)}) collective-permute-start(bf16[32,4992]{1,0:T(8,128)(2,1)S(1)} %get-tuple-element.98.refs_0_), channel_id=1, source_target_pairs={{0,4},{4,8},{8,12},{12,0},{1,5},{5,9},{9,13},{13,1},{2,6},{6,10},{... | collective-permute-start | bytes 958472 | tf_op jit(solution)/shard_map/ppermute | solution.py:46
  69.6 4.4 %collective-permute-start.17 = (bf16[32,2432]{1,0:T(8,128)(2,1)S(1)}, bf16[32,2432]{1,0:T(8,128)(2,1)S(1)}, u32[]{:S(2)}, u32[]{:S(2)}) collective-permute-start(bf16[32,2432]{1,0:T(8,128)(2,1)S(1)} %get-tuple-element.100), channel_id=1, source_target_pairs={{0,12},{4,0},{8,4},{12,8},{1,13},{5,1},{9,5},{13,9},{2,14},{6,2},{... | collective-permute-start | bytes 466952 | tf_op jit(solution)/shard_map/ppermute | solution.py:46
  70.9 6.5 %collective-permute-start.13 = (bf16[32,2560]{1,0:T(8,128)(2,1)S(1)}, bf16[32,2560]{1,0:T(8,128)(2,1)S(1)}, u32[]{:S(2)}, u32[]{:S(2)}) collective-permute-start(bf16[32,2560]{1,0:T(8,128)(2,1)S(1)} %get-tuple-element.97), channel_id=1, source_target_pairs={{0,12},{4,0},{8,4},{12,8},{1,13},{5,1},{9,5},{13,9},{2,14},{6,2},{... | collective-permute-start | bytes 491528 | tf_op jit(solution)/shard_map/ppermute | solution.py:46
  74.2 11.2 %collective-permute-start.20 = (bf16[32,4992]{1,0:T(8,128)(2,1)S(1)}, bf16[32,4992]{1,0:T(8,128)(2,1)S(1)}, u32[]{:S(2)}, u32[]{:S(2)}) collective-permute-start(bf16[32,4992]{1,0:T(8,128)(2,1)S(1)} %collective-permute-done.18.refs_1_), channel_id=1, source_target_pairs={{0,4},{4,8},{8,12},{12,0},{1,5},{5,9},{9,13},{13,1},{2,6},{6,10},{... | collective-permute-start | bytes 958472 | tf_op jit(solution)/shard_map/ppermute | solution.py:46
  77.4 4.5 %collective-permute-start.15 = (bf16[32,2560]{1,0:T(8,128)(2,1)S(1)}, bf16[32,2560]{1,0:T(8,128)(2,1)S(1)}, u32[]{:S(2)}, u32[]{:S(2)}) collective-permute-start(bf16[32,2560]{1,0:T(8,128)(2,1)S(1)} %collective-permute-done.13.refs_2_), channel_id=1, source_target_pairs={{0,12},{4,0},{8,4},{12,8},{1,13},{5,1},{9,5},{13,9},{2,14},{6,2},{... | collective-permute-start | bytes 491528 | tf_op jit(solution)/shard_map/ppermute | solution.py:46
  79.7 5.7 %collective-permute-start.19 = (bf16[32,2432]{1,0:T(8,128)(2,1)S(1)}, bf16[32,2432]{1,0:T(8,128)(2,1)S(1)}, u32[]{:S(2)}, u32[]{:S(2)}) collective-permute-start(bf16[32,2432]{1,0:T(8,128)(2,1)S(1)} %collective-permute-done.17.refs_3_), channel_id=1, source_target_pairs={{0,12},{4,0},{8,4},{12,8},{1,13},{5,1},{9,5},{13,9},{2,14},{6,2},{... | collective-permute-start | bytes 466952 | tf_op jit(solution)/shard_map/ppermute | solution.py:46
  80.3 7.3 %collective-permute-start.22 = (bf16[32,2560]{1,0:T(8,128)(2,1)S(1)}, bf16[32,2560]{1,0:T(8,128)(2,1)S(1)}, u32[]{:S(2)}, u32[]{:S(2)}) collective-permute-start(bf16[32,2560]{1,0:T(8,128)(2,1)S(1)} %collective-permute-done.13.refs_2_), channel_id=1, source_target_pairs={{0,2},{2,0},{1,3},{3,1},{4,6},{6,4},{5,7},{7,5},{8,10},{10,8},{9,1... | collective-permute-start | bytes 491528 | tf_op jit(solution)/shard_map/ppermute | solution.py:58
  80.9 6.7 %collective-permute-start.23 = (bf16[32,2432]{1,0:T(8,128)(2,1)S(1)}, bf16[32,2432]{1,0:T(8,128)(2,1)S(1)}, u32[]{:S(2)}, u32[]{:S(2)}) collective-permute-start(bf16[32,2432]{1,0:T(8,128)(2,1)S(1)} %collective-permute-done.17.refs_3_), channel_id=1, source_target_pairs={{0,2},{2,0},{1,3},{3,1},{4,6},{6,4},{5,7},{7,5},{8,10},{10,8},{9,1... | collective-permute-start | bytes 466952 | tf_op jit(solution)/shard_map/ppermute | solution.py:58
  81.9 8.3 %collective-permute-start.16 = (bf16[32,2560]{1,0:T(8,128)(2,1)S(1)}, bf16[32,2560]{1,0:T(8,128)(2,1)S(1)}, u32[]{:S(2)}, u32[]{:S(2)}) collective-permute-start(bf16[32,2560]{1,0:T(8,128)(2,1)S(1)} %collective-permute-done.15.refs_0_), channel_id=1, source_target_pairs={{0,2},{2,0},{1,3},{3,1},{4,6},{6,4},{5,7},{7,5},{8,10},{10,8},{9,1... | collective-permute-start | bytes 491528 | tf_op jit(solution)/shard_map/ppermute | solution.py:58
  83.5 16.0 %copy-start.1 = (bf16[128,4992]{1,0:T(8,128)(2,1)}, bf16[128,4992]{1,0:T(8,128)(2,1)S(1)}, u32[]{:S(2)}) copy-start(bf16[128,4992]{1,0:T(8,128)(2,1)S(1)} %shard_map.118.refs_0_.early_in) | copy-start | bytes 3833860
  85.4 8.1 %collective-permute-start.21 = (bf16[32,2432]{1,0:T(8,128)(2,1)S(1)}, bf16[32,2432]{1,0:T(8,128)(2,1)S(1)}, u32[]{:S(2)}, u32[]{:S(2)}) collective-permute-start(bf16[32,2432]{1,0:T(8,128)(2,1)S(1)} %collective-permute-done.19.refs_1_), channel_id=1, source_target_pairs={{0,2},{2,0},{1,3},{3,1},{4,6},{6,4},{5,7},{7,5},{8,10},{10,8},{9,1... | collective-permute-start | bytes 466952 | tf_op jit(solution)/shard_map/ppermute | solution.py:58
  95.8 5.0 %collective-permute-start.24 = (bf16[512,320]{1,0:T(8,128)(2,1)S(1)}, bf16[512,320]{1,0:T(8,128)(2,1)S(1)}, u32[]{:S(2)}, u32[]{:S(2)}) collective-permute-start(bf16[512,320]{1,0:T(8,128)(2,1)S(1)} %get-tuple-element.115), channel_id=1, source_target_pairs={{0,1},{1,0},{2,3},{3,2},{4,5},{5,4},{6,7},{7,6},{8,9},{9,8},{10,11... | collective-permute-start | bytes 983048 | tf_op jit(solution)/shard_map/ppermute | solution.py:62
  99.5 7.2 %collective-permute-start.25 = (bf16[128,4992]{1,0:T(8,128)(2,1)S(1)}, bf16[128,4992]{1,0:T(8,128)(2,1)}, u32[]{:S(2)}, u32[]{:S(2)}) collective-permute-start(bf16[128,4992]{1,0:T(8,128)(2,1)S(1)} %shard_map.118.refs_0_.early_in), channel_id=1, source_target_pairs={{0,1},{1,0},{2,3},{3,2},{4,5},{5,4},{6,7},{7,6},{8,9},{9,8},{10,11... | collective-permute-start | bytes 3833864 | tf_op jit(solution)/shard_map/ppermute | solution.py:62
  99.7 2.4 %copy-start.2 = (bf16[128,4992]{1,0:T(8,128)(2,1)}, bf16[128,4992]{1,0:T(8,128)(2,1)S(1)}, u32[]{:S(2)}) copy-start(bf16[128,4992]{1,0:T(8,128)(2,1)S(1)} %shard_map.126.late_in) | copy-start | bytes 3833860
  100.8 5.9 %collective-permute-start.26 = (bf16[128,4992]{1,0:T(8,128)(2,1)S(1)}, bf16[128,4992]{1,0:T(8,128)(2,1)}, u32[]{:S(2)}, u32[]{:S(2)}) collective-permute-start(bf16[128,4992]{1,0:T(8,128)(2,1)S(1)} %shard_map.126.late_in), channel_id=1, source_target_pairs={{0,1},{1,0},{2,3},{3,2},{4,5},{5,4},{6,7},{7,6},{8,9},{9,8},{10,11... | collective-permute-start | bytes 3833864 | tf_op jit(solution)/shard_map/ppermute | solution.py:62
  102.0 16.2 %all-to-all-start.1 = ((bf16[64,8,320]{2,1,0:T(8,128)(2,1)}), bf16[64,8,320]{2,1,0:T(8,128)(2,1)S(1)}, u32[]{:S(2)}, u32[]{:S(2)}) async-start(bf16[64,8,320]{2,1,0:T(8,128)(2,1)} %bitcast.5), calls=%async_computation.1 | async-start | bytes 786432 | tf_op jit(solution)/shard_map/all_to_all | solution.py:508
  106.6 11.5 %copy-start.4 = (bf16[8,128]{1,0:T(8,128)(2,1)S(1)}, bf16[8,128]{1,0:T(8,128)(2,1)}, u32[]{:S(2)}) copy-start(bf16[8,128]{1,0:T(8,128)(2,1)} %get-tuple-element.68.owner) | copy-start | bytes 6148
